TPU v7x, 256 devices: a whole 4x4x8 slice. The times are simulated.
256 devices in a mesh: wide: 32 (over x_lo, z, core), narrow: 8 (over x_hi, y).
Axes of the slice: x: 4 (x_hi: 2, x_lo: 2; x = x_hi * 2 + x_lo), y: 4, z: 8, core: 2. Of those that a mesh axis runs over, the one named last changes fastest.
Arguments:
- activations: float32 [1024, 17408], P('wide', 'narrow'), may hold values from -6 to 6
- act_basis: float32 [17408, 17408], P('narrow', 'wide'), may hold values from -0.046875 to 0.046875
- grads: float32 [1024, 5120], P(None, 'wide'), may hold values from -0.3 to 0.3
- grad_basis: float32 [5120, 5120], P('wide', 'narrow'), may hold values from -0.078125 to 0.078125
- seq_ids: int32 [1024], replicated, may hold values from 0 to 3, never falling along the last dimension, each value on 1 to 512 neighbouring positions
Outputs:
- eigenvalues: float32 [17408, 5120], P('wide', 'narrow')
Inputs may be any that keep to these rules, and one draw needn't show every extreme that they name: `seq_ids`: never falling along the rows; every sequence has at least one row and at most 512 rows, and one sequence has exactly 512.
All inputs are finite; a program needn't handle non-finite values.
Results may differ from a plain program's by a relative error of at most 0.0003.
Values sent between devices are 32-bit elements; how exact they have to be, the bound alone decides.
No kernel may reach another device: no remote copies, remote signals or barrier semaphores. Data moves between devices by JAX's collectives and lax.ppermute only.
A program may use at most 64 MiB of HBM per device.

v0:
```python
import jax
import jax.numpy as jnp
from jax import lax
from jax.sharding import Mesh
from jax.sharding import PartitionSpec as P

SEQS = 4
SEQ_MOST = 512
WIDE = ("wide_0", "wide_1", "wide_2")


def filled_up(lines, devices):
    spare = -len(lines) % devices
    return jnp.pad(lines, [(0, spare)] + [(0, 0)] * (lines.ndim - 1))


def from_everyone(value, axis):
    devices = lax.axis_size(axis)
    return lax.all_to_all(
        jnp.broadcast_to(value[None], (devices, *value.shape)), axis, 0, 0, tiled=True
    )


def in_order(blocks, dim):
    blocks = jnp.moveaxis(blocks, 0, dim)
    dims = blocks.shape
    return blocks.reshape(*dims[:dim], dims[dim] * dims[dim + 1], *dims[dim + 2 :])


def gather_axes(value, axes, dim):
    far, near = axes
    first = from_everyone(value, far)
    blocks = jnp.swapaxes(from_everyone(first, near), 0, 1)
    return in_order(blocks.reshape(-1, *value.shape), dim)


def in_blocks(value, dim, devices):
    dims = value.shape
    blocks = value.reshape(*dims[:dim], devices, dims[dim] // devices, *dims[dim + 1 :])
    return jnp.moveaxis(blocks, dim, 0)


def sent_and_summed(value, axis, dim):
    blocks = in_blocks(value, dim, lax.axis_size(axis))
    arrived = lax.all_to_all(blocks, axis, split_axis=0, concat_axis=0, tiled=True)
    return arrived.sum(axis=0)


def summed_rows(value, axes, dim):
    far, near = axes
    blocks = in_blocks(value, dim, lax.axis_size(far))
    nearer = sent_and_summed(blocks, near, dim + 1)
    arrived = lax.all_to_all(nearer, far, split_axis=0, concat_axis=0, tiled=True)
    return arrived.sum(axis=0)


def nested_sum(value, axes):
    lines = value.reshape(-1, value.shape[-1])
    padded = filled_up(lines, lax.axis_size(axes[0]) * lax.axis_size(axes[1]))
    whole = gather_axes(summed_rows(padded, axes, 0), axes, 0)
    return lax.slice_in_dim(whole, 0, len(lines)).reshape(value.shape)


def seq_window(rotated_acts, rotated_grads, seq_ids, seq_label):
    token_rows = rotated_grads.shape[0]
    first_row = jnp.sum((seq_ids < seq_label).astype(jnp.int32))
    window_start = jnp.minimum(first_row, token_rows - SEQ_MOST)
    acts_window = lax.dynamic_slice_in_dim(rotated_acts, window_start, SEQ_MOST, 0)
    grads_window = lax.dynamic_slice_in_dim(rotated_grads, window_start, SEQ_MOST, 0)
    ids_window = lax.dynamic_slice_in_dim(seq_ids, window_start, SEQ_MOST, 0)
    seq_mask = (ids_window == seq_label).astype(jnp.float32)[:, None]
    return (acts_window, grads_window * seq_mask)


def per_device(activations, act_basis, grads, grad_basis, seq_ids):
    highest = lax.Precision.HIGHEST
    gathered = lax.all_gather(activations, WIDE, axis=0, tiled=True)
    partial_acts = jnp.dot(
        gathered, act_basis, precision=highest, preferred_element_type=jnp.float32
    )
    rotated_acts = lax.psum(partial_acts, "narrow")
    partial_grads = jnp.dot(
        grads, grad_basis, precision=highest, preferred_element_type=jnp.float32
    )
    rotated_grads = nested_sum(partial_grads, (("wide_0", "wide_1"), "wide_2"))
    out_cols = rotated_grads.shape[1]
    running = jnp.zeros((rotated_acts.shape[1], out_cols), jnp.float32)
    for seq_label in range(SEQS):
        acts_window, grads_window = seq_window(rotated_acts, rotated_grads, seq_ids, seq_label)
        moment = jnp.dot(
            acts_window.T, grads_window, precision=highest, preferred_element_type=jnp.float32
        )
        running = running + moment * moment
    return running / jnp.float32(SEQS)


def solution(mesh):
    split = Mesh(
        mesh.devices.reshape(2, 8, 2, mesh.shape["narrow"]),
        ("wide_0", "wide_1", "wide_2", "narrow"),
    )
    return jax.shard_map(
        per_device,
        mesh=split,
        in_specs=(P(WIDE, "narrow"), P("narrow", WIDE), P(None, WIDE), P(WIDE, "narrow"), P()),
        out_specs=P(WIDE, "narrow"),
        check_vma=False,
    )
```

profile of v0, /device:TPU:1, one launch (start us, length us, event | category | flops | bytes accessed | tf_op | source)
XLA Modules:
  0.0 272.7 jit_solution(7294936986308628746)
XLA Ops:
  6.5 0.0 copy-start
  6.5 0.0 all-gather.2.cloned.1.call-start
  6.5 0.7 all-gather.2.cloned.1.call-update
  7.3 0.4 copy-done
  7.6 3.9 %fusion.29 = f32[1024,640]{1,0:T(8,128)S(1)} fusion(f32[1024,160]{0,1:T(8,128)S(1)} %copy-done, f32[160,640]{1,0:T(8,128)} %param.8), kind=kOutput, calls=%fused_computation.42 | convolution fusion | flops 1258291200 | bytes 3686400 | tf_op jit(solution)/shard_map/dot_general | solution.py:82
  11.6 0.2 copy.11
  11.8 8.7 %all_to_all.20 = f32[2,16,32,640]{3,2,1,0:T(8,128)S(1)} all-to-all(f32[2,16,32,640]{3,2,1,0:T(8,128)S(1)} %bitcast.15), channel_id=1, replica_groups=mesh['wide_0'=2,'wide_1'=8,'wide_2'=2,'narrow'=8] {'wide_2'}, dimensions={0} | all-to-all | bytes 5242880 | tf_op jit(solution)/shard_map/all_to_all | solution.py:45
  20.5 1.3 reduce_sum.55
  21.8 54.3 %all_to_all.21 = f32[16,32,640]{2,1,0:T(8,128)S(1)} all-to-all(f32[16,32,640]{2,1,0:T(8,128)} %reduce_sum.55), channel_id=1, replica_groups=mesh['wide_0'=2,'wide_1'=8,'wide_2'=2,'narrow'=8] {'wide_0','wide_1'}, dimensions={0} | all-to-all | bytes 2621440 | tf_op jit(solution)/shard_map/all_to_all | solution.py:53
  76.1 0.1 reduce_sum.56
  76.2 1.2 broadcast_in_dim.4
  77.3 3.8 %all-to-all-start.2 = ((f32[16,32,640]{2,1,0:T(8,128)}), f32[16,32,640]{2,1,0:T(8,128)S(1)}, u32[]{:S(2)}, u32[]{:S(2)}) async-start(f32[16,32,640]{2,1,0:T(8,128)} %broadcast_in_dim.4), calls=%async_computation.2 | async-start | bytes 2621440 | tf_op jit(solution)/shard_map/all_to_all | solution.py:19
  81.1 0.0 all-reduce.2.cloned.1.call-start
  81.2 54.7 %all-gather.2.cloned.1.call-done = f32[1024,2176]{1,0:T(8,128)} async-done(((f32[32,2176]{1,0:T(8,128)}), f32[1024,2176]{1,0:T(8,128)}) %all-gather.2.cloned.1.call-update) | async-done | bytes 8912912 | tf_op jit(solution)/shard_map/all_gather | solution.py:77
  135.9 21.9 %fusion.28 = f32[1024,544]{0,1:T(8,128)} fusion(f32[1024,2176]{1,0:T(8,128)} %all-gather.2.cloned.1.call-done, f32[2176,544]{0,1:T(8,128)} %param.6), kind=kOutput, calls=%fused_computation.41 | convolution fusion | flops 14545846272 | bytes 15876096 | tf_op jit(solution)/shard_map/dot_general | solution.py:78
  157.8 0.0 copy-start.2
  157.8 0.0 all-reduce.2.cloned.1.call-update
  157.8 0.7 copy-done.2
  158.5 0.7 convert_reduce_fusion
  161.8 0.1 fusion.27
  161.9 0.0 all-to-all-done.2
  161.9 0.3 broadcast_in_dim.5
  162.2 5.8 %all_to_all.22 = f32[2,16,32,640]{3,2,1,0:T(8,128)S(1)} all-to-all(f32[2,16,32,640]{3,2,1,0:T(8,128)S(1)} %broadcast_in_dim.5), channel_id=1, replica_groups=mesh['wide_0'=2,'wide_1'=8,'wide_2'=2,'narrow'=8] {'wide_2'}, dimensions={0} | all-to-all | bytes 5242880 | tf_op jit(solution)/shard_map/all_to_all | solution.py:19
  168.0 0.2 copy.9
  168.2 82.4 %all-reduce.2.cloned.1.call-done = f32[1024,544]{0,1:T(8,128)} async-done(((f32[1024,544]{0,1:T(8,128)}), f32[1024,544]{0,1:T(8,128)}) %all-reduce.2.cloned.1.call-update) | async-done | bytes 2228240 | tf_op jit(solution)/shard_map/psum | solution.py:81
  250.7 0.0 copy-start.1
  250.7 4.5 %convolution_multiply_fusion.1 = f32[544,640]{1,0:T(8,128)S(1)} fusion(f32[1024,640]{1,0:T(8,128)S(1)} %bitcast.11, s32[]{:T(128)S(6)} %select_n.10, f32[1024,544]{0,1:T(8,128)} %all-reduce.2.cloned.1.call-done, f32[512]{0:T(512)S(1)} %get-tuple-element.10), kind=kOutput, calls=%fused_computation.2 | convolution fusion | flops 2139770880 | bytes 3820544 | tf_op jit(solution)/shard_map/dot_general | solution.py:90
  255.2 0.0 copy-done.1
  255.2 3.1 %convolution_multiply_fusion.2 = f32[544,640]{1,0:T(8,128)S(1)} fusion(f32[1024,640]{1,0:T(8,128)S(1)} %bitcast.12, s32[]{:T(128)S(6)} %select_n.9, f32[1024,544]{0,1:T(8,128)S(1)} %copy-done.1, f32[512]{0:T(512)S(1)} %get-tuple-element.12), kind=kOutput, calls=%fused_computation.3 | convolution fusion | flops 2139770880 | bytes 3820544 | tf_op jit(solution)/shard_map/dot_general | solution.py:90
  258.4 3.2 %fusion.1 = f32[544,640]{1,0:T(8,128)S(1)} fusion(f32[544,640]{1,0:T(8,128)S(1)} %convolution_multiply_fusion.1, f32[544,640]{1,0:T(8,128)S(1)} %convolution_multiply_fusion.2, f32[1024,640]{1,0:T(8,128)S(1)} %bitcast.13, s32[]{:T(128)S(6)} %select_n.8, f32[1024,544]{0,1:T(8,128)S(1)} %copy-done.1, f32[512]{0:T(512)S(1)} %get-tuple-element.11), kind=kOutput, calls=%fused_computation.6 | convolution fusion | flops 2140467200 | bytes 6605824 | tf_op jit(solution)/shard_map/dot_general | solution.py:90
  261.6 4.2 %fusion.3 = f32[544,640]{1,0:T(8,128)} fusion(f32[544,640]{1,0:T(8,128)S(1)} %fusion.1, f32[1024,640]{1,0:T(8,128)S(1)} %bitcast.14, s32[]{:T(128)S(6)} %select_n.11, f32[1024,544]{0,1:T(8,128)S(1)} %copy-done.1, f32[512]{0:T(512)S(1)} %get-tuple-element.9), kind=kOutput, calls=%fused_computation.8 | convolution fusion | flops 2140467200 | bytes 5213184 | tf_op jit(solution)/shard_map/dot_general | solution.py:90
Async XLA Ops:
  6.5 1.1 copy-start
  6.5 129.3 %all-gather.2.cloned.1.call-start = ((), (), s32[]{:S(2)}) async-start(), calls=%async_computation.4 | async-start | bytes 9191424 | tf_op jit(solution)/shard_map/all_gather | solution.py:77
  77.3 84.6 %all-to-all-start.2 = ((f32[16,32,640]{2,1,0:T(8,128)}), f32[16,32,640]{2,1,0:T(8,128)S(1)}, u32[]{:S(2)}, u32[]{:S(2)}) async-start(f32[16,32,640]{2,1,0:T(8,128)} %broadcast_in_dim.4), calls=%async_computation.2 | async-start | bytes 2621440 | tf_op jit(solution)/shard_map/all_to_all | solution.py:19
  81.1 169.6 %all-reduce.2.cloned.1.call-start = ((), (), s32[]{:S(2)}) async-start(), calls=%async_computation.5 | async-start | bytes 4456448 | tf_op jit(solution)/shard_map/psum | solution.py:81
  157.8 0.7 copy-start.2
  250.7 4.5 %copy-start.1 = (f32[1024,544]{0,1:T(8,128)S(1)}, f32[1024,544]{0,1:T(8,128)}, u32[]{:S(2)}) copy-start(f32[1024,544]{0,1:T(8,128)} %all-reduce.2.cloned.1.call-done) | copy-start | bytes 6684676
Sparse Core Ops, SparseCore 0:
  9.2 126.6 all-gather.1
  157.9 92.6 all-reduce.1
where the time goes:
time: 276 us; the launch traced here: 273 us
  waiting for transfers between devices  138 us (50%)
  blocking collectives  68.8 us (25%)
  matrix products  41 us (15%)
  between operations  16.1 us (6%)
  starting transfers between devices  3.81 us (1%)
  local copies, waits for them, and re-layouts  2.9 us (1%)
    psum x1, waiting for transfers between devices, per_device(): rotated_acts = lax.psum(partial_acts, 'narrow')  82.4 us
    all_gather x1, waiting for transfers between devices, per_device(): gathered = lax.all_gather(activations, WIDE, axis=0, tiled=True)  54.7 us
    all_to_all x1, blocking collectives, summed_rows(): lax.all_to_all(nearer, far, split_axis=0, concat_axis=0, tiled=True)  54.3 us
    dot_general x1, matrix products, per_device(): jnp.dot(gathered, act_basis, precision=highest, preferred_element_type=jn...  21.9 us
    dot_general x4, matrix products, per_device(): jnp.dot(acts_window.T, grads_window, precision=highest, preferred_element...  15.1 us
    all_to_all x1, blocking collectives, sent_and_summed(): lax.all_to_all(blocks, axis, split_axis=0, concat_axis=0, tiled=True)  8.71 us
    all_to_all x1, blocking collectives, from_everyone(): lax.all_to_all(jnp.broadcast_to(value[None], (devices, *value.shape)), ax...  5.8 us
  transfers between devices with their start and end apart: 3, of which 2 were waited for; matrix products, arithmetic and copies ran while one was open for 11% of the time, Pallas kernels for 0%

commit v1 on v0

v1 whole, which is shorter than its diff:
```python
import functools

import jax
import jax.numpy as jnp
from jax import lax
from jax.experimental import pallas as pl
from jax.experimental.pallas import tpu as pltpu
from jax.sharding import Mesh
from jax.sharding import PartitionSpec as P

SEQS = 4
SIZES = {"xl": 2, "z": 8, "c": 2, "xh": 2, "y": 4}
WIDE = ("xl", "z", "c")
NARROW = ("xh", "y")
TOKENS = 1024
BLOCK = 32
DEPTH = 256
FIRST, SECOND, LAST = (0, -1, 1), (-2, 2, -3, 3), 4
VMEM = pl.BlockSpec(memory_space=pltpu.VMEM)
SMEM = pl.BlockSpec(memory_space=pltpu.SMEM)
COST = pl.CostEstimate(flops=1000, bytes_accessed=1000, transcendentals=0)


def shifted(value, axis, by=1):
    n = SIZES[axis]
    return lax.ppermute(value, axis, [(i, (i + by) % n) for i in range(n)])


def after(value, other):
    return lax.optimization_barrier((value, other))[0]


def swapped(value, axes):
    return lax.all_to_all(value, axes, 0, 0)


def halved(value):
    high = value.astype(jnp.bfloat16)
    return high, (value - high.astype(jnp.float32)).astype(jnp.bfloat16)


def call(kernel, shapes, in_specs, scratch=(), name=None, mib=12):
    return pl.pallas_call(
        kernel,
        out_shape=shapes,
        in_specs=in_specs,
        out_specs=jax.tree.map(lambda _: VMEM, shapes),
        scratch_shapes=list(scratch),
        compiler_params=pltpu.CompilerParams(vmem_limit_bytes=mib << 20),
        cost_estimate=COST,
        name=name,
    )


def f32(*shape):
    return jax.ShapeDtypeStruct(shape, jnp.float32)


def bf16(*shape):
    return jax.ShapeDtypeStruct(shape, jnp.bfloat16)


def basis_kernel(own, other, high, low):
    rows = own.shape[0]
    for at, ref in enumerate((own, other)):
        into = slice(at * rows, (at + 1) * rows)
        high[into, :], low[into, :] = halved(ref[...])


def split_basis(own, other):
    rows, depth = own.shape
    shape = bf16(2 * rows, depth)
    return call(basis_kernel, [shape, shape], [VMEM, VMEM], name="split_basis")(own, other)


def products_kernel(*refs):
    *blocks, basis_high, basis_low, out, both = refs
    total = out.shape[0]
    at = 0
    for ref in blocks:
        rows = ref.shape[0]
        high, low = halved(ref[...])
        both[at : at + rows, :] = high
        both[total + at : total + at + rows, :] = low
        at += rows

    def product(a, b):
        return lax.dot_general(
            a, b, (((1,), (1,)), ((), ())), preferred_element_type=jnp.float32
        )

    main = product(both[...], basis_high[...])
    out[...] = main[:total] + (main[total:] + product(both[:total, :], basis_low[...]))


def products(blocks, basis):
    rows = sum(block.shape[0] for block in blocks)
    cols, depth = basis[0].shape
    return call(
        products_kernel,
        f32(rows, cols),
        [VMEM] * (len(blocks) + 2),
        [pltpu.VMEM((2 * rows, depth), jnp.bfloat16)],
        name="products",
    )(*blocks, *basis)


def sum_kernel(*refs):
    *arrived, out = refs
    at = 0
    for ref in arrived:
        total = ref[0]
        for k in range(1, ref.shape[0]):
            total = total + ref[k]
        rows = total.shape[0]
        for k in range(out.shape[0]):
            out[k, at : at + rows, :] = total
        at += rows


def sum_copies(*arrived):
    n, _, cols = arrived[0].shape
    rows = sum(part.shape[1] for part in arrived)
    return call(sum_kernel, f32(n, rows, cols), [VMEM] * len(arrived), name="sum_copies")(*arrived)


def in_pieces(value, n):
    return value.reshape(n, -1, value.shape[1])


def grads_kernel(place, grads, basis, own, other):
    rows = own.shape[0]
    basis_high, basis_low = halved(basis[...])

    def product(a, b):
        return lax.dot_general(
            a, b, (((0,), (0,)), ((), ())), preferred_element_type=jnp.float32
        )

    for out, half in ((other, 1 - place[1]), (own, place[1])):
        high, low = halved(grads[:, pl.ds(pl.multiple_of(half * rows, rows), rows)])
        out[...] = product(high, basis_high) + (
            product(low, basis_high) + product(high, basis_low)
        )


def add_kernel(a, b, out):
    out[...] = a[...] + b[...]


def split_store(value, high_ref, low_ref, row):
    high = value.astype(jnp.bfloat16)
    rows = pl.ds(pl.multiple_of(row, BLOCK), value.shape[0])
    high_ref[rows, :] = high
    low_ref[rows, :] = (value - high.astype(jnp.float32)).astype(jnp.bfloat16)


def moments_kernel(place, bounds, *refs):
    acts_refs, grads_refs, out = refs[:4], refs[4:6], refs[6]
    acts_high, acts_low, grads_high, grads_low, moment = refs[7:]
    z, core, lo = place[0], place[1], place[2]
    cols = out.shape[0]
    for from_other in range(2):
        of_core = 1 - core if from_other else core
        first, second = acts_refs[2 * from_other : 2 * from_other + 2]
        sides = slice(cols, 2 * cols) if from_other else slice(0, cols)

        def store(value, distance, far):
            xl = 1 - lo if far else lo
            row = ((xl * 8 + lax.rem(z + distance + 8, 8)) * 2 + of_core) * BLOCK
            split_store(value, acts_high, acts_low, row)

        for at in range(6):
            store(first[at * BLOCK : (at + 1) * BLOCK, sides], FIRST[at // 2], at % 2)
        step = second.shape[0] // 8
        for at in range(8):
            store(second[at * step : at * step + BLOCK, sides], SECOND[at // 2], at % 2)
        for far in range(2):
            ends = [
                second[at * step + BLOCK : (at + 1) * step, sides]
                for at in range(4 * far, 4 * far + 4)
            ]
            store(jnp.concatenate(ends, 0), LAST, far)
        ref = grads_refs[from_other]
        rows = pl.ds(pl.multiple_of(of_core * ref.shape[0], ref.shape[0]), ref.shape[0])
        grads_high[rows, :], grads_low[rows, :] = halved(ref[...])

    def product(a, b):
        return lax.dot_general(
            a, b, (((0,), (0,)), ((), ())), preferred_element_type=jnp.float32
        )

    for seq in range(SEQS):
        first, end = bounds[seq], bounds[seq + 1]
        moment[...] = jnp.zeros_like(moment)

        def block(step, carry):
            rows = pl.ds(pl.multiple_of(step * DEPTH, DEPTH), DEPTH)
            number = step * DEPTH + lax.broadcasted_iota(jnp.int32, (DEPTH, 1), 0)
            mine = (number >= first) & (number < end)
            grads_h = jnp.where(mine, grads_high[rows, :].astype(jnp.float32), 0.0).astype(jnp.bfloat16)
            grads_l = jnp.where(mine, grads_low[rows, :].astype(jnp.float32), 0.0).astype(jnp.bfloat16)
            acts_h, acts_l = acts_high[rows, :], acts_low[rows, :]
            moment[...] += product(acts_h, grads_h) + (
                product(acts_l, grads_h) + product(acts_h, grads_l)
            )
            return carry

        lax.fori_loop(first // DEPTH, (end + DEPTH - 1) // DEPTH, block, 0)
        squared = moment[...] * moment[...]
        if seq == 0:
            out[...] = squared
        elif seq < SEQS - 1:
            out[...] += squared
        else:
            out[...] = (out[...] + squared) * (1.0 / SEQS)


def eigenvalues(place, acts, grads, seq_ids):
    labels = jnp.arange(SEQS + 1, dtype=jnp.int32)
    bounds = jnp.sum((seq_ids[None, :] < labels[:, None]).astype(jnp.int32), axis=1)
    cols, out_cols = acts[0].shape[1] // 2, grads[0].shape[1]
    return call(
        moments_kernel,
        f32(cols, out_cols),
        [SMEM, SMEM] + [VMEM] * (len(acts) + len(grads)),
        [
            pltpu.VMEM((TOKENS, cols), jnp.bfloat16),
            pltpu.VMEM((TOKENS, cols), jnp.bfloat16),
            pltpu.VMEM((TOKENS, out_cols), jnp.bfloat16),
            pltpu.VMEM((TOKENS, out_cols), jnp.bfloat16),
            pltpu.VMEM((cols, out_cols), jnp.float32),
        ],
        name="moments",
        mib=28,
    )(place, bounds, *acts, *grads)


def tied(values, *others):
    held = lax.optimization_barrier((tuple(values), others))
    return list(held[0])


def per_device(activations, act_basis, grads, grad_basis, seq_ids):
    place = jnp.stack([lax.axis_index("z"), lax.axis_index("c"), lax.axis_index("xl")])
    place = place.astype(jnp.int32)
    half, cols = grads.shape[0] // 2, grad_basis.shape[1]

    other_basis = shifted(act_basis, "c").T
    block = jnp.concatenate([activations, shifted(activations, "xl")], 0)
    own, other = call(
        grads_kernel, [f32(half, cols)] * 2, [SMEM, VMEM, VMEM], name="rotate_grads"
    )(place, grads.T, grad_basis)
    block, own, other = tied([block, own, other])

    near = [shifted(block, "z", 1), shifted(block, "z", -1)]
    part = call(add_kernel, f32(half, cols), [VMEM, VMEM], name="add")(own, shifted(other, "c"))
    basis = split_basis(act_basis.T, other_basis)
    part, *basis = tied([part, *basis])
    near = tied(near, part, basis[0])
    part = lax.psum_scatter(part, "z", tiled=True)

    second = [shifted(near[0], "z", 1), shifted(near[1], "z", -1)]
    first_products = products([block, *near], basis)
    *second, first_products = tied([*second, first_products])

    third = [shifted(second[0], "z", 1), shifted(second[1], "z", -1)]
    first_arrived = swapped(in_pieces(first_products, 8), NARROW)
    *third, first_arrived = tied([*third, first_arrived])

    far = [shifted(third[0][:BLOCK], "z", 1), shifted(third[1][BLOCK:], "z", -1)]
    second_products = products([*second, *third], basis)
    first_acts = swapped(sum_copies(first_arrived), NARROW)
    part = part + shifted(part, "xl")
    *far, second_products, part = tied([*far, second_products, part])
    part = lax.all_gather(part, "z", tiled=True)

    third_products = products(far, basis)
    tail = jnp.concatenate([in_pieces(second_products, 8), in_pieces(third_products, 8)], 1)
    tail, first_acts = tied([tail, first_acts])
    second_arrived = swapped(tail, NARROW)
    second_acts = swapped(sum_copies(second_arrived), NARROW)
    acts = [first_acts, second_acts]
    parts = [part, shifted(part, "c")]
    acts = acts + [shifted(value, "c") for value in acts]
    flat = [value.reshape(-1, value.shape[2]) for value in acts]
    return eigenvalues(place, flat, parts, seq_ids)


def solution(mesh):
    split = Mesh(mesh.devices.reshape(tuple(SIZES.values())), tuple(SIZES))
    return jax.shard_map(
        per_device,
        mesh=split,
        in_specs=(P(WIDE, NARROW), P(NARROW, WIDE), P(None, WIDE), P(WIDE, NARROW), P()),
        out_specs=P(WIDE, NARROW),
        check_vma=False,
    )
```

time: 276 us -> 209 us (0.76)
  waiting for transfers between devices: 138 us -> 60.2 us
  matrix products: 41 us -> 0 us
  blocking collectives: 68.8 us -> 28.4 us
  starting transfers between devices: 3.81 us -> 42.6 us
  Pallas kernels: 0 us -> 32.3 us
  local copies, waits for them, and re-layouts: 2.9 us -> 27.7 us
    psum x1 -> x0, waiting for transfers between devices: 82.4 us -> none  [per_device(): rotated_acts = lax.psum(partial_acts, 'narrow')]
    all_gather x1, waiting for transfers between devices: 54.7 us -> 0.01 us  [per_device(): part = lax.all_gather(part, 'z', tiled=True)]
    ppermute x0 -> x15, waiting for transfers between devices: none -> 45.6 us  [shifted(): return lax.ppermute(value, axis, [(i, (i + by) % n) for i in range(n)])]
    dot_general x6 -> x0, matrix products: 41 us -> none  [the longest x1 21.9 us: per_device(): jnp.dot(gathered, act_basis, precision=highest, preferred_element_type=jn...]
    all_to_all x3 -> x1, blocking collectives: 68.8 us -> 28.4 us  [swapped(): return lax.all_to_all(value, axes, 0, 0)]
    pallas_call x0 -> x9, Pallas kernels: none -> 32.3 us  [the longest x3 13.5 us: products(): call(products_kernel, f32(rows, cols), [VMEM] * (len(blocks) + 2), [pltpu...]
    unnamed x6 -> x36, local copies, waits for them, and re-layouts: 1.03 us -> 26.3 us
    ppermute x0 -> x15, starting transfers between devices: none -> 22.4 us  [shifted(): return lax.ppermute(value, axis, [(i, (i + by) % n) for i in range(n)])]
  transfers between devices with their start and end apart: 3 -> 20, of which waited for: 2 -> 9; matrix products, arithmetic and copies ran while one was open for 11% -> 2% of each run, Pallas kernels for 0% -> 9%
where the time goes in v1:
time: 209 us; the launch traced here: 208 us
  waiting for transfers between devices  60.2 us (29%)
  starting transfers between devices  42.6 us (20%)
  Pallas kernels  32.3 us (15%)
  blocking collectives  28.4 us (14%)
  local copies, waits for them, and re-layouts  27.7 us (13%)
  between operations  13.5 us (6%)
  other arithmetic  3.13 us (1%)
    ppermute x15, waiting for transfers between devices, shifted(): return lax.ppermute(value, axis, [(i, (i + by) % n) for i in range(n)])  45.6 us
    all_to_all x1, blocking collectives, swapped(): return lax.all_to_all(value, axes, 0, 0)  28.4 us
    unnamed x36, local copies, waits for them, and re-layouts  26.3 us
    ppermute x15, starting transfers between devices, shifted(): return lax.ppermute(value, axis, [(i, (i + by) % n) for i in range(n)])  22.4 us
    all_to_all x3, starting transfers between devices, swapped(): return lax.all_to_all(value, axes, 0, 0)  20.2 us
    all_to_all x3, waiting for transfers between devices, swapped(): return lax.all_to_all(value, axes, 0, 0)  13.9 us
    pallas_call x3, Pallas kernels, products(): call(products_kernel, f32(rows, cols), [VMEM] * (len(blocks) + 2), [pltpu...  13.5 us
    pallas_call x1, Pallas kernels, eigenvalues(): call(moments_kernel, f32(cols, out_cols), [SMEM, SMEM] + [VMEM] * (len(ac...  10.8 us
  transfers between devices with their start and end apart: 20, of which 9 were waited for; matrix products, arithmetic and copies ran while one was open for 2% of the time, Pallas kernels for 9%

profile of v1, /device:TPU:1, one launch (start us, length us, event | category | flops | bytes accessed | tf_op | source)
XLA Modules:
  0.0 208.0 jit_solution(7591357007580937062)
XLA Ops:
  6.5 3.2 %collective-permute-start.4 = (f32[2176,544]{0,1:T(8,128)}, f32[2176,544]{0,1:T(8,128)}, u32[]{:S(2)}, u32[]{:S(2)}) collective-permute-start(f32[2176,544]{0,1:T(8,128)} %param.6), channel_id=1, source_target_pairs={{0,8},{8,0},{1,9},{9,1},{2,10},{10,2},{3,11},{11,3},{4,12},{12,4},... | collective-permute-start | bytes 14204936 | tf_op jit(solution)/shard_map/ppermute | solution.py:26
  9.9 1.1 copy-done.10
  10.9 1.0 copy-done.15
  11.9 2.0 rotate_grads.1
  14.0 4.3 %collective-permute-done = f32[32,2176]{1,0:T(8,128)S(1)} collective-permute-done((f32[32,2176]{1,0:T(8,128)}, f32[32,2176]{1,0:T(8,128)S(1)}, u32[]{:S(2)}, u32[]{:S(2)}) %collective-permute-start) | collective-permute-done | bytes 278560 | tf_op jit(solution)/shard_map/ppermute | solution.py:26
  18.3 1.0 pad_maximum_fusion.1.refs_0_
  19.3 0.9 collective-permute-start.3
  20.1 2.7 %collective-permute-done.3.b = f32[512,640]{1,0:T(8,128)S(1)} collective-permute-done((f32[512,640]{1,0:T(8,128)S(1)}, f32[512,640]{1,0:T(8,128)S(1)}, u32[]{:S(2)}, u32[]{:S(2)}) %collective-permute-start.3) | collective-permute-done | bytes 1310752 | tf_op jit(solution)/shard_map/ppermute | solution.py:26
  22.8 1.2 add.12
  24.0 2.3 %copy-done.8 = f32[2176,544]{0,1:T(8,128)S(1)} copy-done((f32[2176,544]{0,1:T(8,128)S(1)}, f32[2176,544]{0,1:T(8,128)}, u32[]{:S(2)}) %copy-start.8) | copy-done | bytes 4735000
  26.3 3.8 %split_basis.1 = (bf16[1088,2176]{1,0:T(8,128)(2,1)S(1)}, bf16[1088,2176]{1,0:T(8,128)(2,1)S(1)}) custom-call(f32[544,2176]{1,0:T(8,128)S(1)} %bitcast.14, f32[544,2176]{1,0:T(8,128)} %bitcast.5.other), custom_call_target="tpu_custom_call" | custom-call | flops 1000 | bytes 1000 | tf_op jit(solution)/shard_map/split_basis/pallas_call | solution.py:73
  30.2 2.1 %copy-done = bf16[1088,2176]{1,0:T(8,128)(2,1)} copy-done((bf16[1088,2176]{1,0:T(8,128)(2,1)}, bf16[1088,2176]{1,0:T(8,128)(2,1)S(1)}, u32[]{:S(2)}) %copy-start) | copy-done | bytes 4735000
  32.3 2.2 %copy-done.4 = bf16[1088,2176]{1,0:T(8,128)(2,1)} copy-done((bf16[1088,2176]{1,0:T(8,128)(2,1)}, bf16[1088,2176]{1,0:T(8,128)(2,1)S(1)}, u32[]{:S(2)}) %copy-start.4) | copy-done | bytes 4735000
  34.6 3.9 %collective-permute-start.2 = (f32[64,2176]{1,0:T(8,128)S(1)}, f32[64,2176]{1,0:T(8,128)S(1)}, u32[]{:S(2)}, u32[]{:S(2)}) collective-permute-start(f32[64,2176]{1,0:T(8,128)S(1)} %pad_maximum_fusion.1.refs_0_), channel_id=1, source_target_pairs={{0,112},{16,0},{32,16},{48,32},{64,48},{80,64},{96,80},{112,96},{1... | collective-permute-start | bytes 1671176 | tf_op jit(solution)/shard_map/ppermute | solution.py:26
  38.5 13.0 %collective-permute-done.1.refs_1_ = f32[64,2176]{1,0:T(8,128)S(1)} collective-permute-done((f32[64,2176]{1,0:T(8,128)S(1)}, f32[64,2176]{1,0:T(8,128)S(1)}, u32[]{:S(2)}, u32[]{:S(2)}) %collective-permute-start.1) | collective-permute-done | bytes 557088 | tf_op jit(solution)/shard_map/ppermute | solution.py:26
  51.4 0.4 collective-permute-done.2.refs_2_
  51.9 3.4 %collective-permute-start.6 = (f32[64,2176]{1,0:T(8,128)S(1)}, f32[64,2176]{1,0:T(8,128)S(1)}, u32[]{:S(2)}, u32[]{:S(2)}) collective-permute-start(f32[64,2176]{1,0:T(8,128)S(1)} %collective-permute-done.2.refs_2_), channel_id=1, source_target_pairs={{0,112},{16,0},{32,16},{48,32},{64,48},{80,64},{96,80},{112,96},{1... | collective-permute-start | bytes 1671176 | tf_op jit(solution)/shard_map/ppermute | solution.py:26
  55.3 2.4 %copy-done.1 = bf16[1088,2176]{1,0:T(8,128)(2,1)S(1)} copy-done((bf16[1088,2176]{1,0:T(8,128)(2,1)S(1)}, bf16[1088,2176]{1,0:T(8,128)(2,1)}, u32[]{:S(2)}) %copy-start.1) | copy-done | bytes 4735000
  57.7 2.4 %copy-done.5 = bf16[1088,2176]{1,0:T(8,128)(2,1)S(1)} copy-done((bf16[1088,2176]{1,0:T(8,128)(2,1)S(1)}, bf16[1088,2176]{1,0:T(8,128)(2,1)}, u32[]{:S(2)}) %copy-start.5) | copy-done | bytes 4735000
  60.1 4.9 %products.3 = f32[192,1088]{1,0:T(8,128)} custom-call(f32[64,2176]{1,0:T(8,128)S(1)} %pad_maximum_fusion.1.refs_0_, f32[64,2176]{1,0:T(8,128)S(1)} %collective-permute-done.1.refs_1_, f32[64,2176]{1,0:T(8,128)S(1)} %collective-permute-done.2.refs_2_, bf16[1088,2176]{1,0:T(8,128)(2,1)S(1)} %copy-done.1, bf16[1088,2176]{1,0:T(8,128)(2,1)S(1)} %copy-done.5), custom_call_target="tpu_custom_call" | custom-call | flops 1000 | bytes 1000 | tf_op jit(solution)/shard_map/products/pallas_call | solution.py:99
  64.9 10.8 %collective-permute-done.5.refs_0_ = f32[64,2176]{1,0:T(8,128)S(1)} collective-permute-done((f32[64,2176]{1,0:T(8,128)S(1)}, f32[64,2176]{1,0:T(8,128)S(1)}, u32[]{:S(2)}, u32[]{:S(2)}) %collective-permute-start.5) | collective-permute-done | bytes 557088 | tf_op jit(solution)/shard_map/ppermute | solution.py:26
  75.7 6.6 %all-to-all-start = ((f32[8,24,1088]{2,1,0:T(8,128)}), f32[8,24,1088]{2,1,0:T(8,128)S(1)}, u32[]{:S(2)}, u32[]{:S(2)}) async-start(f32[8,24,1088]{2,1,0:T(8,128)} %bitcast.6), calls=%async_computation | async-start | bytes 1769472 | tf_op jit(solution)/shard_map/all_to_all | solution.py:34
  82.3 2.9 %collective-permute-start.8 = (f32[64,2176]{1,0:T(8,128)S(1)}, f32[64,2176]{1,0:T(8,128)S(1)}, u32[]{:S(2)}, u32[]{:S(2)}) collective-permute-start(f32[64,2176]{1,0:T(8,128)S(1)} %collective-permute-done.6.refs_1_), channel_id=1, source_target_pairs={{0,112},{16,0},{32,16},{48,32},{64,48},{80,64},{96,80},{112,96},{1... | collective-permute-start | bytes 1671176 | tf_op jit(solution)/shard_map/ppermute | solution.py:26
  85.2 10.3 %collective-permute-done.7.refs_2_ = f32[64,2176]{1,0:T(8,128)S(1)} collective-permute-done((f32[64,2176]{1,0:T(8,128)S(1)}, f32[64,2176]{1,0:T(8,128)S(1)}, u32[]{:S(2)}, u32[]{:S(2)}) %collective-permute-start.7) | collective-permute-done | bytes 557088 | tf_op jit(solution)/shard_map/ppermute | solution.py:26
  95.5 1.0 sum_copies.2
  96.5 6.4 %all-to-all-start.1 = ((f32[8,24,1088]{2,1,0:T(8,128)}), f32[8,24,1088]{2,1,0:T(8,128)S(1)}, u32[]{:S(2)}, u32[]{:S(2)}) async-start(f32[8,24,1088]{2,1,0:T(8,128)} %sum_copies.2), calls=%async_computation.2 | async-start | bytes 1769472 | tf_op jit(solution)/shard_map/all_to_all | solution.py:34
  102.9 0.7 slice.7
  103.6 2.4 %collective-permute-start.10 = (f32[32,2176]{1,0:T(8,128)}, f32[32,2176]{1,0:T(8,128)S(1)}, u32[]{:S(2)}, u32[]{:S(2)}) collective-permute-start(f32[32,2176]{1,0:T(8,128)} %slice.7), channel_id=1, source_target_pairs={{0,112},{16,0},{32,16},{48,32},{64,48},{80,64},{96,80},{112,96},{1... | collective-permute-start | bytes 835592 | tf_op jit(solution)/shard_map/ppermute | solution.py:26
  106.0 0.7 slice.6
  107.0 2.3 %copy-done.2 = bf16[1088,2176]{1,0:T(8,128)(2,1)S(1)} copy-done((bf16[1088,2176]{1,0:T(8,128)(2,1)S(1)}, bf16[1088,2176]{1,0:T(8,128)(2,1)}, u32[]{:S(2)}) %copy-start.2) | copy-done | bytes 4735000
  109.4 2.3 %copy-done.6 = bf16[1088,2176]{1,0:T(8,128)(2,1)S(1)} copy-done((bf16[1088,2176]{1,0:T(8,128)(2,1)S(1)}, bf16[1088,2176]{1,0:T(8,128)(2,1)}, u32[]{:S(2)}) %copy-start.6) | copy-done | bytes 4735000
  111.7 1.1 copy-done.12
  112.8 1.1 copy-done.14
  113.8 4.7 %products.4 = f32[256,1088]{1,0:T(8,128)S(1)} custom-call(f32[64,2176]{1,0:T(8,128)S(1)} %copy-done.12, f32[64,2176]{1,0:T(8,128)S(1)} %copy-done.14, f32[64,2176]{1,0:T(8,128)S(1)} %collective-permute-done.7.refs_2_, f32[64,2176]{1,0:T(8,128)S(1)} %collective-permute-done.8.refs_3_, bf16[1088,2176]{1,0:T(8,128)(2,1)S(1)} %copy-done.2, ...), custom_call_target="tpu_custom_call" | custom-call | flops 1000 | bytes 1000 | tf_op jit(solution)/shard_map/products/pallas_call | solution.py:99
  118.6 0.7 add.6
  119.3 2.3 %copy-done.3 = bf16[1088,2176]{1,0:T(8,128)(2,1)S(1)} copy-done((bf16[1088,2176]{1,0:T(8,128)(2,1)S(1)}, bf16[1088,2176]{1,0:T(8,128)(2,1)}, u32[]{:S(2)}) %copy-start.3) | copy-done | bytes 4735000
  121.6 2.3 %copy-done.7 = bf16[1088,2176]{1,0:T(8,128)(2,1)S(1)} copy-done((bf16[1088,2176]{1,0:T(8,128)(2,1)S(1)}, bf16[1088,2176]{1,0:T(8,128)(2,1)}, u32[]{:S(2)}) %copy-start.7) | copy-done | bytes 4735000
  124.0 3.9 %products.5 = f32[64,1088]{1,0:T(8,128)S(1)} custom-call(f32[32,2176]{1,0:T(8,128)} %collective-permute-done.9.refs_0_, f32[32,2176]{1,0:T(8,128)S(1)} %collective-permute-done.10.refs_1_, bf16[1088,2176]{1,0:T(8,128)(2,1)S(1)} %copy-done.3, bf16[1088,2176]{1,0:T(8,128)(2,1)S(1)} %copy-done.7), custom_call_target="tpu_custom_call" | custom-call | flops 1000 | bytes 1000 | tf_op jit(solution)/shard_map/products/pallas_call | solution.py:99
  127.8 1.2 pad_maximum_fusion
  129.1 7.2 %all-to-all-start.2 = ((f32[8,40,1088]{2,1,0:T(8,128)}), f32[8,40,1088]{2,1,0:T(8,128)S(1)}, u32[]{:S(2)}, u32[]{:S(2)}) async-start(f32[8,40,1088]{2,1,0:T(8,128)} %pad_maximum_fusion), calls=%async_computation.3 | async-start | bytes 2949120 | tf_op jit(solution)/shard_map/all_to_all | solution.py:34
  136.4 0.7 all-gather.2.cloned.1.call-update
  137.1 13.9 %all-to-all-done.2.refs_0_ = f32[8,40,1088]{2,1,0:T(8,128)S(1)} async-done(((f32[8,40,1088]{2,1,0:T(8,128)}), f32[8,40,1088]{2,1,0:T(8,128)S(1)}, u32[]{:S(2)}, u32[]{:S(2)}) %all-to-all-start.2) | async-done | bytes 1392672 | tf_op jit(solution)/shard_map/all_to_all | solution.py:34
  151.1 28.4 %all_to_all.20 = f32[8,40,1088]{2,1,0:T(8,128)S(1)} all-to-all(f32[8,40,1088]{2,1,0:T(8,128)S(1)} %sum_copies.3), channel_id=1, replica_groups=mesh['xl'=2,'z'=8,'c'=2,'xh'=2,'y'=4] {'xh','y'}, dimensions={0} | all-to-all | bytes 2785280 | tf_op jit(solution)/shard_map/all_to_all | solution.py:34
  179.6 3.3 %collective-permute-start.13 = (f32[8,40,1088]{2,1,0:T(8,128)S(1)}, f32[8,40,1088]{2,1,0:T(8,128)}, u32[]{:S(2)}, u32[]{:S(2)}) collective-permute-start(f32[8,40,1088]{2,1,0:T(8,128)S(1)} %all_to_all.20), channel_id=1, source_target_pairs={{0,8},{8,0},{1,9},{9,1},{2,10},{10,2},{3,11},{11,3},{4,12},{12,4},... | collective-permute-start | bytes 4177928 | tf_op jit(solution)/shard_map/ppermute | solution.py:26
  182.8 2.0 collective-permute-start.14
  185.0 3.8 %collective-permute-done.12 = f32[8,24,1088]{2,1,0:T(8,128)S(1)} collective-permute-done((f32[8,24,1088]{2,1,0:T(8,128)S(1)}, f32[8,24,1088]{2,1,0:T(8,128)S(1)}, u32[]{:S(2)}, u32[]{:S(2)}) %collective-permute-start.12) | collective-permute-done | bytes 835616 | tf_op jit(solution)/shard_map/ppermute | solution.py:26
  189.1 1.3 copy-done.9
  190.4 10.8 %moments.1 = f32[544,640]{1,0:T(8,128)} custom-call(s32[3]{0:T(128)S(1)} %pad_add_fusion.place, s32[5]{0:T(128)S(1)} %convert_reduce_fusion.bounds, f32[192,1088]{1,0:T(8,128)S(1)} %bitcast.16, f32[320,1088]{1,0:T(8,128)S(1)} %bitcast.13, f32[192,1088]{1,0:T(8,128)S(1)} %bitcast.18, f32[320,1088]{1,0:T(8,128)} %bitcast.12.refs_3_, f32[512,640]{1,0:T(8,128)S(1)} %copy-done.9, ...), custom_call_target="tpu_custom_call" | custom-call | flops 1000 | bytes 1000 | tf_op jit(solution)/shard_map/moments/pallas_call | solution.py:223
  (47 shorter events, 1.2 us)
Async XLA Ops:
  6.5 100.2 %reduce-scatter.2.cloned.1.call-start = ((), (), s32[]{:S(2)}) async-start(), calls=%async_computation.5 | async-start | bytes 1474560 | tf_op jit(solution)/shard_map/reduce_scatter | solution.py:261
  6.5 17.5 %collective-permute-start.4 = (f32[2176,544]{0,1:T(8,128)}, f32[2176,544]{0,1:T(8,128)}, u32[]{:S(2)}, u32[]{:S(2)}) collective-permute-start(f32[2176,544]{0,1:T(8,128)} %param.6), channel_id=1, source_target_pairs={{0,8},{8,0},{1,9},{9,1},{2,10},{10,2},{3,11},{11,3},{4,12},{12,4},... | collective-permute-start | bytes 14204936 | tf_op jit(solution)/shard_map/ppermute | solution.py:26
  9.8 8.5 %collective-permute-start = (f32[32,2176]{1,0:T(8,128)}, f32[32,2176]{1,0:T(8,128)S(1)}, u32[]{:S(2)}, u32[]{:S(2)}) collective-permute-start(f32[32,2176]{1,0:T(8,128)} %param.5), channel_id=1, source_target_pairs={{0,128},{128,0},{1,129},{129,1},{2,130},{130,2},{3,131},{131,3},{4... | collective-permute-start | bytes 835592 | tf_op jit(solution)/shard_map/ppermute | solution.py:26
  9.9 1.1 copy-start.10
  10.9 1.0 copy-start.15
  19.3 3.5 %collective-permute-start.3 = (f32[512,640]{1,0:T(8,128)S(1)}, f32[512,640]{1,0:T(8,128)S(1)}, u32[]{:S(2)}, u32[]{:S(2)}) collective-permute-start(f32[512,640]{1,0:T(8,128)S(1)} %get-tuple-element.33), channel_id=1, source_target_pairs={{0,8},{8,0},{1,9},{9,1},{2,10},{10,2},{3,11},{11,3},{4,12},{12,4},... | collective-permute-start | bytes 3932168 | tf_op jit(solution)/shard_map/ppermute | solution.py:26
  24.0 2.3 %copy-start.8 = (f32[2176,544]{0,1:T(8,128)S(1)}, f32[2176,544]{0,1:T(8,128)}, u32[]{:S(2)}) copy-start(f32[2176,544]{0,1:T(8,128)} %param.6) | copy-start | bytes 14204932
  30.2 2.1 %copy-start = (bf16[1088,2176]{1,0:T(8,128)(2,1)}, bf16[1088,2176]{1,0:T(8,128)(2,1)S(1)}, u32[]{:S(2)}) copy-start(bf16[1088,2176]{1,0:T(8,128)(2,1)S(1)} %get-tuple-element.37.refs_3_.refs_4_.refs_2_) | copy-start | bytes 14204932
  32.3 2.2 %copy-start.4 = (bf16[1088,2176]{1,0:T(8,128)(2,1)}, bf16[1088,2176]{1,0:T(8,128)(2,1)S(1)}, u32[]{:S(2)}) copy-start(bf16[1088,2176]{1,0:T(8,128)(2,1)S(1)} %get-tuple-element.40.refs_4_.refs_5_.refs_3_) | copy-start | bytes 14204932
  34.5 17.0 %collective-permute-start.1 = (f32[64,2176]{1,0:T(8,128)S(1)}, f32[64,2176]{1,0:T(8,128)S(1)}, u32[]{:S(2)}, u32[]{:S(2)}) collective-permute-start(f32[64,2176]{1,0:T(8,128)S(1)} %pad_maximum_fusion.1.refs_0_), channel_id=1, source_target_pairs={{0,16},{16,32},{32,48},{48,64},{64,80},{80,96},{96,112},{112,0},{1... | collective-permute-start | bytes 1671176 | tf_op jit(solution)/shard_map/ppermute | solution.py:26
  34.6 17.3 %collective-permute-start.2 = (f32[64,2176]{1,0:T(8,128)S(1)}, f32[64,2176]{1,0:T(8,128)S(1)}, u32[]{:S(2)}, u32[]{:S(2)}) collective-permute-start(f32[64,2176]{1,0:T(8,128)S(1)} %pad_maximum_fusion.1.refs_0_), channel_id=1, source_target_pairs={{0,112},{16,0},{32,16},{48,32},{64,48},{80,64},{96,80},{112,96},{1... | collective-permute-start | bytes 1671176 | tf_op jit(solution)/shard_map/ppermute | solution.py:26
  51.9 23.8 %collective-permute-start.5 = (f32[64,2176]{1,0:T(8,128)S(1)}, f32[64,2176]{1,0:T(8,128)S(1)}, u32[]{:S(2)}, u32[]{:S(2)}) collective-permute-start(f32[64,2176]{1,0:T(8,128)S(1)} %collective-permute-done.1.refs_1_), channel_id=1, source_target_pairs={{0,16},{16,32},{32,48},{48,64},{64,80},{80,96},{96,112},{112,0},{1... | collective-permute-start | bytes 1671176 | tf_op jit(solution)/shard_map/ppermute | solution.py:26
  51.9 23.8 %collective-permute-start.6 = (f32[64,2176]{1,0:T(8,128)S(1)}, f32[64,2176]{1,0:T(8,128)S(1)}, u32[]{:S(2)}, u32[]{:S(2)}) collective-permute-start(f32[64,2176]{1,0:T(8,128)S(1)} %collective-permute-done.2.refs_2_), channel_id=1, source_target_pairs={{0,112},{16,0},{32,16},{48,32},{64,48},{80,64},{96,80},{112,96},{1... | collective-permute-start | bytes 1671176 | tf_op jit(solution)/shard_map/ppermute | solution.py:26
  55.3 2.4 %copy-start.1 = (bf16[1088,2176]{1,0:T(8,128)(2,1)S(1)}, bf16[1088,2176]{1,0:T(8,128)(2,1)}, u32[]{:S(2)}) copy-start(bf16[1088,2176]{1,0:T(8,128)(2,1)} %copy-done) | copy-start | bytes 14204932
  57.7 2.4 %copy-start.5 = (bf16[1088,2176]{1,0:T(8,128)(2,1)S(1)}, bf16[1088,2176]{1,0:T(8,128)(2,1)}, u32[]{:S(2)}) copy-start(bf16[1088,2176]{1,0:T(8,128)(2,1)} %copy-done.4) | copy-start | bytes 14204932
  75.7 20.8 %copy-start.11 = (f32[64,2176]{1,0:T(8,128)}, f32[64,2176]{1,0:T(8,128)S(1)}, u32[]{:S(2)}) copy-start(f32[64,2176]{1,0:T(8,128)S(1)} %collective-permute-done.5.refs_0_) | copy-start | bytes 1671172
  75.7 20.8 %copy-start.13 = (f32[64,2176]{1,0:T(8,128)}, f32[64,2176]{1,0:T(8,128)S(1)}, u32[]{:S(2)}) copy-start(f32[64,2176]{1,0:T(8,128)S(1)} %collective-permute-done.6.refs_1_) | copy-start | bytes 1671172
  75.7 19.8 %all-to-all-start = ((f32[8,24,1088]{2,1,0:T(8,128)}), f32[8,24,1088]{2,1,0:T(8,128)S(1)}, u32[]{:S(2)}, u32[]{:S(2)}) async-start(f32[8,24,1088]{2,1,0:T(8,128)} %bitcast.6), calls=%async_computation | async-start | bytes 1769472 | tf_op jit(solution)/shard_map/all_to_all | solution.py:34
  82.3 13.2 %collective-permute-start.7 = (f32[64,2176]{1,0:T(8,128)S(1)}, f32[64,2176]{1,0:T(8,128)S(1)}, u32[]{:S(2)}, u32[]{:S(2)}) collective-permute-start(f32[64,2176]{1,0:T(8,128)S(1)} %collective-permute-done.5.refs_0_), channel_id=1, source_target_pairs={{0,16},{16,32},{32,48},{48,64},{64,80},{80,96},{96,112},{112,0},{1... | collective-permute-start | bytes 1671176 | tf_op jit(solution)/shard_map/ppermute | solution.py:26
  82.3 13.2 %collective-permute-start.8 = (f32[64,2176]{1,0:T(8,128)S(1)}, f32[64,2176]{1,0:T(8,128)S(1)}, u32[]{:S(2)}, u32[]{:S(2)}) collective-permute-start(f32[64,2176]{1,0:T(8,128)S(1)} %collective-permute-done.6.refs_1_), channel_id=1, source_target_pairs={{0,112},{16,0},{32,16},{48,32},{64,48},{80,64},{96,80},{112,96},{1... | collective-permute-start | bytes 1671176 | tf_op jit(solution)/shard_map/ppermute | solution.py:26
  96.5 32.6 %all-to-all-start.1 = ((f32[8,24,1088]{2,1,0:T(8,128)}), f32[8,24,1088]{2,1,0:T(8,128)S(1)}, u32[]{:S(2)}, u32[]{:S(2)}) async-start(f32[8,24,1088]{2,1,0:T(8,128)} %sum_copies.2), calls=%async_computation.2 | async-start | bytes 1769472 | tf_op jit(solution)/shard_map/all_to_all | solution.py:34
  103.6 15.7 %collective-permute-start.10 = (f32[32,2176]{1,0:T(8,128)}, f32[32,2176]{1,0:T(8,128)S(1)}, u32[]{:S(2)}, u32[]{:S(2)}) collective-permute-start(f32[32,2176]{1,0:T(8,128)} %slice.7), channel_id=1, source_target_pairs={{0,112},{16,0},{32,16},{48,32},{64,48},{80,64},{96,80},{112,96},{1... | collective-permute-start | bytes 835592 | tf_op jit(solution)/shard_map/ppermute | solution.py:26
  106.7 12.6 %collective-permute-start.9 = (f32[32,2176]{1,0:T(8,128)}, f32[32,2176]{1,0:T(8,128)}, u32[]{:S(2)}, u32[]{:S(2)}) collective-permute-start(f32[32,2176]{1,0:T(8,128)} %slice.6), channel_id=1, source_target_pairs={{0,16},{16,32},{32,48},{48,64},{64,80},{80,96},{96,112},{112,0},{1... | collective-permute-start | bytes 835592 | tf_op jit(solution)/shard_map/ppermute | solution.py:26
  106.7 11.8 %collective-permute-start.11 = (f32[64,640]{1,0:T(8,128)}, f32[64,640]{1,0:T(8,128)S(1)}, u32[]{:S(2)}, u32[]{:S(2)}) collective-permute-start(f32[64,640]{1,0:T(8,128)} %reduce-scatter.2.cloned.1.call-done), channel_id=1, source_target_pairs={{0,128},{128,0},{1,129},{129,1},{2,130},{130,2},{3,131},{131,3},{4... | collective-permute-start | bytes 491528 | tf_op jit(solution)/shard_map/ppermute | solution.py:26
  107.0 2.3 %copy-start.2 = (bf16[1088,2176]{1,0:T(8,128)(2,1)S(1)}, bf16[1088,2176]{1,0:T(8,128)(2,1)}, u32[]{:S(2)}) copy-start(bf16[1088,2176]{1,0:T(8,128)(2,1)} %copy-done) | copy-start | bytes 14204932
  109.4 2.3 %copy-start.6 = (bf16[1088,2176]{1,0:T(8,128)(2,1)S(1)}, bf16[1088,2176]{1,0:T(8,128)(2,1)}, u32[]{:S(2)}) copy-start(bf16[1088,2176]{1,0:T(8,128)(2,1)} %copy-done.4) | copy-start | bytes 14204932
  111.7 1.1 copy-start.12
  112.8 1.1 copy-start.14
  113.8 4.7 %copy-start.16 = (f32[64,640]{1,0:T(8,128)S(1)}, f32[64,640]{1,0:T(8,128)}, u32[]{:S(2)}) copy-start(f32[64,640]{1,0:T(8,128)} %reduce-scatter.2.cloned.1.call-done) | copy-start | bytes 491524
  119.3 2.3 %copy-start.3 = (bf16[1088,2176]{1,0:T(8,128)(2,1)S(1)}, bf16[1088,2176]{1,0:T(8,128)(2,1)}, u32[]{:S(2)}) copy-start(bf16[1088,2176]{1,0:T(8,128)(2,1)} %copy-done) | copy-start | bytes 14204932
  121.6 2.3 %copy-start.7 = (bf16[1088,2176]{1,0:T(8,128)(2,1)S(1)}, bf16[1088,2176]{1,0:T(8,128)(2,1)}, u32[]{:S(2)}) copy-start(bf16[1088,2176]{1,0:T(8,128)(2,1)} %copy-done.4) | copy-start | bytes 14204932
  129.1 21.9 %all-to-all-start.2 = ((f32[8,40,1088]{2,1,0:T(8,128)}), f32[8,40,1088]{2,1,0:T(8,128)S(1)}, u32[]{:S(2)}, u32[]{:S(2)}) async-start(f32[8,40,1088]{2,1,0:T(8,128)} %pad_maximum_fusion), calls=%async_computation.3 | async-start | bytes 2949120 | tf_op jit(solution)/shard_map/all_to_all | solution.py:34
  136.3 46.5 %all-gather.2.cloned.1.call-start = ((), (), s32[]{:S(2)}) async-start(), calls=%async_computation.6 | async-start | bytes 1474560 | tf_op jit(solution)/shard_map/all_gather | solution.py:276
  151.1 33.7 %copy-start.17 = (s32[1024]{0:T(1024)S(1)}, s32[1024]{0:T(1024)}, u32[]{:S(2)}) copy-start(s32[1024]{0:T(1024)} %param.9) | copy-start | bytes 12292
  179.6 9.5 %collective-permute-start.13 = (f32[8,40,1088]{2,1,0:T(8,128)S(1)}, f32[8,40,1088]{2,1,0:T(8,128)}, u32[]{:S(2)}, u32[]{:S(2)}) collective-permute-start(f32[8,40,1088]{2,1,0:T(8,128)S(1)} %all_to_all.20), channel_id=1, source_target_pairs={{0,8},{8,0},{1,9},{9,1},{2,10},{10,2},{3,11},{11,3},{4,12},{12,4},... | collective-permute-start | bytes 4177928 | tf_op jit(solution)/shard_map/ppermute | solution.py:26
  182.8 6.2 %collective-permute-start.14 = (f32[512,640]{1,0:T(8,128)}, f32[512,640]{1,0:T(8,128)S(1)}, u32[]{:S(2)}, u32[]{:S(2)}) collective-permute-start(f32[512,640]{1,0:T(8,128)} %all-gather.2.cloned.1.call-done.refs_4_), channel_id=1, source_target_pairs={{0,8},{8,0},{1,9},{9,1},{2,10},{10,2},{3,11},{11,3},{4,12},{12,4},... | collective-permute-start | bytes 3932168 | tf_op jit(solution)/shard_map/ppermute | solution.py:26
  184.8 3.9 %collective-permute-start.12 = (f32[8,24,1088]{2,1,0:T(8,128)S(1)}, f32[8,24,1088]{2,1,0:T(8,128)S(1)}, u32[]{:S(2)}, u32[]{:S(2)}) collective-permute-start(f32[8,24,1088]{2,1,0:T(8,128)S(1)} %all-to-all-done.1), channel_id=1, source_target_pairs={{0,8},{8,0},{1,9},{9,1},{2,10},{10,2},{3,11},{11,3},{4,12},{12,4},... | collective-permute-start | bytes 2506760 | tf_op jit(solution)/shard_map/ppermute | solution.py:26
  189.1 1.3 copy-start.9
Sparse Core Ops, SparseCore 0:
  34.6 41.2 reduce-scatter.1
  139.0 40.9 all-gather.1

commit v2 on v1

--- a/solution.py
+++ b/solution.py
@@ -15,10 +15,10 @@
 TOKENS = 1024
 BLOCK = 32
 DEPTH = 256
-FIRST, SECOND, LAST = (0, -1, 1), (-2, 2, -3, 3), 4
+TILE = 256
+FIRST, SECOND, LAST = (0, -1, 1, -2, 2), (-3, 3), 4
 VMEM = pl.BlockSpec(memory_space=pltpu.VMEM)
 SMEM = pl.BlockSpec(memory_space=pltpu.SMEM)
-COST = pl.CostEstimate(flops=1000, bytes_accessed=1000, transcendentals=0)
 
 
 def shifted(value, axis, by=1):
@@ -39,7 +39,7 @@
     return high, (value - high.astype(jnp.float32)).astype(jnp.bfloat16)
 
 
-def call(kernel, shapes, in_specs, scratch=(), name=None, mib=12):
+def call(kernel, shapes, in_specs, scratch=(), name=None, mib=12, flops=1000):
     return pl.pallas_call(
         kernel,
         out_shape=shapes,
@@ -47,7 +47,7 @@
         out_specs=jax.tree.map(lambda _: VMEM, shapes),
         scratch_shapes=list(scratch),
         compiler_params=pltpu.CompilerParams(vmem_limit_bytes=mib << 20),
-        cost_estimate=COST,
+        cost_estimate=pl.CostEstimate(flops=flops, bytes_accessed=1000, transcendentals=0),
         name=name,
     )
 
@@ -60,28 +60,27 @@
     return jax.ShapeDtypeStruct(shape, jnp.bfloat16)
 
 
-def basis_kernel(own, other, high, low):
-    rows = own.shape[0]
-    for at, ref in enumerate((own, other)):
-        into = slice(at * rows, (at + 1) * rows)
-        high[into, :], low[into, :] = halved(ref[...])
-
-
-def split_basis(own, other):
-    rows, depth = own.shape
-    shape = bf16(2 * rows, depth)
-    return call(basis_kernel, [shape, shape], [VMEM, VMEM], name="split_basis")(own, other)
-
-
-def products_kernel(*refs):
-    *blocks, basis_high, basis_low, out, both = refs
-    total = out.shape[0]
+def products_kernel(order, *refs):
+    *blocks, own, other, out, both, basis, done = refs
+    total, (own_cols, depth) = out.shape[0], own.shape
+    cols = 2 * own_cols
+    tiles, copies = [], []
+    for start in range(0, cols, TILE):
+        end = min(start + TILE, cols)
+        tiles.append((start, end, []))
+        for ref, base in ((own, 0), (other, own_cols)):
+            low, high = max(start - base, 0), min(end - base, own_cols)
+            if low < high:
+                copy = pltpu.make_async_copy(
+                    ref.at[low:high], basis.at[base + low : base + high], done.at[len(copies)]
+                )
+                copy.start()
+                copies.append(copy)
+                tiles[-1][2].append(copy)
     at = 0
     for ref in blocks:
         rows = ref.shape[0]
-        high, low = halved(ref[...])
-        both[at : at + rows, :] = high
-        both[total + at : total + at + rows, :] = low
+        both[at : at + rows, :], both[total + at : total + at + rows, :] = halved(ref[...])
         at += rows
 
     def product(a, b):
@@ -89,20 +88,31 @@
             a, b, (((1,), (1,)), ((), ())), preferred_element_type=jnp.float32
         )
 
-    main = product(both[...], basis_high[...])
-    out[...] = main[:total] + (main[total:] + product(both[:total, :], basis_low[...]))
-
-
-def products(blocks, basis):
+    for start, end, waits in tiles:
+        for copy in waits:
+            copy.wait()
+        high, low = halved(basis[start:end, :])
+        main = product(both[...], high)
+        out[:, start:end] = main[:total] + (main[total:] + product(both[:total, :], low))
+
+
+def products(blocks, own, other, order, flops):
     rows = sum(block.shape[0] for block in blocks)
-    cols, depth = basis[0].shape
+    own_cols, depth = own.shape
+    cols = 2 * own_cols
     return call(
         products_kernel,
         f32(rows, cols),
-        [VMEM] * (len(blocks) + 2),
-        [pltpu.VMEM((2 * rows, depth), jnp.bfloat16)],
+        [VMEM] * (1 + len(blocks)) + [pl.BlockSpec(memory_space=pltpu.HBM)] * 2,
+        [
+            pltpu.VMEM((2 * rows, depth), jnp.bfloat16),
+            pltpu.VMEM((cols, depth), jnp.float32),
+            pltpu.SemaphoreType.DMA((cols // TILE + 2,)),
+        ],
         name="products",
-    )(*blocks, *basis)
+        mib=22,
+        flops=flops,
+    )(order, *blocks, own, other)
 
 
 def sum_kernel(*refs):
@@ -156,31 +166,30 @@
 
 
 def moments_kernel(place, bounds, *refs):
-    acts_refs, grads_refs, out = refs[:4], refs[4:6], refs[6]
-    acts_high, acts_low, grads_high, grads_low, moment = refs[7:]
+    acts_refs, grads_refs, out = refs[:2], refs[2:4], refs[4]
+    acts_high, acts_low, grads_high, grads_low, moment = refs[5:]
     z, core, lo = place[0], place[1], place[2]
     cols = out.shape[0]
+    first_rows = 2 * len(FIRST) * BLOCK // 8
     for from_other in range(2):
         of_core = 1 - core if from_other else core
-        first, second = acts_refs[2 * from_other : 2 * from_other + 2]
+        ref = acts_refs[from_other]
         sides = slice(cols, 2 * cols) if from_other else slice(0, cols)
-
-        def store(value, distance, far):
-            xl = 1 - lo if far else lo
-            row = ((xl * 8 + lax.rem(z + distance + 8, 8)) * 2 + of_core) * BLOCK
-            split_store(value, acts_high, acts_low, row)
-
-        for at in range(6):
-            store(first[at * BLOCK : (at + 1) * BLOCK, sides], FIRST[at // 2], at % 2)
-        step = second.shape[0] // 8
-        for at in range(8):
-            store(second[at * step : at * step + BLOCK, sides], SECOND[at // 2], at % 2)
-        for far in range(2):
-            ends = [
-                second[at * step + BLOCK : (at + 1) * step, sides]
-                for at in range(4 * far, 4 * far + 4)
-            ]
-            store(jnp.concatenate(ends, 0), LAST, far)
+        blocks = [(distance, far) for distance in FIRST for far in range(2)]
+        rest = [(distance, far) for distance in (*SECOND, LAST) for far in range(2)]
+        for start, size, listed in ((0, first_rows, blocks), (first_rows, 64 - first_rows, rest)):
+            for at, (distance, far) in enumerate(listed):
+                parts, row = [], at * BLOCK
+                while row < (at + 1) * BLOCK:
+                    inner = row % size
+                    count = min(size - inner, (at + 1) * BLOCK - row)
+                    spot = start + inner
+                    parts.append(ref[row // size, spot : spot + count, sides])
+                    row += count
+                value = parts[0] if len(parts) == 1 else jnp.concatenate(parts, 0)
+                xl = 1 - lo if far else lo
+                row = ((xl * 8 + lax.rem(z + distance + 8, 8)) * 2 + of_core) * BLOCK
+                split_store(value, acts_high, acts_low, row)
         ref = grads_refs[from_other]
         rows = pl.ds(pl.multiple_of(of_core * ref.shape[0], ref.shape[0]), ref.shape[0])
         grads_high[rows, :], grads_low[rows, :] = halved(ref[...])
@@ -219,7 +228,7 @@
 def eigenvalues(place, acts, grads, seq_ids):
     labels = jnp.arange(SEQS + 1, dtype=jnp.int32)
     bounds = jnp.sum((seq_ids[None, :] < labels[:, None]).astype(jnp.int32), axis=1)
-    cols, out_cols = acts[0].shape[1] // 2, grads[0].shape[1]
+    cols, out_cols = acts[0].shape[2] // 2, grads[0].shape[1]
     return call(
         moments_kernel,
         f32(cols, out_cols),
@@ -241,50 +250,42 @@
     return list(held[0])
 
 
+def turn(value):
+    return shifted(value[:8, :128], "c")
+
+
 def per_device(activations, act_basis, grads, grad_basis, seq_ids):
     place = jnp.stack([lax.axis_index("z"), lax.axis_index("c"), lax.axis_index("xl")])
     place = place.astype(jnp.int32)
     half, cols = grads.shape[0] // 2, grad_basis.shape[1]
 
-    other_basis = shifted(act_basis, "c").T
-    block = jnp.concatenate([activations, shifted(activations, "xl")], 0)
+    basis = (act_basis.T, shifted(act_basis, "c").T)
     own, other = call(
         grads_kernel, [f32(half, cols)] * 2, [SMEM, VMEM, VMEM], name="rotate_grads"
     )(place, grads.T, grad_basis)
-    block, own, other = tied([block, own, other])
+    part = call(add_kernel, f32(half, cols), [VMEM, VMEM], name="add")(own, shifted(other, "c"))
+    arrived, part = tied([shifted(activations, "xl"), part])
+    block = jnp.concatenate([activations, arrived], 0)
+    part = lax.psum_scatter(part, "z", tiled=True)
 
     near = [shifted(block, "z", 1), shifted(block, "z", -1)]
-    part = call(add_kernel, f32(half, cols), [VMEM, VMEM], name="add")(own, shifted(other, "c"))
-    basis = split_basis(act_basis.T, other_basis)
-    part, *basis = tied([part, *basis])
-    near = tied(near, part, basis[0])
-    part = lax.psum_scatter(part, "z", tiled=True)
-
     second = [shifted(near[0], "z", 1), shifted(near[1], "z", -1)]
-    first_products = products([block, *near], basis)
-    *second, first_products = tied([*second, first_products])
-
     third = [shifted(second[0], "z", 1), shifted(second[1], "z", -1)]
+    first_products = products([block, *near, *second], *basis, turn(second[0]), 1000)
     first_arrived = swapped(in_pieces(first_products, 8), NARROW)
-    *third, first_arrived = tied([*third, first_arrived])
+    third, part = tied([third, part])
 
     far = [shifted(third[0][:BLOCK], "z", 1), shifted(third[1][BLOCK:], "z", -1)]
-    second_products = products([*second, *third], basis)
-    first_acts = swapped(sum_copies(first_arrived), NARROW)
     part = part + shifted(part, "xl")
-    *far, second_products, part = tied([*far, second_products, part])
+    *far, part = tied([*far, part])
     part = lax.all_gather(part, "z", tiled=True)
-
-    third_products = products(far, basis)
-    tail = jnp.concatenate([in_pieces(second_products, 8), in_pieces(third_products, 8)], 1)
-    tail, first_acts = tied([tail, first_acts])
-    second_arrived = swapped(tail, NARROW)
-    second_acts = swapped(sum_copies(second_arrived), NARROW)
-    acts = [first_acts, second_acts]
-    parts = [part, shifted(part, "c")]
-    acts = acts + [shifted(value, "c") for value in acts]
-    flat = [value.reshape(-1, value.shape[2]) for value in acts]
-    return eigenvalues(place, flat, parts, seq_ids)
+    second_products = products([*third, *far], *basis, far[0], 5 * 10**9)
+    second_products, first_arrived = tied([second_products, first_arrived])
+    second_arrived = swapped(in_pieces(second_products, 8), NARROW)
+    acts = swapped(sum_copies(first_arrived, second_arrived), NARROW)
+    return eigenvalues(
+        place, [acts, shifted(acts, "c")], [part, shifted(part, "c")], seq_ids
+    )
 
 
 def solution(mesh):

time: 209 us -> 219 us (1.048)
  waiting for transfers between devices: 60.2 us -> 97.3 us
  local copies, waits for them, and re-layouts: 27.7 us -> 12.2 us
  blocking collectives: 28.4 us -> 20.3 us
  starting transfers between devices: 42.6 us -> 36.4 us
  Pallas kernels: 32.3 us -> 36.4 us
    unnamed x36 -> x21, local copies, waits for them, and re-layouts: 26.3 us -> 11.2 us
    all_to_all x3 -> x2, waiting for transfers between devices: 13.9 us -> 28.2 us  [swapped(): return lax.all_to_all(value, axes, 0, 0)]
    ppermute x15, waiting for transfers between devices: 45.6 us -> 57.5 us  [shifted(): return lax.ppermute(value, axis, [(i, (i + by) % n) for i in range(n)])]
    all_gather x1, waiting for transfers between devices: 0.01 us -> 10.8 us  [per_device(): part = lax.all_gather(part, 'z', tiled=True)]
    all_to_all x3 -> x2, starting transfers between devices: 20.2 us -> 10.4 us  [swapped(): return lax.all_to_all(value, axes, 0, 0)]
    all_to_all x1, blocking collectives: 28.4 us -> 20.3 us  [swapped(): return lax.all_to_all(value, axes, 0, 0)]
    pallas_call x4 -> x2, Pallas kernels: 17.3 us -> 23.1 us  [products(): call(products_kernel, f32(rows, cols), [VMEM] * (1 + len(blocks)) + [pl.B...]
    ppermute x15, starting transfers between devices: 22.4 us -> 26 us  [shifted(): return lax.ppermute(value, axis, [(i, (i + by) % n) for i in range(n)])]
  transfers between devices with their start and end apart: 20 -> 19, of which waited for: 9 -> 10; matrix products, arithmetic and copies ran while one was open for 2% -> 1% of each run, Pallas kernels for 9% -> 12%
where the time goes in v2:
time: 219 us; the launch traced here: 218 us
  waiting for transfers between devices  97.3 us (44%)
  starting transfers between devices  36.4 us (17%)
  Pallas kernels  36.4 us (17%)
  blocking collectives  20.3 us (9%)
  between operations  13.6 us (6%)
  local copies, waits for them, and re-layouts  12.2 us (6%)
    ppermute x15, waiting for transfers between devices, shifted(): return lax.ppermute(value, axis, [(i, (i + by) % n) for i in range(n)])  57.5 us
    all_to_all x2, waiting for transfers between devices, swapped(): return lax.all_to_all(value, axes, 0, 0)  28.2 us
    ppermute x15, starting transfers between devices, shifted(): return lax.ppermute(value, axis, [(i, (i + by) % n) for i in range(n)])  26 us
    pallas_call x2, Pallas kernels, products(): call(products_kernel, f32(rows, cols), [VMEM] * (1 + len(blocks)) + [pl.B...  23.1 us
    all_to_all x1, blocking collectives, swapped(): return lax.all_to_all(value, axes, 0, 0)  20.3 us
    unnamed x21, local copies, waits for them, and re-layouts  11.2 us
    all_gather x1, waiting for transfers between devices, per_device(): part = lax.all_gather(part, 'z', tiled=True)  10.8 us
    all_to_all x2, starting transfers between devices, swapped(): return lax.all_to_all(value, axes, 0, 0)  10.4 us
  transfers between devices with their start and end apart: 19, of which 10 were waited for; matrix products, arithmetic and copies ran while one was open for 1% of the time, Pallas kernels for 12%

profile of v2, /device:TPU:1, one launch (start us, length us, event | category | flops | bytes accessed | tf_op | source)
XLA Modules:
  0.0 217.9 jit_solution(1405509524467479227)
XLA Ops:
  6.5 3.2 %collective-permute-start.11 = (f32[2176,544]{0,1:T(8,128)}, f32[2176,544]{0,1:T(8,128)}, u32[]{:S(2)}, u32[]{:S(2)}) collective-permute-start(f32[2176,544]{0,1:T(8,128)} %param.6), channel_id=1, source_target_pairs={{0,8},{8,0},{1,9},{9,1},{2,10},{10,2},{3,11},{11,3},{4,12},{12,4},... | collective-permute-start | bytes 14204936 | tf_op jit(solution)/shard_map/ppermute | solution.py:26
  9.8 0.1 pad_add_fusion.place
  9.9 1.1 copy-done.4
  10.9 1.0 copy-done.5
  11.9 2.0 rotate_grads.1
  13.9 0.1 collective-permute-start.1
  14.0 0.1 collective-permute-start
  14.2 5.1 %collective-permute-done.1.b = f32[512,640]{1,0:T(8,128)S(1)} collective-permute-done((f32[512,640]{1,0:T(8,128)S(1)}, f32[512,640]{1,0:T(8,128)S(1)}, u32[]{:S(2)}, u32[]{:S(2)}) %collective-permute-start.1) | collective-permute-done | bytes 1310752 | tf_op jit(solution)/shard_map/ppermute | solution.py:26
  19.2 1.2 add.12
  20.4 1.8 collective-permute-done
  22.2 0.0 reduce-scatter.2.cloned.1.call-update
  22.3 0.1 collective-permute-start.2
  22.4 3.9 %collective-permute-start.5 = (f32[64,2176]{1,0:T(8,128)S(1)}, f32[64,2176]{1,0:T(8,128)S(1)}, u32[]{:S(2)}, u32[]{:S(2)}) collective-permute-start(f32[64,2176]{1,0:T(8,128)S(1)} %constant_dynamic-update-slice_fusion.refs_0_), channel_id=1, source_target_pairs={{0,112},{16,0},{32,16},{48,32},{64,48},{80,64},{96,80},{112,96},{1... | collective-permute-start | bytes 1671176 | tf_op jit(solution)/shard_map/ppermute | solution.py:26
  26.3 11.6 %collective-permute-done.2.refs_1_ = f32[64,2176]{1,0:T(8,128)S(1)} collective-permute-done((f32[64,2176]{1,0:T(8,128)S(1)}, f32[64,2176]{1,0:T(8,128)S(1)}, u32[]{:S(2)}, u32[]{:S(2)}) %collective-permute-start.2) | collective-permute-done | bytes 557088 | tf_op jit(solution)/shard_map/ppermute | solution.py:26
  37.9 0.4 collective-permute-done.5.refs_2_
  38.3 3.5 %collective-permute-start.6 = (f32[64,2176]{1,0:T(8,128)S(1)}, f32[64,2176]{1,0:T(8,128)S(1)}, u32[]{:S(2)}, u32[]{:S(2)}) collective-permute-start(f32[64,2176]{1,0:T(8,128)S(1)} %collective-permute-done.5.refs_2_), channel_id=1, source_target_pairs={{0,112},{16,0},{32,16},{48,32},{64,48},{80,64},{96,80},{112,96},{1... | collective-permute-start | bytes 1671176 | tf_op jit(solution)/shard_map/ppermute | solution.py:26
  41.8 18.9 %collective-permute-done.3.refs_3_ = f32[64,2176]{1,0:T(8,128)S(1)} collective-permute-done((f32[64,2176]{1,0:T(8,128)S(1)}, f32[64,2176]{1,0:T(8,128)S(1)}, u32[]{:S(2)}, u32[]{:S(2)}) %collective-permute-start.3) | collective-permute-done | bytes 557088 | tf_op jit(solution)/shard_map/ppermute | solution.py:26
  60.7 2.7 %collective-permute-start.7 = (f32[64,2176]{1,0:T(8,128)S(1)}, f32[64,2176]{1,0:T(8,128)}, u32[]{:S(2)}, u32[]{:S(2)}) collective-permute-start(f32[64,2176]{1,0:T(8,128)S(1)} %collective-permute-done.6.refs_4_), channel_id=1, source_target_pairs={{0,112},{16,0},{32,16},{48,32},{64,48},{80,64},{96,80},{112,96},{1... | collective-permute-start | bytes 1671176 | tf_op jit(solution)/shard_map/ppermute | solution.py:26
  63.4 3.6 %collective-permute-start.12 = (f32[8,128]{1,0:T(8,128)S(1)}, f32[8,128]{1,0:T(8,128)S(1)}, u32[]{:S(2)}, u32[]{:S(2)}) collective-permute-start(f32[8,128]{1,0:T(8,128)S(1)} %slice.12), channel_id=1, source_target_pairs={{0,8},{8,0},{1,9},{9,1},{2,10},{10,2},{3,11},{11,3},{4,12},{12,4},... | collective-permute-start | bytes 12296 | tf_op jit(solution)/shard_map/ppermute | solution.py:26
  67.0 0.8 collective-permute-done.12.order
  67.9 2.3 %copy-done.1 = f32[2176,544]{0,1:T(8,128)S(1)} copy-done((f32[2176,544]{0,1:T(8,128)S(1)}, f32[2176,544]{0,1:T(8,128)}, u32[]{:S(2)}) %copy-start.1) | copy-done | bytes 4735000
  70.2 13.4 %products.3 = f32[320,1088]{1,0:T(8,128)} custom-call(f32[8,128]{1,0:T(8,128)S(1)} %collective-permute-done.12.order, f32[64,2176]{1,0:T(8,128)S(1)} %constant_dynamic-update-slice_fusion.refs_0_, f32[64,2176]{1,0:T(8,128)S(1)} %collective-permute-done.2.refs_1_, f32[64,2176]{1,0:T(8,128)S(1)} %collective-permute-done.5.refs_2_, ...), custom_call_target="tpu_custom_call" | custom-call | flops 1000 | bytes 1000 | tf_op jit(solution)/shard_map/products/pallas_call | solution.py:103
  83.7 6.7 %all-to-all-start = ((f32[8,40,1088]{2,1,0:T(8,128)}), f32[8,40,1088]{2,1,0:T(8,128)S(1)}, u32[]{:S(2)}, u32[]{:S(2)}) async-start(f32[8,40,1088]{2,1,0:T(8,128)} %bitcast.6), calls=%async_computation.1 | async-start | bytes 2949120 | tf_op jit(solution)/shard_map/all_to_all | solution.py:34
  90.3 0.0 reduce-scatter.2.cloned.1.call-done
  90.4 0.1 collective-permute-start.8
  90.5 1.0 slice.10
  91.5 2.7 %collective-permute-start.9 = (f32[32,2176]{1,0:T(8,128)S(1)}, f32[32,2176]{1,0:T(8,128)S(1)}, u32[]{:S(2)}, u32[]{:S(2)}) collective-permute-start(f32[32,2176]{1,0:T(8,128)S(1)} %slice.10), channel_id=1, source_target_pairs={{0,112},{16,0},{32,16},{48,32},{64,48},{80,64},{96,80},{112,96},{1... | collective-permute-start | bytes 835592 | tf_op jit(solution)/shard_map/ppermute | solution.py:26
  94.2 0.3 collective-permute-start.10
  94.5 16.1 %collective-permute-done.10 = f32[64,640]{1,0:T(8,128)S(1)} collective-permute-done((f32[64,640]{1,0:T(8,128)}, f32[64,640]{1,0:T(8,128)S(1)}, u32[]{:S(2)}, u32[]{:S(2)}) %collective-permute-start.10) | collective-permute-done | bytes 163872 | tf_op jit(solution)/shard_map/ppermute | solution.py:26
  110.6 1.6 add.6
  112.2 0.7 copy-done.6
  113.0 2.3 %copy-done.2 = f32[2176,544]{0,1:T(8,128)S(1)} copy-done((f32[2176,544]{0,1:T(8,128)S(1)}, f32[2176,544]{0,1:T(8,128)}, u32[]{:S(2)}) %copy-start.2) | copy-done | bytes 4735000
  115.3 1.0 copy-done.7
  116.2 9.6 %products.2 = f32[192,1088]{1,0:T(8,128)S(1)} custom-call(f32[32,2176]{1,0:T(8,128)S(1)} %collective-permute-done.8.order.refs_2_, f32[64,2176]{1,0:T(8,128)S(1)} %collective-permute-done.4.refs_0_, f32[64,2176]{1,0:T(8,128)} %collective-permute-done.7.refs_1_, f32[32,2176]{1,0:T(8,128)S(1)} %collective-permute-done.8.order.refs_2_, ...), custom_call_target="tpu_custom_call" | custom-call | flops 5000000000 | bytes 1000 | tf_op jit(solution)/shard_map/products/pallas_call | solution.py:103
  125.9 20.3 %all_to_all.15.refs_1_ = f32[8,24,1088]{2,1,0:T(8,128)S(1)} all-to-all(f32[8,24,1088]{2,1,0:T(8,128)S(1)} %bitcast.10), channel_id=1, replica_groups=mesh['xl'=2,'z'=8,'c'=2,'xh'=2,'y'=4] {'xh','y'}, dimensions={0} | all-to-all | bytes 1671168 | tf_op jit(solution)/shard_map/all_to_all | solution.py:34
  146.1 0.2 sum_copies.1
  146.3 1.4 copy-done
  147.7 3.7 %all-to-all-start.2 = ((f32[8,64,1088]{2,1,0:T(8,128)}), f32[8,64,1088]{2,1,0:T(8,128)S(1)}, u32[]{:S(2)}, u32[]{:S(2)}) async-start(f32[8,64,1088]{2,1,0:T(8,128)} %copy-done), calls=%async_computation.3 | async-start | bytes 4718592 | tf_op jit(solution)/shard_map/all_to_all | solution.py:34
  151.5 0.0 all-gather.2.cloned.1.call-start
  151.5 0.7 all-gather.2.cloned.1.call-update
  152.2 28.2 %all-to-all-done.2.refs_0_ = f32[8,64,1088]{2,1,0:T(8,128)S(1)} async-done(((f32[8,64,1088]{2,1,0:T(8,128)}), f32[8,64,1088]{2,1,0:T(8,128)S(1)}, u32[]{:S(2)}, u32[]{:S(2)}) %all-to-all-start.2) | async-done | bytes 2228256 | tf_op jit(solution)/shard_map/all_to_all | solution.py:34
  180.5 1.1 collective-permute-start.13
  181.5 10.8 %all-gather.2.cloned.1.call-done.refs_2_ = f32[512,640]{1,0:T(8,128)} async-done(((f32[64,640]{1,0:T(8,128)}), f32[512,640]{1,0:T(8,128)}) %all-gather.2.cloned.1.call-update) | async-done | bytes 1310736 | tf_op jit(solution)/shard_map/all_gather | solution.py:281
  192.4 4.5 %collective-permute-start.14 = (f32[512,640]{1,0:T(8,128)}, f32[512,640]{1,0:T(8,128)S(1)}, u32[]{:S(2)}, u32[]{:S(2)}) collective-permute-start(f32[512,640]{1,0:T(8,128)} %all-gather.2.cloned.1.call-done.refs_2_), channel_id=1, source_target_pairs={{0,8},{8,0},{1,9},{9,1},{2,10},{10,2},{3,11},{11,3},{4,12},{12,4},... | collective-permute-start | bytes 3932168 | tf_op jit(solution)/shard_map/ppermute | solution.py:26
  196.9 0.1 convert_reduce_fusion.bounds
  197.0 2.7 %collective-permute-done.14.refs_3_ = f32[512,640]{1,0:T(8,128)S(1)} collective-permute-done((f32[512,640]{1,0:T(8,128)}, f32[512,640]{1,0:T(8,128)S(1)}, u32[]{:S(2)}, u32[]{:S(2)}) %collective-permute-start.14) | collective-permute-done | bytes 1310752 | tf_op jit(solution)/shard_map/ppermute | solution.py:26
  199.8 1.3 copy-done.3
  201.1 10.0 %moments.1 = f32[544,640]{1,0:T(8,128)} custom-call(s32[3]{0:T(128)S(1)} %pad_add_fusion.place, s32[5]{0:T(128)S(1)} %convert_reduce_fusion.bounds, f32[8,64,1088]{2,1,0:T(8,128)S(1)} %all-to-all-done.2.refs_0_, f32[8,64,1088]{2,1,0:T(8,128)} %collective-permute-done.13.refs_1_, f32[512,640]{1,0:T(8,128)S(1)} %copy-done.3, ...), custom_call_target="tpu_custom_call" | custom-call | flops 1000 | bytes 1000 | tf_op jit(solution)/shard_map/moments/pallas_call | solution.py:232
  (27 shorter events, 0.1 us)
Async XLA Ops:
  6.5 83.8 %reduce-scatter.2.cloned.1.call-start = ((), (), s32[]{:S(2)}) async-start(), calls=%async_computation.4 | async-start | bytes 1474560 | tf_op jit(solution)/shard_map/reduce_scatter | solution.py:269
  6.5 61.3 %collective-permute-start.11 = (f32[2176,544]{0,1:T(8,128)}, f32[2176,544]{0,1:T(8,128)}, u32[]{:S(2)}, u32[]{:S(2)}) collective-permute-start(f32[2176,544]{0,1:T(8,128)} %param.6), channel_id=1, source_target_pairs={{0,8},{8,0},{1,9},{9,1},{2,10},{10,2},{3,11},{11,3},{4,12},{12,4},... | collective-permute-start | bytes 14204936 | tf_op jit(solution)/shard_map/ppermute | solution.py:26
  9.9 1.1 copy-start.4
  10.9 1.0 copy-start.5
  13.9 5.3 %collective-permute-start.1 = (f32[512,640]{1,0:T(8,128)S(1)}, f32[512,640]{1,0:T(8,128)S(1)}, u32[]{:S(2)}, u32[]{:S(2)}) collective-permute-start(f32[512,640]{1,0:T(8,128)S(1)} %get-tuple-element.18), channel_id=1, source_target_pairs={{0,8},{8,0},{1,9},{9,1},{2,10},{10,2},{3,11},{11,3},{4,12},{12,4},... | collective-permute-start | bytes 3932168 | tf_op jit(solution)/shard_map/ppermute | solution.py:26
  14.0 8.1 %collective-permute-start = (f32[32,2176]{1,0:T(8,128)}, f32[32,2176]{1,0:T(8,128)S(1)}, u32[]{:S(2)}, u32[]{:S(2)}) collective-permute-start(f32[32,2176]{1,0:T(8,128)} %param.5), channel_id=1, source_target_pairs={{0,128},{128,0},{1,129},{129,1},{2,130},{130,2},{3,131},{131,3},{4... | collective-permute-start | bytes 835592 | tf_op jit(solution)/shard_map/ppermute | solution.py:26
  20.4 1.8 copy-start.8
  22.3 15.6 %collective-permute-start.2 = (f32[64,2176]{1,0:T(8,128)S(1)}, f32[64,2176]{1,0:T(8,128)S(1)}, u32[]{:S(2)}, u32[]{:S(2)}) collective-permute-start(f32[64,2176]{1,0:T(8,128)S(1)} %constant_dynamic-update-slice_fusion.refs_0_), channel_id=1, source_target_pairs={{0,16},{16,32},{32,48},{48,64},{64,80},{80,96},{96,112},{112,0},{1... | collective-permute-start | bytes 1671176 | tf_op jit(solution)/shard_map/ppermute | solution.py:26
  22.4 15.9 %collective-permute-start.5 = (f32[64,2176]{1,0:T(8,128)S(1)}, f32[64,2176]{1,0:T(8,128)S(1)}, u32[]{:S(2)}, u32[]{:S(2)}) collective-permute-start(f32[64,2176]{1,0:T(8,128)S(1)} %constant_dynamic-update-slice_fusion.refs_0_), channel_id=1, source_target_pairs={{0,112},{16,0},{32,16},{48,32},{64,48},{80,64},{96,80},{112,96},{1... | collective-permute-start | bytes 1671176 | tf_op jit(solution)/shard_map/ppermute | solution.py:26
  37.9 22.8 %collective-permute-start.3 = (f32[64,2176]{1,0:T(8,128)S(1)}, f32[64,2176]{1,0:T(8,128)S(1)}, u32[]{:S(2)}, u32[]{:S(2)}) collective-permute-start(f32[64,2176]{1,0:T(8,128)S(1)} %collective-permute-done.2.refs_1_), channel_id=1, source_target_pairs={{0,16},{16,32},{32,48},{48,64},{64,80},{80,96},{96,112},{112,0},{1... | collective-permute-start | bytes 1671176 | tf_op jit(solution)/shard_map/ppermute | solution.py:26
  38.3 22.4 %collective-permute-start.6 = (f32[64,2176]{1,0:T(8,128)S(1)}, f32[64,2176]{1,0:T(8,128)S(1)}, u32[]{:S(2)}, u32[]{:S(2)}) collective-permute-start(f32[64,2176]{1,0:T(8,128)S(1)} %collective-permute-done.5.refs_2_), channel_id=1, source_target_pairs={{0,112},{16,0},{32,16},{48,32},{64,48},{80,64},{96,80},{112,96},{1... | collective-permute-start | bytes 1671176 | tf_op jit(solution)/shard_map/ppermute | solution.py:26
  60.7 29.6 %collective-permute-start.4 = (f32[64,2176]{1,0:T(8,128)S(1)}, f32[64,2176]{1,0:T(8,128)S(1)}, u32[]{:S(2)}, u32[]{:S(2)}) collective-permute-start(f32[64,2176]{1,0:T(8,128)S(1)} %collective-permute-done.3.refs_3_), channel_id=1, source_target_pairs={{0,16},{16,32},{32,48},{48,64},{64,80},{80,96},{96,112},{112,0},{1... | collective-permute-start | bytes 1671176 | tf_op jit(solution)/shard_map/ppermute | solution.py:26
  60.7 29.6 %collective-permute-start.7 = (f32[64,2176]{1,0:T(8,128)S(1)}, f32[64,2176]{1,0:T(8,128)}, u32[]{:S(2)}, u32[]{:S(2)}) collective-permute-start(f32[64,2176]{1,0:T(8,128)S(1)} %collective-permute-done.6.refs_4_), channel_id=1, source_target_pairs={{0,112},{16,0},{32,16},{48,32},{64,48},{80,64},{96,80},{112,96},{1... | collective-permute-start | bytes 1671176 | tf_op jit(solution)/shard_map/ppermute | solution.py:26
  63.4 4.5 %collective-permute-start.12 = (f32[8,128]{1,0:T(8,128)S(1)}, f32[8,128]{1,0:T(8,128)S(1)}, u32[]{:S(2)}, u32[]{:S(2)}) collective-permute-start(f32[8,128]{1,0:T(8,128)S(1)} %slice.12), channel_id=1, source_target_pairs={{0,8},{8,0},{1,9},{9,1},{2,10},{10,2},{3,11},{11,3},{4,12},{12,4},... | collective-permute-start | bytes 12296 | tf_op jit(solution)/shard_map/ppermute | solution.py:26
  67.9 2.3 %copy-start.1 = (f32[2176,544]{0,1:T(8,128)S(1)}, f32[2176,544]{0,1:T(8,128)}, u32[]{:S(2)}) copy-start(f32[2176,544]{0,1:T(8,128)} %param.6) | copy-start | bytes 14204932
  83.7 42.2 %all-to-all-start = ((f32[8,40,1088]{2,1,0:T(8,128)}), f32[8,40,1088]{2,1,0:T(8,128)S(1)}, u32[]{:S(2)}, u32[]{:S(2)}) async-start(f32[8,40,1088]{2,1,0:T(8,128)} %bitcast.6), calls=%async_computation.1 | async-start | bytes 2949120 | tf_op jit(solution)/shard_map/all_to_all | solution.py:34
  90.4 21.8 %collective-permute-start.8 = (f32[32,2176]{1,0:T(8,128)S(1)}, f32[32,2176]{1,0:T(8,128)S(1)}, u32[]{:S(2)}, u32[]{:S(2)}) collective-permute-start(f32[32,2176]{1,0:T(8,128)S(1)} %slice.9), channel_id=1, source_target_pairs={{0,16},{16,32},{32,48},{48,64},{64,80},{80,96},{96,112},{112,0},{1... | collective-permute-start | bytes 835592 | tf_op jit(solution)/shard_map/ppermute | solution.py:26
  91.5 20.8 %collective-permute-start.9 = (f32[32,2176]{1,0:T(8,128)S(1)}, f32[32,2176]{1,0:T(8,128)S(1)}, u32[]{:S(2)}, u32[]{:S(2)}) collective-permute-start(f32[32,2176]{1,0:T(8,128)S(1)} %slice.10), channel_id=1, source_target_pairs={{0,112},{16,0},{32,16},{48,32},{64,48},{80,64},{96,80},{112,96},{1... | collective-permute-start | bytes 835592 | tf_op jit(solution)/shard_map/ppermute | solution.py:26
  94.2 16.4 %collective-permute-start.10 = (f32[64,640]{1,0:T(8,128)}, f32[64,640]{1,0:T(8,128)S(1)}, u32[]{:S(2)}, u32[]{:S(2)}) collective-permute-start(f32[64,640]{1,0:T(8,128)} %reduce-scatter.2.cloned.1.call-done), channel_id=1, source_target_pairs={{0,128},{128,0},{1,129},{129,1},{2,130},{130,2},{3,131},{131,3},{4... | collective-permute-start | bytes 491528 | tf_op jit(solution)/shard_map/ppermute | solution.py:26
  112.2 0.7 copy-start.6
  113.0 2.3 %copy-start.2 = (f32[2176,544]{0,1:T(8,128)S(1)}, f32[2176,544]{0,1:T(8,128)}, u32[]{:S(2)}) copy-start(f32[2176,544]{0,1:T(8,128)} %param.6) | copy-start | bytes 14204932
  115.3 1.0 copy-start.7
  146.3 1.4 copy-start
  147.7 49.2 %copy-start.9 = (s32[1024]{0:T(1024)S(1)}, s32[1024]{0:T(1024)}, u32[]{:S(2)}) copy-start(s32[1024]{0:T(1024)} %param.9) | copy-start | bytes 12292
  147.7 32.7 %all-to-all-start.2 = ((f32[8,64,1088]{2,1,0:T(8,128)}), f32[8,64,1088]{2,1,0:T(8,128)S(1)}, u32[]{:S(2)}, u32[]{:S(2)}) async-start(f32[8,64,1088]{2,1,0:T(8,128)} %copy-done), calls=%async_computation.3 | async-start | bytes 4718592 | tf_op jit(solution)/shard_map/all_to_all | solution.py:34
  151.5 40.9 %all-gather.2.cloned.1.call-start = ((), (), s32[]{:S(2)}) async-start(), calls=%async_computation.5 | async-start | bytes 1474560 | tf_op jit(solution)/shard_map/all_gather | solution.py:281
  180.5 19.3 %collective-permute-start.13 = (f32[8,64,1088]{2,1,0:T(8,128)S(1)}, f32[8,64,1088]{2,1,0:T(8,128)}, u32[]{:S(2)}, u32[]{:S(2)}) collective-permute-start(f32[8,64,1088]{2,1,0:T(8,128)S(1)} %all-to-all-done.2.refs_0_), channel_id=1, source_target_pairs={{0,8},{8,0},{1,9},{9,1},{2,10},{10,2},{3,11},{11,3},{4,12},{12,4},... | collective-permute-start | bytes 6684680 | tf_op jit(solution)/shard_map/ppermute | solution.py:26
  192.4 7.4 %collective-permute-start.14 = (f32[512,640]{1,0:T(8,128)}, f32[512,640]{1,0:T(8,128)S(1)}, u32[]{:S(2)}, u32[]{:S(2)}) collective-permute-start(f32[512,640]{1,0:T(8,128)} %all-gather.2.cloned.1.call-done.refs_2_), channel_id=1, source_target_pairs={{0,8},{8,0},{1,9},{9,1},{2,10},{10,2},{3,11},{11,3},{4,12},{12,4},... | collective-permute-start | bytes 3932168 | tf_op jit(solution)/shard_map/ppermute | solution.py:26
  199.8 1.3 copy-start.3
Sparse Core Ops, SparseCore 0:
  22.3 41.4 reduce-scatter.1
  154.1 38.2 all-gather.1

commit v3 on v2

--- a/solution.py
+++ b/solution.py
@@ -15,8 +15,8 @@
 TOKENS = 1024
 BLOCK = 32
 DEPTH = 256
-TILE = 256
 FIRST, SECOND, LAST = (0, -1, 1, -2, 2), (-3, 3), 4
+AROUND = (0, -1, 1, -2, 2, -3, 3, 4)
 VMEM = pl.BlockSpec(memory_space=pltpu.VMEM)
 SMEM = pl.BlockSpec(memory_space=pltpu.SMEM)
 
@@ -44,7 +44,7 @@
         kernel,
         out_shape=shapes,
         in_specs=in_specs,
-        out_specs=jax.tree.map(lambda _: VMEM, shapes),
+        out_specs=VMEM if not isinstance(shapes, list) else [VMEM] * len(shapes),
         scratch_shapes=list(scratch),
         compiler_params=pltpu.CompilerParams(vmem_limit_bytes=mib << 20),
         cost_estimate=pl.CostEstimate(flops=flops, bytes_accessed=1000, transcendentals=0),
@@ -60,23 +60,26 @@
     return jax.ShapeDtypeStruct(shape, jnp.bfloat16)
 
 
-def products_kernel(order, *refs):
-    *blocks, own, other, out, both, basis, done = refs
-    total, (own_cols, depth) = out.shape[0], own.shape
-    cols = 2 * own_cols
-    tiles, copies = [], []
-    for start in range(0, cols, TILE):
-        end = min(start + TILE, cols)
-        tiles.append((start, end, []))
-        for ref, base in ((own, 0), (other, own_cols)):
-            low, high = max(start - base, 0), min(end - base, own_cols)
-            if low < high:
-                copy = pltpu.make_async_copy(
-                    ref.at[low:high], basis.at[base + low : base + high], done.at[len(copies)]
-                )
-                copy.start()
-                copies.append(copy)
-                tiles[-1][2].append(copy)
+def basis_kernel(own, other, out):
+    rows = own.shape[0]
+    for at, ref in enumerate((own, other)):
+        into = slice(at * rows, (at + 1) * rows)
+        out[0, into, :], out[1, into, :] = halved(ref[...])
+
+
+def split_basis(own, other):
+    rows, depth = own.shape
+    return call(
+        basis_kernel,
+        pltpu.VMEM((2, 2 * rows, depth), jnp.bfloat16),
+        [VMEM, VMEM],
+        name="split_basis",
+    )(own, other)
+
+
+def products_kernel(*refs):
+    *blocks, basis, out, both = refs
+    total = out.shape[0]
     at = 0
     for ref in blocks:
         rows = ref.shape[0]
@@ -88,31 +91,22 @@
             a, b, (((1,), (1,)), ((), ())), preferred_element_type=jnp.float32
         )
 
-    for start, end, waits in tiles:
-        for copy in waits:
-            copy.wait()
-        high, low = halved(basis[start:end, :])
-        main = product(both[...], high)
-        out[:, start:end] = main[:total] + (main[total:] + product(both[:total, :], low))
-
-
-def products(blocks, own, other, order, flops):
+    main = product(both[...], basis[0])
+    out[...] = main[:total] + (main[total:] + product(both[:total, :], basis[1]))
+
+
+def products(blocks, basis, flops):
     rows = sum(block.shape[0] for block in blocks)
-    own_cols, depth = own.shape
-    cols = 2 * own_cols
+    _, cols, depth = basis.shape
     return call(
         products_kernel,
         f32(rows, cols),
-        [VMEM] * (1 + len(blocks)) + [pl.BlockSpec(memory_space=pltpu.HBM)] * 2,
-        [
-            pltpu.VMEM((2 * rows, depth), jnp.bfloat16),
-            pltpu.VMEM((cols, depth), jnp.float32),
-            pltpu.SemaphoreType.DMA((cols // TILE + 2,)),
-        ],
+        [VMEM] * (1 + len(blocks)),
+        [pltpu.VMEM((2 * rows, depth), jnp.bfloat16)],
         name="products",
-        mib=22,
+        mib=16,
         flops=flops,
-    )(order, *blocks, own, other)
+    )(*blocks, basis)
 
 
 def sum_kernel(*refs):
@@ -128,10 +122,10 @@
         at += rows
 
 
-def sum_copies(*arrived):
-    n, _, cols = arrived[0].shape
+def sum_copies(*arrived, copies=8):
+    cols = arrived[0].shape[2]
     rows = sum(part.shape[1] for part in arrived)
-    return call(sum_kernel, f32(n, rows, cols), [VMEM] * len(arrived), name="sum_copies")(*arrived)
+    return call(sum_kernel, f32(copies, rows, cols), [VMEM] * len(arrived), name="sum_copies")(*arrived)
 
 
 def in_pieces(value, n):
@@ -154,8 +148,32 @@
         )
 
 
+def halves_kernel(place, own, arrived, keep, send):
+    rows = keep.shape[0]
+    kept = pl.ds(pl.multiple_of(place[2] * rows, rows), rows)
+    sent = pl.ds(pl.multiple_of((1 - place[2]) * rows, rows), rows)
+    keep[...] = own[kept, :] + arrived[kept, :]
+    send[...] = own[sent, :] + arrived[sent, :]
+
+
 def add_kernel(a, b, out):
     out[...] = a[...] + b[...]
+
+
+def pair_kernel(place, own, other, out):
+    rows = own.shape[1]
+    out[pl.ds(pl.multiple_of(place[2] * rows, rows), rows), :] = own[0]
+    out[pl.ds(pl.multiple_of((1 - place[2]) * rows, rows), rows), :] = other[0]
+
+
+def place_kernel(place, *refs):
+    *pieces, out = refs
+    rows = pieces[0].shape[0] // 2
+    for ref, distance in zip(pieces, AROUND):
+        row = lax.rem(place[0] + distance + 8, 8) * rows
+        for lo in range(2):
+            into = pl.ds(pl.multiple_of(lo * 8 * rows + row, rows), rows)
+            out[into, :] = ref[lo * rows : (lo + 1) * rows, :]
 
 
 def split_store(value, high_ref, low_ref, row):
@@ -166,8 +184,8 @@
 
 
 def moments_kernel(place, bounds, *refs):
-    acts_refs, grads_refs, out = refs[:2], refs[2:4], refs[4]
-    acts_high, acts_low, grads_high, grads_low, moment = refs[5:]
+    acts_refs, grads_refs, out = refs[:2], refs[2:-6], refs[-6]
+    acts_high, acts_low, grads_high, grads_low, moment = refs[-5:]
     z, core, lo = place[0], place[1], place[2]
     cols = out.shape[0]
     first_rows = 2 * len(FIRST) * BLOCK // 8
@@ -250,39 +268,56 @@
     return list(held[0])
 
 
-def turn(value):
-    return shifted(value[:8, :128], "c")
-
-
 def per_device(activations, act_basis, grads, grad_basis, seq_ids):
     place = jnp.stack([lax.axis_index("z"), lax.axis_index("c"), lax.axis_index("xl")])
     place = place.astype(jnp.int32)
     half, cols = grads.shape[0] // 2, grad_basis.shape[1]
 
-    basis = (act_basis.T, shifted(act_basis, "c").T)
-    own, other = call(
-        grads_kernel, [f32(half, cols)] * 2, [SMEM, VMEM, VMEM], name="rotate_grads"
-    )(place, grads.T, grad_basis)
-    part = call(add_kernel, f32(half, cols), [VMEM, VMEM], name="add")(own, shifted(other, "c"))
-    arrived, part = tied([shifted(activations, "xl"), part])
+    def placed(kernel, shapes, name, *values):
+        specs = [SMEM] + [VMEM] * len(values)
+        return call(kernel, shapes, specs, name=name)(place, *values)
+
+    other_basis = shifted(act_basis, "c").T
+    arrived = shifted(activations, "xl")
+    own, other = placed(
+        grads_kernel, [f32(half, cols)] * 2, "rotate_grads", grads.T, grad_basis
+    )
+    keep, send = placed(
+        halves_kernel, [f32(half // 2, cols)] * 2, "add_halves", own, shifted(other, "c")
+    )
+    arrived, keep, send = tied([arrived, keep, send])
     block = jnp.concatenate([activations, arrived], 0)
-    part = lax.psum_scatter(part, "z", tiled=True)
 
     near = [shifted(block, "z", 1), shifted(block, "z", -1)]
+    basis = split_basis(act_basis.T, other_basis)
+    part = call(add_kernel, f32(half // 2, cols), [VMEM, VMEM], name="add")(
+        keep, shifted(send, "xl")
+    )
+    *near, basis = tied([*near, basis])
+    part_arrived = swapped(in_pieces(part, 8), "z")
     second = [shifted(near[0], "z", 1), shifted(near[1], "z", -1)]
     third = [shifted(second[0], "z", 1), shifted(second[1], "z", -1)]
-    first_products = products([block, *near, *second], *basis, turn(second[0]), 1000)
+    first_products = products([block, *near, *second], basis, 1000)
+    first_products, part_arrived = tied([first_products, part_arrived])
     first_arrived = swapped(in_pieces(first_products, 8), NARROW)
-    third, part = tied([third, part])
 
     far = [shifted(third[0][:BLOCK], "z", 1), shifted(third[1][BLOCK:], "z", -1)]
-    part = part + shifted(part, "xl")
-    *far, part = tied([*far, part])
-    part = lax.all_gather(part, "z", tiled=True)
-    second_products = products([*third, *far], *basis, far[0], 5 * 10**9)
-    second_products, first_arrived = tied([second_products, first_arrived])
+    second_products = products([*third, *far], basis, 5 * 10**9)
+    piece = sum_copies(part_arrived, copies=1)
+    part = placed(
+        pair_kernel, f32(2 * piece.shape[1], cols), "pair", piece, shifted(piece, "xl")
+    )
+    second_products, first_arrived, part = tied([second_products, first_arrived, part])
     second_arrived = swapped(in_pieces(second_products, 8), NARROW)
+
+    up1, down1 = shifted(part, "z", 1), shifted(part, "z", -1)
+    second_arrived, up1, down1 = tied([second_arrived, up1, down1])
     acts = swapped(sum_copies(first_arrived, second_arrived), NARROW)
+    up2, down2 = shifted(up1, "z", 1), shifted(down1, "z", -1)
+    up3, down3 = shifted(up2, "z", 1), shifted(down2, "z", -1)
+    parts = [part, up1, down1, up2, down2, up3, down3, shifted(up3, "z", 1)]
+    part = placed(place_kernel, f32(half, cols), "place", *parts)
+    acts, part = tied([acts, part])
     return eigenvalues(
         place, [acts, shifted(acts, "c")], [part, shifted(part, "c")], seq_ids
     )

time: 219 us -> 190 us (0.87)
  blocking collectives: 20.3 us -> 0 us
  starting transfers between devices: 36.4 us -> 53.9 us
  between operations: 13.6 us -> 0.2 us
  waiting for transfers between devices: 97.3 us -> 85 us
  local copies, waits for them, and re-layouts: 12.2 us -> 17.5 us
  Pallas kernels: 36.4 us -> 32.6 us
    all_to_all x1 -> x0, blocking collectives: 20.3 us -> none  [swapped(): return lax.all_to_all(value, axes, 0, 0)]
    all_to_all x2 -> x4, starting transfers between devices: 10.4 us -> 28.2 us  [swapped(): return lax.all_to_all(value, axes, 0, 0)]
    all_to_all x2 -> x4, waiting for transfers between devices: 28.2 us -> 15.2 us  [swapped(): return lax.all_to_all(value, axes, 0, 0)]
    ppermute x15 -> x22, waiting for transfers between devices: 57.5 us -> 69.8 us  [shifted(): return lax.ppermute(value, axis, [(i, (i + by) % n) for i in range(n)])]
    all_gather x1 -> x0, waiting for transfers between devices: 10.8 us -> none  [per_device(): part = lax.all_gather(part, 'z', tiled=True)]
    unnamed x21, local copies, waits for them, and re-layouts: 11.2 us -> 15.6 us
    pallas_call x5 -> x10, Pallas kernels: 26.4 us -> 22.9 us  [the longest x2 14.1 us: products(): call(products_kernel, f32(rows, cols), [VMEM] * (1 + len(blocks)), [pltpu...]
    ppermute x15 -> x22, starting transfers between devices: 26 us -> 25.7 us  [shifted(): return lax.ppermute(value, axis, [(i, (i + by) % n) for i in range(n)])]
  transfers between devices with their start and end apart: 19 -> 26, of which waited for: 10 -> 13; matrix products, arithmetic and copies ran while one was open for 1% -> 1% of each run, Pallas kernels for 12% -> 12%
where the time goes in v3:
time: 190 us; the launch traced here: 189 us
  waiting for transfers between devices  85 us (45%)
  starting transfers between devices  53.9 us (28%)
  Pallas kernels  32.6 us (17%)
  local copies, waits for them, and re-layouts  17.5 us (9%)
    ppermute x22, waiting for transfers between devices, shifted(): return lax.ppermute(value, axis, [(i, (i + by) % n) for i in range(n)])  69.8 us
    all_to_all x4, starting transfers between devices, swapped(): return lax.all_to_all(value, axes, 0, 0)  28.2 us
    ppermute x22, starting transfers between devices, shifted(): return lax.ppermute(value, axis, [(i, (i + by) % n) for i in range(n)])  25.7 us
    unnamed x21, local copies, waits for them, and re-layouts  15.6 us
    all_to_all x4, waiting for transfers between devices, swapped(): return lax.all_to_all(value, axes, 0, 0)  15.2 us
    pallas_call x2, Pallas kernels, products(): call(products_kernel, f32(rows, cols), [VMEM] * (1 + len(blocks)), [pltpu...  14.1 us
    pallas_call x1, Pallas kernels, eigenvalues(): call(moments_kernel, f32(cols, out_cols), [SMEM, SMEM] + [VMEM] * (len(ac...  9.69 us
    pallas_call x4, Pallas kernels, placed(): return call(kernel, shapes, specs, name=name)(place, *values)  3.92 us
  transfers between devices with their start and end apart: 26, of which 13 were waited for; matrix products, arithmetic and copies ran while one was open for 1% of the time, Pallas kernels for 12%

profile of v3, /device:TPU:1, one launch (start us, length us, event | category | flops | bytes accessed | tf_op | source)
XLA Modules:
  0.0 189.5 jit_solution(18220727761848625997)
XLA Ops:
  0.0 3.2 %collective-permute-start.4 = (f32[2176,544]{0,1:T(8,128)}, f32[2176,544]{0,1:T(8,128)}, u32[]{:S(2)}, u32[]{:S(2)}) collective-permute-start(f32[2176,544]{0,1:T(8,128)} %param.6), channel_id=1, source_target_pairs={{0,8},{8,0},{1,9},{9,1},{2,10},{10,2},{3,11},{11,3},{4,12},{12,4},... | collective-permute-start | bytes 14204936 | tf_op jit(solution)/shard_map/ppermute | solution.py:26
  3.3 1.1 copy-done.6
  4.4 1.0 copy-done.7
  5.4 2.0 %rotate_grads.1 = (f32[512,640]{1,0:T(8,128)S(1)}, f32[512,640]{1,0:T(8,128)S(1)}) custom-call(s32[3]{0:T(128)S(1)} %pad_add_fusion.place, f32[160,1024]{1,0:T(8,128)S(1)} %bitcast.10, f32[160,640]{1,0:T(8,128)S(1)} %copy-done.7), custom_call_target="tpu_custom_call" | custom-call | flops 1000 | bytes 1000 | tf_op jit(solution)/shard_map/rotate_grads/pallas_call | solution.py:278
  7.6 5.0 %collective-permute-done.1.arrived = f32[512,640]{1,0:T(8,128)S(1)} collective-permute-done((f32[512,640]{1,0:T(8,128)S(1)}, f32[512,640]{1,0:T(8,128)S(1)}, u32[]{:S(2)}, u32[]{:S(2)}) %collective-permute-start.1) | collective-permute-done | bytes 1310752 | tf_op jit(solution)/shard_map/ppermute | solution.py:26
  12.7 0.7 add_halves.1
  13.4 2.2 %collective-permute-done = f32[32,2176]{1,0:T(8,128)S(1)} collective-permute-done((f32[32,2176]{1,0:T(8,128)}, f32[32,2176]{1,0:T(8,128)S(1)}, u32[]{:S(2)}, u32[]{:S(2)}) %collective-permute-start) | collective-permute-done | bytes 278560 | tf_op jit(solution)/shard_map/ppermute | solution.py:26
  15.6 0.3 collective-permute-start.11
  16.0 4.8 %collective-permute-start.3 = (f32[64,2176]{1,0:T(8,128)S(1)}, f32[64,2176]{1,0:T(8,128)S(1)}, u32[]{:S(2)}, u32[]{:S(2)}) collective-permute-start(f32[64,2176]{1,0:T(8,128)S(1)} %constant_dynamic-update-slice_fusion.refs_0_), channel_id=1, source_target_pairs={{0,112},{16,0},{32,16},{48,32},{64,48},{80,64},{96,80},{112,96},{1... | collective-permute-start | bytes 1671176 | tf_op jit(solution)/shard_map/ppermute | solution.py:26
  20.8 9.8 %collective-permute-done.11.b = f32[256,640]{1,0:T(8,128)S(1)} collective-permute-done((f32[256,640]{1,0:T(8,128)S(1)}, f32[256,640]{1,0:T(8,128)S(1)}, u32[]{:S(2)}, u32[]{:S(2)}) %collective-permute-start.11) | collective-permute-done | bytes 655392 | tf_op jit(solution)/shard_map/ppermute | solution.py:26
  30.6 0.9 add.5
  31.5 6.5 %all-to-all-start = ((f32[8,32,640]{2,1,0:T(8,128)}), f32[8,32,640]{2,1,0:T(8,128)S(1)}, u32[]{:S(2)}, u32[]{:S(2)}) async-start(f32[8,32,640]{2,1,0:T(8,128)} %bitcast.6), calls=%async_computation | async-start | bytes 1310720 | tf_op jit(solution)/shard_map/all_to_all | solution.py:34
  38.0 2.3 %copy-done.5 = f32[2176,544]{0,1:T(8,128)S(1)} copy-done((f32[2176,544]{0,1:T(8,128)S(1)}, f32[2176,544]{0,1:T(8,128)}, u32[]{:S(2)}) %copy-start.5) | copy-done | bytes 4735000
  40.3 3.8 %split_basis.1.refs_4_.refs_5_ = bf16[2,1088,2176]{2,1,0:T(8,128)(2,1)S(1)} custom-call(f32[544,2176]{1,0:T(8,128)S(1)} %bitcast.9, f32[544,2176]{1,0:T(8,128)} %bitcast.5.other), custom_call_target="tpu_custom_call" | custom-call | flops 1000 | bytes 1000 | tf_op jit(solution)/shard_map/split_basis/pallas_call | solution.py:72
  44.2 1.5 collective-permute-start.5
  45.7 1.3 collective-permute-start.7
  47.0 20.1 %collective-permute-done.5.refs_3_ = f32[64,2176]{1,0:T(8,128)} collective-permute-done((f32[64,2176]{1,0:T(8,128)S(1)}, f32[64,2176]{1,0:T(8,128)}, u32[]{:S(2)}, u32[]{:S(2)}) %collective-permute-start.5) | collective-permute-done | bytes 557088 | tf_op jit(solution)/shard_map/ppermute | solution.py:26
  67.1 2.7 %collective-permute-start.8 = (f32[64,2176]{1,0:T(8,128)S(1)}, f32[64,2176]{1,0:T(8,128)}, u32[]{:S(2)}, u32[]{:S(2)}) collective-permute-start(f32[64,2176]{1,0:T(8,128)S(1)} %collective-permute-done.7.refs_4_), channel_id=1, source_target_pairs={{0,112},{16,0},{32,16},{48,32},{64,48},{80,64},{96,80},{112,96},{1... | collective-permute-start | bytes 1671176 | tf_op jit(solution)/shard_map/ppermute | solution.py:26
  69.8 8.0 %products.3 = f32[320,1088]{1,0:T(8,128)} custom-call(f32[64,2176]{1,0:T(8,128)S(1)} %constant_dynamic-update-slice_fusion.refs_0_, f32[64,2176]{1,0:T(8,128)S(1)} %collective-permute-done.2.refs_1_, f32[64,2176]{1,0:T(8,128)S(1)} %collective-permute-done.3.refs_2_, f32[64,2176]{1,0:T(8,128)} %collective-permute-done.5.refs_3_, ...), custom_call_target="tpu_custom_call" | custom-call | flops 1000 | bytes 1000 | tf_op jit(solution)/shard_map/products/pallas_call | solution.py:101
  77.8 3.6 %copy-done = bf16[2,1088,2176]{2,1,0:T(8,128)(2,1)} copy-done((bf16[2,1088,2176]{2,1,0:T(8,128)(2,1)}, bf16[2,1088,2176]{2,1,0:T(8,128)(2,1)S(1)}, u32[]{:S(2)}) %copy-start) | copy-done | bytes 9469976
  81.4 6.7 %all-to-all-start.1 = ((f32[8,40,1088]{2,1,0:T(8,128)}), f32[8,40,1088]{2,1,0:T(8,128)S(1)}, u32[]{:S(2)}, u32[]{:S(2)}) async-start(f32[8,40,1088]{2,1,0:T(8,128)} %bitcast.7), calls=%async_computation.1 | async-start | bytes 2949120 | tf_op jit(solution)/shard_map/all_to_all | solution.py:34
  88.1 1.0 slice.8
  89.2 1.0 slice.9
  90.2 2.7 %collective-permute-start.10 = (f32[32,2176]{1,0:T(8,128)S(1)}, f32[32,2176]{1,0:T(8,128)S(1)}, u32[]{:S(2)}, u32[]{:S(2)}) collective-permute-start(f32[32,2176]{1,0:T(8,128)S(1)} %slice.9), channel_id=1, source_target_pairs={{0,112},{16,0},{32,16},{48,32},{64,48},{80,64},{96,80},{112,96},{1... | collective-permute-start | bytes 835592 | tf_op jit(solution)/shard_map/ppermute | solution.py:26
  92.9 0.4 collective-permute-start.12
  93.3 11.5 %collective-permute-done.12.other = f32[1,32,640]{2,1,0:T(8,128)S(1)} collective-permute-done((f32[1,32,640]{2,1,0:T(8,128)S(1)}, f32[1,32,640]{2,1,0:T(8,128)S(1)}, u32[]{:S(2)}, u32[]{:S(2)}) %collective-permute-start.12) | collective-permute-done | bytes 81952 | tf_op jit(solution)/shard_map/ppermute | solution.py:26
  104.8 0.6 pair.1.refs_0_
  105.4 3.7 %copy-done.1 = bf16[2,1088,2176]{2,1,0:T(8,128)(2,1)S(1)} copy-done((bf16[2,1088,2176]{2,1,0:T(8,128)(2,1)S(1)}, bf16[2,1088,2176]{2,1,0:T(8,128)(2,1)}, u32[]{:S(2)}) %copy-start.1) | copy-done | bytes 9469976
  109.1 6.1 %products.2 = f32[192,1088]{1,0:T(8,128)} custom-call(f32[64,2176]{1,0:T(8,128)} %collective-permute-done.6.refs_0_, f32[64,2176]{1,0:T(8,128)} %collective-permute-done.8.refs_1_, f32[32,2176]{1,0:T(8,128)S(1)} %collective-permute-done.9.refs_2_, f32[32,2176]{1,0:T(8,128)S(1)} %collective-permute-done.10.refs_3_, bf16[2,1088,2176]{2,1,0:T(8,128)(2,1)S(1)} %copy-done.1), custom_call_target="tpu_custom_call" | custom-call | flops 5000000000 | bytes 1000 | tf_op jit(solution)/shard_map/products/pallas_call | solution.py:101
  115.2 7.8 %all-to-all-start.2 = ((f32[8,24,1088]{2,1,0:T(8,128)}), f32[8,24,1088]{2,1,0:T(8,128)S(1)}, u32[]{:S(2)}, u32[]{:S(2)}) async-start(f32[8,24,1088]{2,1,0:T(8,128)} %bitcast.8), calls=%async_computation.2 | async-start | bytes 1769472 | tf_op jit(solution)/shard_map/all_to_all | solution.py:34
  123.0 1.4 collective-permute-start.13
  124.5 2.7 %collective-permute-done.14.refs_2_ = f32[64,640]{1,0:T(8,128)S(1)} collective-permute-done((f32[64,640]{1,0:T(8,128)S(1)}, f32[64,640]{1,0:T(8,128)S(1)}, u32[]{:S(2)}, u32[]{:S(2)}) %collective-permute-start.14) | collective-permute-done | bytes 163872 | tf_op jit(solution)/shard_map/ppermute | solution.py:26
  127.2 1.3 collective-permute-done.13.refs_1_
  128.5 4.8 %all-to-all-done.2.refs_1_ = f32[8,24,1088]{2,1,0:T(8,128)S(1)} async-done(((f32[8,24,1088]{2,1,0:T(8,128)}), f32[8,24,1088]{2,1,0:T(8,128)S(1)}, u32[]{:S(2)}, u32[]{:S(2)}) %all-to-all-start.2) | async-done | bytes 835616 | tf_op jit(solution)/shard_map/all_to_all | solution.py:34
  133.5 1.4 copy-done.2
  134.9 7.3 %all-to-all-start.3 = ((f32[8,64,1088]{2,1,0:T(8,128)}), f32[8,64,1088]{2,1,0:T(8,128)S(1)}, u32[]{:S(2)}, u32[]{:S(2)}) async-start(f32[8,64,1088]{2,1,0:T(8,128)} %copy-done.2), calls=%async_computation.3 | async-start | bytes 4718592 | tf_op jit(solution)/shard_map/all_to_all | solution.py:34
  142.3 2.7 %collective-permute-start.16 = (f32[64,640]{1,0:T(8,128)S(1)}, f32[64,640]{1,0:T(8,128)S(1)}, u32[]{:S(2)}, u32[]{:S(2)}) collective-permute-start(f32[64,640]{1,0:T(8,128)S(1)} %collective-permute-done.14.refs_2_), channel_id=1, source_target_pairs={{0,112},{16,0},{32,16},{48,32},{64,48},{80,64},{96,80},{112,96},{1... | collective-permute-start | bytes 491528 | tf_op jit(solution)/shard_map/ppermute | solution.py:26
  144.9 2.7 %collective-permute-done.15.refs_3_ = f32[64,640]{1,0:T(8,128)S(1)} collective-permute-done((f32[64,640]{1,0:T(8,128)S(1)}, f32[64,640]{1,0:T(8,128)S(1)}, u32[]{:S(2)}, u32[]{:S(2)}) %collective-permute-start.15) | collective-permute-done | bytes 163872 | tf_op jit(solution)/shard_map/ppermute | solution.py:26
  147.7 3.0 %collective-permute-start.18 = (f32[64,640]{1,0:T(8,128)S(1)}, f32[64,640]{1,0:T(8,128)S(1)}, u32[]{:S(2)}, u32[]{:S(2)}) collective-permute-start(f32[64,640]{1,0:T(8,128)S(1)} %collective-permute-done.16.refs_4_), channel_id=1, source_target_pairs={{0,112},{16,0},{32,16},{48,32},{64,48},{80,64},{96,80},{112,96},{1... | collective-permute-start | bytes 491528 | tf_op jit(solution)/shard_map/ppermute | solution.py:26
  150.6 2.7 %collective-permute-done.17.refs_5_ = f32[64,640]{1,0:T(8,128)S(1)} collective-permute-done((f32[64,640]{1,0:T(8,128)S(1)}, f32[64,640]{1,0:T(8,128)S(1)}, u32[]{:S(2)}, u32[]{:S(2)}) %collective-permute-start.17) | collective-permute-done | bytes 163872 | tf_op jit(solution)/shard_map/ppermute | solution.py:26
  153.3 5.7 %collective-permute-done.19.refs_7_ = f32[64,640]{1,0:T(8,128)S(1)} collective-permute-done((f32[64,640]{1,0:T(8,128)S(1)}, f32[64,640]{1,0:T(8,128)S(1)}, u32[]{:S(2)}, u32[]{:S(2)}) %collective-permute-start.19) | collective-permute-done | bytes 163872 | tf_op jit(solution)/shard_map/ppermute | solution.py:26
  159.0 0.6 place.1.refs_2_
  159.6 1.0 copy-done.3
  160.7 10.4 %all-to-all-done.3.refs_0_ = f32[8,64,1088]{2,1,0:T(8,128)S(1)} async-done(((f32[8,64,1088]{2,1,0:T(8,128)}), f32[8,64,1088]{2,1,0:T(8,128)S(1)}, u32[]{:S(2)}, u32[]{:S(2)}) %all-to-all-start.3) | async-done | bytes 2228256 | tf_op jit(solution)/shard_map/all_to_all | solution.py:34
  171.1 1.2 collective-permute-start.20
  172.5 6.0 %collective-permute-done.21.refs_3_ = f32[512,640]{1,0:T(8,128)S(1)} collective-permute-done((f32[512,640]{1,0:T(8,128)}, f32[512,640]{1,0:T(8,128)S(1)}, u32[]{:S(2)}, u32[]{:S(2)}) %collective-permute-start.21) | collective-permute-done | bytes 1310752 | tf_op jit(solution)/shard_map/ppermute | solution.py:26
  178.5 1.3 copy-done.4
  179.8 9.7 %moments.1 = f32[544,640]{1,0:T(8,128)} custom-call(s32[3]{0:T(128)S(1)} %pad_add_fusion.place, s32[5]{0:T(128)S(1)} %convert_reduce_fusion.bounds, f32[8,64,1088]{2,1,0:T(8,128)S(1)} %all-to-all-done.3.refs_0_, f32[8,64,1088]{2,1,0:T(8,128)S(1)} %collective-permute-done.20.refs_1_, f32[512,640]{1,0:T(8,128)S(1)} %copy-done.4, ...), custom_call_target="tpu_custom_call" | custom-call | flops 1000 | bytes 1000 | tf_op jit(solution)/shard_map/moments/pallas_call | solution.py:250
  (41 shorter events, 0.9 us)
Async XLA Ops:
  0.0 38.0 %collective-permute-start.4 = (f32[2176,544]{0,1:T(8,128)}, f32[2176,544]{0,1:T(8,128)}, u32[]{:S(2)}, u32[]{:S(2)}) collective-permute-start(f32[2176,544]{0,1:T(8,128)} %param.6), channel_id=1, source_target_pairs={{0,8},{8,0},{1,9},{9,1},{2,10},{10,2},{3,11},{11,3},{4,12},{12,4},... | collective-permute-start | bytes 14204936 | tf_op jit(solution)/shard_map/ppermute | solution.py:26
  3.3 1.1 copy-start.6
  4.4 1.0 copy-start.7
  7.4 8.6 %copy-start.8 = (f32[32,2176]{1,0:T(8,128)S(1)}, f32[32,2176]{1,0:T(8,128)}, u32[]{:S(2)}) copy-start(f32[32,2176]{1,0:T(8,128)} %param.5) | copy-start | bytes 835588
  7.4 5.3 %collective-permute-start.1 = (f32[512,640]{1,0:T(8,128)S(1)}, f32[512,640]{1,0:T(8,128)S(1)}, u32[]{:S(2)}, u32[]{:S(2)}) collective-permute-start(f32[512,640]{1,0:T(8,128)S(1)} %get-tuple-element.26), channel_id=1, source_target_pairs={{0,8},{8,0},{1,9},{9,1},{2,10},{10,2},{3,11},{11,3},{4,12},{12,4},... | collective-permute-start | bytes 3932168 | tf_op jit(solution)/shard_map/ppermute | solution.py:26
  7.5 8.1 %collective-permute-start = (f32[32,2176]{1,0:T(8,128)}, f32[32,2176]{1,0:T(8,128)S(1)}, u32[]{:S(2)}, u32[]{:S(2)}) collective-permute-start(f32[32,2176]{1,0:T(8,128)} %param.5), channel_id=1, source_target_pairs={{0,128},{128,0},{1,129},{129,1},{2,130},{130,2},{3,131},{131,3},{4... | collective-permute-start | bytes 835592 | tf_op jit(solution)/shard_map/ppermute | solution.py:26
  15.6 15.0 %collective-permute-start.11 = (f32[256,640]{1,0:T(8,128)S(1)}, f32[256,640]{1,0:T(8,128)S(1)}, u32[]{:S(2)}, u32[]{:S(2)}) collective-permute-start(f32[256,640]{1,0:T(8,128)S(1)} %get-tuple-element.34), channel_id=1, source_target_pairs={{0,128},{128,0},{1,129},{129,1},{2,130},{130,2},{3,131},{131,3},{4... | collective-permute-start | bytes 1966088 | tf_op jit(solution)/shard_map/ppermute | solution.py:26
  16.0 28.1 %collective-permute-start.3 = (f32[64,2176]{1,0:T(8,128)S(1)}, f32[64,2176]{1,0:T(8,128)S(1)}, u32[]{:S(2)}, u32[]{:S(2)}) collective-permute-start(f32[64,2176]{1,0:T(8,128)S(1)} %constant_dynamic-update-slice_fusion.refs_0_), channel_id=1, source_target_pairs={{0,112},{16,0},{32,16},{48,32},{64,48},{80,64},{96,80},{112,96},{1... | collective-permute-start | bytes 1671176 | tf_op jit(solution)/shard_map/ppermute | solution.py:26
  20.8 23.3 %collective-permute-start.2 = (f32[64,2176]{1,0:T(8,128)S(1)}, f32[64,2176]{1,0:T(8,128)S(1)}, u32[]{:S(2)}, u32[]{:S(2)}) collective-permute-start(f32[64,2176]{1,0:T(8,128)S(1)} %constant_dynamic-update-slice_fusion.refs_0_), channel_id=1, source_target_pairs={{0,16},{16,32},{32,48},{48,64},{64,80},{80,96},{96,112},{112,0},{1... | collective-permute-start | bytes 1671176 | tf_op jit(solution)/shard_map/ppermute | solution.py:26
  31.5 49.9 %all-to-all-start = ((f32[8,32,640]{2,1,0:T(8,128)}), f32[8,32,640]{2,1,0:T(8,128)S(1)}, u32[]{:S(2)}, u32[]{:S(2)}) async-start(f32[8,32,640]{2,1,0:T(8,128)} %bitcast.6), calls=%async_computation | async-start | bytes 1310720 | tf_op jit(solution)/shard_map/all_to_all | solution.py:34
  38.0 2.3 %copy-start.5 = (f32[2176,544]{0,1:T(8,128)S(1)}, f32[2176,544]{0,1:T(8,128)}, u32[]{:S(2)}) copy-start(f32[2176,544]{0,1:T(8,128)} %param.6) | copy-start | bytes 14204932
  44.2 22.9 %collective-permute-start.5 = (f32[64,2176]{1,0:T(8,128)S(1)}, f32[64,2176]{1,0:T(8,128)}, u32[]{:S(2)}, u32[]{:S(2)}) collective-permute-start(f32[64,2176]{1,0:T(8,128)S(1)} %collective-permute-done.2.refs_1_), channel_id=1, source_target_pairs={{0,16},{16,32},{32,48},{48,64},{64,80},{80,96},{96,112},{112,0},{1... | collective-permute-start | bytes 1671176 | tf_op jit(solution)/shard_map/ppermute | solution.py:26
  45.7 21.4 %collective-permute-start.7 = (f32[64,2176]{1,0:T(8,128)S(1)}, f32[64,2176]{1,0:T(8,128)S(1)}, u32[]{:S(2)}, u32[]{:S(2)}) collective-permute-start(f32[64,2176]{1,0:T(8,128)S(1)} %collective-permute-done.3.refs_2_), channel_id=1, source_target_pairs={{0,112},{16,0},{32,16},{48,32},{64,48},{80,64},{96,80},{112,96},{1... | collective-permute-start | bytes 1671176 | tf_op jit(solution)/shard_map/ppermute | solution.py:26
  67.1 21.0 %collective-permute-start.6 = (f32[64,2176]{1,0:T(8,128)}, f32[64,2176]{1,0:T(8,128)}, u32[]{:S(2)}, u32[]{:S(2)}) collective-permute-start(f32[64,2176]{1,0:T(8,128)} %collective-permute-done.5.refs_3_), channel_id=1, source_target_pairs={{0,16},{16,32},{32,48},{48,64},{64,80},{80,96},{96,112},{112,0},{1... | collective-permute-start | bytes 1671176 | tf_op jit(solution)/shard_map/ppermute | solution.py:26
  67.1 22.1 %collective-permute-start.8 = (f32[64,2176]{1,0:T(8,128)S(1)}, f32[64,2176]{1,0:T(8,128)}, u32[]{:S(2)}, u32[]{:S(2)}) collective-permute-start(f32[64,2176]{1,0:T(8,128)S(1)} %collective-permute-done.7.refs_4_), channel_id=1, source_target_pairs={{0,112},{16,0},{32,16},{48,32},{64,48},{80,64},{96,80},{112,96},{1... | collective-permute-start | bytes 1671176 | tf_op jit(solution)/shard_map/ppermute | solution.py:26
  77.8 3.6 %copy-start = (bf16[2,1088,2176]{2,1,0:T(8,128)(2,1)}, bf16[2,1088,2176]{2,1,0:T(8,128)(2,1)S(1)}, u32[]{:S(2)}) copy-start(bf16[2,1088,2176]{2,1,0:T(8,128)(2,1)S(1)} %split_basis.1.refs_4_.refs_5_) | copy-start | bytes 28409860
  81.4 33.7 %all-to-all-start.1 = ((f32[8,40,1088]{2,1,0:T(8,128)}), f32[8,40,1088]{2,1,0:T(8,128)S(1)}, u32[]{:S(2)}, u32[]{:S(2)}) async-start(f32[8,40,1088]{2,1,0:T(8,128)} %bitcast.7), calls=%async_computation.1 | async-start | bytes 2949120 | tf_op jit(solution)/shard_map/all_to_all | solution.py:34
  89.1 16.3 %collective-permute-start.9 = (f32[32,2176]{1,0:T(8,128)S(1)}, f32[32,2176]{1,0:T(8,128)S(1)}, u32[]{:S(2)}, u32[]{:S(2)}) collective-permute-start(f32[32,2176]{1,0:T(8,128)S(1)} %slice.8), channel_id=1, source_target_pairs={{0,16},{16,32},{32,48},{48,64},{64,80},{80,96},{96,112},{112,0},{1... | collective-permute-start | bytes 835592 | tf_op jit(solution)/shard_map/ppermute | solution.py:26
  90.2 15.2 %collective-permute-start.10 = (f32[32,2176]{1,0:T(8,128)S(1)}, f32[32,2176]{1,0:T(8,128)S(1)}, u32[]{:S(2)}, u32[]{:S(2)}) collective-permute-start(f32[32,2176]{1,0:T(8,128)S(1)} %slice.9), channel_id=1, source_target_pairs={{0,112},{16,0},{32,16},{48,32},{64,48},{80,64},{96,80},{112,96},{1... | collective-permute-start | bytes 835592 | tf_op jit(solution)/shard_map/ppermute | solution.py:26
  92.9 11.9 %collective-permute-start.12 = (f32[1,32,640]{2,1,0:T(8,128)S(1)}, f32[1,32,640]{2,1,0:T(8,128)S(1)}, u32[]{:S(2)}, u32[]{:S(2)}) collective-permute-start(f32[1,32,640]{2,1,0:T(8,128)S(1)} %sum_copies.2.own), channel_id=1, source_target_pairs={{0,128},{128,0},{1,129},{129,1},{2,130},{130,2},{3,131},{131,3},{4... | collective-permute-start | bytes 245768 | tf_op jit(solution)/shard_map/ppermute | solution.py:26
  105.4 3.7 %copy-start.1 = (bf16[2,1088,2176]{2,1,0:T(8,128)(2,1)S(1)}, bf16[2,1088,2176]{2,1,0:T(8,128)(2,1)}, u32[]{:S(2)}) copy-start(bf16[2,1088,2176]{2,1,0:T(8,128)(2,1)} %copy-done) | copy-start | bytes 28409860
  115.2 18.1 %all-to-all-start.2 = ((f32[8,24,1088]{2,1,0:T(8,128)}), f32[8,24,1088]{2,1,0:T(8,128)S(1)}, u32[]{:S(2)}, u32[]{:S(2)}) async-start(f32[8,24,1088]{2,1,0:T(8,128)} %bitcast.8), calls=%async_computation.2 | async-start | bytes 1769472 | tf_op jit(solution)/shard_map/all_to_all | solution.py:34
  123.0 4.2 %collective-permute-start.14 = (f32[64,640]{1,0:T(8,128)S(1)}, f32[64,640]{1,0:T(8,128)S(1)}, u32[]{:S(2)}, u32[]{:S(2)}) collective-permute-start(f32[64,640]{1,0:T(8,128)S(1)} %pair.1.refs_0_), channel_id=1, source_target_pairs={{0,112},{16,0},{32,16},{48,32},{64,48},{80,64},{96,80},{112,96},{1... | collective-permute-start | bytes 491528 | tf_op jit(solution)/shard_map/ppermute | solution.py:26
  123.0 5.4 %collective-permute-start.13 = (f32[64,640]{1,0:T(8,128)S(1)}, f32[64,640]{1,0:T(8,128)S(1)}, u32[]{:S(2)}, u32[]{:S(2)}) collective-permute-start(f32[64,640]{1,0:T(8,128)S(1)} %pair.1.refs_0_), channel_id=1, source_target_pairs={{0,16},{16,32},{32,48},{48,64},{64,80},{80,96},{96,112},{112,0},{1... | collective-permute-start | bytes 491528 | tf_op jit(solution)/shard_map/ppermute | solution.py:26
  133.5 1.4 copy-start.2
  134.9 36.2 %all-to-all-start.3 = ((f32[8,64,1088]{2,1,0:T(8,128)}), f32[8,64,1088]{2,1,0:T(8,128)S(1)}, u32[]{:S(2)}, u32[]{:S(2)}) async-start(f32[8,64,1088]{2,1,0:T(8,128)} %copy-done.2), calls=%async_computation.3 | async-start | bytes 4718592 | tf_op jit(solution)/shard_map/all_to_all | solution.py:34
  142.2 30.2 %copy-start.9 = (s32[1024]{0:T(1024)S(1)}, s32[1024]{0:T(1024)}, u32[]{:S(2)}) copy-start(s32[1024]{0:T(1024)} %param.9) | copy-start | bytes 12292
  142.2 5.5 %collective-permute-start.15 = (f32[64,640]{1,0:T(8,128)S(1)}, f32[64,640]{1,0:T(8,128)S(1)}, u32[]{:S(2)}, u32[]{:S(2)}) collective-permute-start(f32[64,640]{1,0:T(8,128)S(1)} %collective-permute-done.13.refs_1_), channel_id=1, source_target_pairs={{0,16},{16,32},{32,48},{48,64},{64,80},{80,96},{96,112},{112,0},{1... | collective-permute-start | bytes 491528 | tf_op jit(solution)/shard_map/ppermute | solution.py:26
  142.3 5.4 %collective-permute-start.16 = (f32[64,640]{1,0:T(8,128)S(1)}, f32[64,640]{1,0:T(8,128)S(1)}, u32[]{:S(2)}, u32[]{:S(2)}) collective-permute-start(f32[64,640]{1,0:T(8,128)S(1)} %collective-permute-done.14.refs_2_), channel_id=1, source_target_pairs={{0,112},{16,0},{32,16},{48,32},{64,48},{80,64},{96,80},{112,96},{1... | collective-permute-start | bytes 491528 | tf_op jit(solution)/shard_map/ppermute | solution.py:26
  147.6 5.7 %collective-permute-start.17 = (f32[64,640]{1,0:T(8,128)S(1)}, f32[64,640]{1,0:T(8,128)S(1)}, u32[]{:S(2)}, u32[]{:S(2)}) collective-permute-start(f32[64,640]{1,0:T(8,128)S(1)} %collective-permute-done.15.refs_3_), channel_id=1, source_target_pairs={{0,16},{16,32},{32,48},{48,64},{64,80},{80,96},{96,112},{112,0},{1... | collective-permute-start | bytes 491528 | tf_op jit(solution)/shard_map/ppermute | solution.py:26
  147.7 5.7 %collective-permute-start.18 = (f32[64,640]{1,0:T(8,128)S(1)}, f32[64,640]{1,0:T(8,128)S(1)}, u32[]{:S(2)}, u32[]{:S(2)}) collective-permute-start(f32[64,640]{1,0:T(8,128)S(1)} %collective-permute-done.16.refs_4_), channel_id=1, source_target_pairs={{0,112},{16,0},{32,16},{48,32},{64,48},{80,64},{96,80},{112,96},{1... | collective-permute-start | bytes 491528 | tf_op jit(solution)/shard_map/ppermute | solution.py:26
  153.3 5.7 %collective-permute-start.19 = (f32[64,640]{1,0:T(8,128)S(1)}, f32[64,640]{1,0:T(8,128)S(1)}, u32[]{:S(2)}, u32[]{:S(2)}) collective-permute-start(f32[64,640]{1,0:T(8,128)S(1)} %collective-permute-done.17.refs_5_), channel_id=1, source_target_pairs={{0,16},{16,32},{32,48},{48,64},{64,80},{80,96},{96,112},{112,0},{1... | collective-permute-start | bytes 491528 | tf_op jit(solution)/shard_map/ppermute | solution.py:26
  159.6 1.1 copy-start.3
  171.1 7.3 %collective-permute-start.20 = (f32[8,64,1088]{2,1,0:T(8,128)S(1)}, f32[8,64,1088]{2,1,0:T(8,128)S(1)}, u32[]{:S(2)}, u32[]{:S(2)}) collective-permute-start(f32[8,64,1088]{2,1,0:T(8,128)S(1)} %all-to-all-done.3.refs_0_), channel_id=1, source_target_pairs={{0,8},{8,0},{1,9},{9,1},{2,10},{10,2},{3,11},{11,3},{4,12},{12,4},... | collective-permute-start | bytes 6684680 | tf_op jit(solution)/shard_map/ppermute | solution.py:26
  172.4 6.1 %collective-permute-start.21 = (f32[512,640]{1,0:T(8,128)}, f32[512,640]{1,0:T(8,128)S(1)}, u32[]{:S(2)}, u32[]{:S(2)}) collective-permute-start(f32[512,640]{1,0:T(8,128)} %copy-done.3), channel_id=1, source_target_pairs={{0,8},{8,0},{1,9},{9,1},{2,10},{10,2},{3,11},{11,3},{4,12},{12,4},... | collective-permute-start | bytes 3932168 | tf_op jit(solution)/shard_map/ppermute | solution.py:26
  178.5 1.3 copy-start.4

commit v4 on v3

--- a/solution.py
+++ b/solution.py
@@ -282,31 +282,32 @@
     own, other = placed(
         grads_kernel, [f32(half, cols)] * 2, "rotate_grads", grads.T, grad_basis
     )
+    arrived, own, other = tied([arrived, own, other])
+    block = jnp.concatenate([activations, arrived], 0)
     keep, send = placed(
         halves_kernel, [f32(half // 2, cols)] * 2, "add_halves", own, shifted(other, "c")
     )
-    arrived, keep, send = tied([arrived, keep, send])
-    block = jnp.concatenate([activations, arrived], 0)
 
     near = [shifted(block, "z", 1), shifted(block, "z", -1)]
-    basis = split_basis(act_basis.T, other_basis)
     part = call(add_kernel, f32(half // 2, cols), [VMEM, VMEM], name="add")(
         keep, shifted(send, "xl")
     )
-    *near, basis = tied([*near, basis])
     part_arrived = swapped(in_pieces(part, 8), "z")
     second = [shifted(near[0], "z", 1), shifted(near[1], "z", -1)]
+    basis = split_basis(*tied([act_basis.T, other_basis], near[0]))
+    *second, basis = tied([*second, basis])
     third = [shifted(second[0], "z", 1), shifted(second[1], "z", -1)]
     first_products = products([block, *near, *second], basis, 1000)
     first_products, part_arrived = tied([first_products, part_arrived])
     first_arrived = swapped(in_pieces(first_products, 8), NARROW)
 
     far = [shifted(third[0][:BLOCK], "z", 1), shifted(third[1][BLOCK:], "z", -1)]
+    basis = split_basis(*tied([act_basis.T, other_basis], third[0]))
+    *far, basis = tied([*far, basis])
     second_products = products([*third, *far], basis, 5 * 10**9)
     piece = sum_copies(part_arrived, copies=1)
-    part = placed(
-        pair_kernel, f32(2 * piece.shape[1], cols), "pair", piece, shifted(piece, "xl")
-    )
+    far_piece, second_products = tied([shifted(piece, "xl"), second_products])
+    part = placed(pair_kernel, f32(2 * piece.shape[1], cols), "pair", piece, far_piece)
     second_products, first_arrived, part = tied([second_products, first_arrived, part])
     second_arrived = swapped(in_pieces(second_products, 8), NARROW)
 
@@ -317,10 +318,8 @@
     up3, down3 = shifted(up2, "z", 1), shifted(down2, "z", -1)
     parts = [part, up1, down1, up2, down2, up3, down3, shifted(up3, "z", 1)]
     part = placed(place_kernel, f32(half, cols), "place", *parts)
-    acts, part = tied([acts, part])
-    return eigenvalues(
-        place, [acts, shifted(acts, "c")], [part, shifted(part, "c")], seq_ids
-    )
+    acts, *parts = tied([acts, part, shifted(part, "c")])
+    return eigenvalues(place, [acts, shifted(acts, "c")], parts, seq_ids)
 
 
 def solution(mesh):

time: 190 us -> 177 us (0.932)
  waiting for transfers between devices: 85 us -> 66.2 us
  starting transfers between devices: 53.9 us -> 58.6 us
  Pallas kernels: 32.6 us -> 35.6 us
  local copies, waits for them, and re-layouts: 17.5 us -> 14.9 us
    ppermute x22, waiting for transfers between devices: 69.8 us -> 58.8 us  [shifted(): return lax.ppermute(value, axis, [(i, (i + by) % n) for i in range(n)])]
    all_to_all x4, waiting for transfers between devices: 15.2 us -> 7.42 us  [swapped(): return lax.all_to_all(value, axes, 0, 0)]
    ppermute x22, starting transfers between devices: 25.7 us -> 31.4 us  [shifted(): return lax.ppermute(value, axis, [(i, (i + by) % n) for i in range(n)])]
    pallas_call x1 -> x2, Pallas kernels: 3.81 us -> 7.61 us  [split_basis(): call(basis_kernel, pltpu.VMEM((2, 2 * rows, depth), jnp.bfloat16), [VMEM,...]
    unnamed x21 -> x23, local copies, waits for them, and re-layouts: 15.6 us -> 13 us
  transfers between devices with their start and end apart: 26 -> 26, of which waited for: 13 -> 14; matrix products, arithmetic and copies ran while one was open for 1% -> 1% of each run, Pallas kernels for 12% -> 15%
where the time goes in v4:
time: 177 us; the launch traced here: 176 us
  waiting for transfers between devices  66.2 us (37%)
  starting transfers between devices  58.6 us (33%)
  Pallas kernels  35.6 us (20%)
  local copies, waits for them, and re-layouts  14.9 us (8%)
    ppermute x22, waiting for transfers between devices, shifted(): return lax.ppermute(value, axis, [(i, (i + by) % n) for i in range(n)])  58.8 us
    ppermute x22, starting transfers between devices, shifted(): return lax.ppermute(value, axis, [(i, (i + by) % n) for i in range(n)])  31.4 us
    all_to_all x4, starting transfers between devices, swapped(): return lax.all_to_all(value, axes, 0, 0)  27.3 us
    pallas_call x2, Pallas kernels, products(): call(products_kernel, f32(rows, cols), [VMEM] * (1 + len(blocks)), [pltpu...  14.1 us
    unnamed x23, local copies, waits for them, and re-layouts  13 us
    pallas_call x1, Pallas kernels, eigenvalues(): call(moments_kernel, f32(cols, out_cols), [SMEM, SMEM] + [VMEM] * (len(ac...  8.84 us
    pallas_call x2, Pallas kernels, split_basis(): call(basis_kernel, pltpu.VMEM((2, 2 * rows, depth), jnp.bfloat16), [VMEM,...  7.61 us
    all_to_all x4, waiting for transfers between devices, swapped(): return lax.all_to_all(value, axes, 0, 0)  7.42 us
  transfers between devices with their start and end apart: 26, of which 14 were waited for; matrix products, arithmetic and copies ran while one was open for 1% of the time, Pallas kernels for 15%

profile of v4, /device:TPU:1, one launch (start us, length us, event | category | flops | bytes accessed | tf_op | source)
XLA Modules:
  0.0 175.8 jit_solution(8468739979681492928)
XLA Ops:
  0.0 3.2 %collective-permute-start.5 = (f32[2176,544]{0,1:T(8,128)}, f32[2176,544]{0,1:T(8,128)}, u32[]{:S(2)}, u32[]{:S(2)}) collective-permute-start(f32[2176,544]{0,1:T(8,128)} %param.6), channel_id=1, source_target_pairs={{0,8},{8,0},{1,9},{9,1},{2,10},{10,2},{3,11},{11,3},{4,12},{12,4},... | collective-permute-start | bytes 14204936 | tf_op jit(solution)/shard_map/ppermute | solution.py:26
  3.3 1.1 copy-done.7
  4.4 1.0 copy-done.8
  5.4 2.0 %rotate_grads.1 = (f32[512,640]{1,0:T(8,128)S(1)}, f32[512,640]{1,0:T(8,128)S(1)}) custom-call(s32[3]{0:T(128)S(1)} %pad_add_fusion.place, f32[160,1024]{1,0:T(8,128)S(1)} %bitcast.11, f32[160,640]{1,0:T(8,128)S(1)} %copy-done.8), custom_call_target="tpu_custom_call" | custom-call | flops 1000 | bytes 1000 | tf_op jit(solution)/shard_map/rotate_grads/pallas_call | solution.py:278
  7.4 4.3 %collective-permute-done = f32[32,2176]{1,0:T(8,128)S(1)} collective-permute-done((f32[32,2176]{1,0:T(8,128)}, f32[32,2176]{1,0:T(8,128)S(1)}, u32[]{:S(2)}, u32[]{:S(2)}) %collective-permute-start) | collective-permute-done | bytes 278560 | tf_op jit(solution)/shard_map/ppermute | solution.py:26
  11.7 0.8 collective-permute-start.6
  12.5 2.7 %collective-permute-done.6.arrived = f32[512,640]{1,0:T(8,128)S(1)} collective-permute-done((f32[512,640]{1,0:T(8,128)S(1)}, f32[512,640]{1,0:T(8,128)S(1)}, u32[]{:S(2)}, u32[]{:S(2)}) %collective-permute-start.6) | collective-permute-done | bytes 1310752 | tf_op jit(solution)/shard_map/ppermute | solution.py:26
  15.2 0.7 add_halves.1
  16.1 5.1 %collective-permute-start.2 = (f32[64,2176]{1,0:T(8,128)S(1)}, f32[64,2176]{1,0:T(8,128)S(1)}, u32[]{:S(2)}, u32[]{:S(2)}) collective-permute-start(f32[64,2176]{1,0:T(8,128)S(1)} %constant_dynamic-update-slice_fusion.refs_0_), channel_id=1, source_target_pairs={{0,112},{16,0},{32,16},{48,32},{64,48},{80,64},{96,80},{112,96},{1... | collective-permute-start | bytes 1671176 | tf_op jit(solution)/shard_map/ppermute | solution.py:26
  21.2 10.8 %collective-permute-done.7.b = f32[256,640]{1,0:T(8,128)S(1)} collective-permute-done((f32[256,640]{1,0:T(8,128)S(1)}, f32[256,640]{1,0:T(8,128)S(1)}, u32[]{:S(2)}, u32[]{:S(2)}) %collective-permute-start.7) | collective-permute-done | bytes 655392 | tf_op jit(solution)/shard_map/ppermute | solution.py:26
  32.0 0.9 add.5
  32.9 6.5 %all-to-all-start = ((f32[8,32,640]{2,1,0:T(8,128)}), f32[8,32,640]{2,1,0:T(8,128)S(1)}, u32[]{:S(2)}, u32[]{:S(2)}) async-start(f32[8,32,640]{2,1,0:T(8,128)} %bitcast.6), calls=%async_computation | async-start | bytes 1310720 | tf_op jit(solution)/shard_map/all_to_all | solution.py:34
  39.3 2.7 %collective-permute-start.4 = (f32[64,2176]{1,0:T(8,128)S(1)}, f32[64,2176]{1,0:T(8,128)S(1)}, u32[]{:S(2)}, u32[]{:S(2)}) collective-permute-start(f32[64,2176]{1,0:T(8,128)S(1)} %collective-permute-done.2.refs_2_), channel_id=1, source_target_pairs={{0,112},{16,0},{32,16},{48,32},{64,48},{80,64},{96,80},{112,96},{1... | collective-permute-start | bytes 1671176 | tf_op jit(solution)/shard_map/ppermute | solution.py:26
  42.0 2.3 %copy-done = f32[2176,544]{0,1:T(8,128)S(1)} copy-done((f32[2176,544]{0,1:T(8,128)S(1)}, f32[2176,544]{0,1:T(8,128)}, u32[]{:S(2)}) %copy-start) | copy-done | bytes 4735000
  44.3 3.8 %split_basis.2.refs_5_ = bf16[2,1088,2176]{2,1,0:T(8,128)(2,1)S(1)} custom-call(f32[544,2176]{1,0:T(8,128)S(1)} %bitcast.9, f32[544,2176]{1,0:T(8,128)} %bitcast.5.other), custom_call_target="tpu_custom_call" | custom-call | flops 1000 | bytes 1000 | tf_op jit(solution)/shard_map/split_basis/pallas_call | solution.py:72
  48.2 18.2 %collective-permute-done.4.refs_4_ = f32[64,2176]{1,0:T(8,128)S(1)} collective-permute-done((f32[64,2176]{1,0:T(8,128)S(1)}, f32[64,2176]{1,0:T(8,128)S(1)}, u32[]{:S(2)}, u32[]{:S(2)}) %collective-permute-start.4) | collective-permute-done | bytes 557088 | tf_op jit(solution)/shard_map/ppermute | solution.py:26
  66.4 2.1 %collective-permute-done.3.refs_3_ = f32[64,2176]{1,0:T(8,128)} collective-permute-done((f32[64,2176]{1,0:T(8,128)S(1)}, f32[64,2176]{1,0:T(8,128)}, u32[]{:S(2)}, u32[]{:S(2)}) %collective-permute-start.3) | collective-permute-done | bytes 557088 | tf_op jit(solution)/shard_map/ppermute | solution.py:26
  68.5 2.7 %collective-permute-start.10 = (f32[64,2176]{1,0:T(8,128)S(1)}, f32[64,2176]{1,0:T(8,128)}, u32[]{:S(2)}, u32[]{:S(2)}) collective-permute-start(f32[64,2176]{1,0:T(8,128)S(1)} %collective-permute-done.4.refs_4_), channel_id=1, source_target_pairs={{0,112},{16,0},{32,16},{48,32},{64,48},{80,64},{96,80},{112,96},{1... | collective-permute-start | bytes 1671176 | tf_op jit(solution)/shard_map/ppermute | solution.py:26
  71.1 8.1 %products.2 = f32[320,1088]{1,0:T(8,128)} custom-call(f32[64,2176]{1,0:T(8,128)S(1)} %constant_dynamic-update-slice_fusion.refs_0_, f32[64,2176]{1,0:T(8,128)S(1)} %collective-permute-done.1.refs_1_, f32[64,2176]{1,0:T(8,128)S(1)} %collective-permute-done.2.refs_2_, f32[64,2176]{1,0:T(8,128)} %collective-permute-done.3.refs_3_, ...), custom_call_target="tpu_custom_call" | custom-call | flops 1000 | bytes 1000 | tf_op jit(solution)/shard_map/products/pallas_call | solution.py:101
  79.2 6.7 %all-to-all-start.1 = ((f32[8,40,1088]{2,1,0:T(8,128)}), f32[8,40,1088]{2,1,0:T(8,128)S(1)}, u32[]{:S(2)}, u32[]{:S(2)}) async-start(f32[8,40,1088]{2,1,0:T(8,128)} %bitcast.7), calls=%async_computation.1 | async-start | bytes 2949120 | tf_op jit(solution)/shard_map/all_to_all | solution.py:34
  85.9 1.0 slice.8
  87.0 1.0 slice.9
  87.9 2.7 %collective-permute-start.12 = (f32[32,2176]{1,0:T(8,128)S(1)}, f32[32,2176]{1,0:T(8,128)S(1)}, u32[]{:S(2)}, u32[]{:S(2)}) collective-permute-start(f32[32,2176]{1,0:T(8,128)S(1)} %slice.9), channel_id=1, source_target_pairs={{0,112},{16,0},{32,16},{48,32},{64,48},{80,64},{96,80},{112,96},{1... | collective-permute-start | bytes 835592 | tf_op jit(solution)/shard_map/ppermute | solution.py:26
  91.1 2.3 %copy-done.1 = f32[2176,544]{0,1:T(8,128)S(1)} copy-done((f32[2176,544]{0,1:T(8,128)S(1)}, f32[2176,544]{0,1:T(8,128)}, u32[]{:S(2)}) %copy-start.1) | copy-done | bytes 4735000
  93.4 3.8 %split_basis.3.refs_4_ = bf16[2,1088,2176]{2,1,0:T(8,128)(2,1)S(1)} custom-call(f32[544,2176]{1,0:T(8,128)S(1)} %bitcast.10, f32[544,2176]{1,0:T(8,128)} %bitcast.5.other), custom_call_target="tpu_custom_call" | custom-call | flops 1000 | bytes 1000 | tf_op jit(solution)/shard_map/split_basis/pallas_call | solution.py:72
  97.3 6.1 %products.3 = f32[192,1088]{1,0:T(8,128)} custom-call(f32[64,2176]{1,0:T(8,128)} %collective-permute-done.9.refs_0_, f32[64,2176]{1,0:T(8,128)} %collective-permute-done.10.refs_1_, f32[32,2176]{1,0:T(8,128)S(1)} %collective-permute-done.11.refs_2_, f32[32,2176]{1,0:T(8,128)S(1)} %collective-permute-done.12.refs_3_, ...), custom_call_target="tpu_custom_call" | custom-call | flops 5000000000 | bytes 1000 | tf_op jit(solution)/shard_map/products/pallas_call | solution.py:101
  103.9 7.3 %all-to-all-start.2 = ((f32[8,24,1088]{2,1,0:T(8,128)}), f32[8,24,1088]{2,1,0:T(8,128)S(1)}, u32[]{:S(2)}, u32[]{:S(2)}) async-start(f32[8,24,1088]{2,1,0:T(8,128)} %bitcast.8), calls=%async_computation.2 | async-start | bytes 1769472 | tf_op jit(solution)/shard_map/all_to_all | solution.py:34
  111.2 1.5 collective-permute-start.13
  112.6 2.7 %collective-permute-done.14.refs_2_ = f32[64,640]{1,0:T(8,128)S(1)} collective-permute-done((f32[64,640]{1,0:T(8,128)S(1)}, f32[64,640]{1,0:T(8,128)S(1)}, u32[]{:S(2)}, u32[]{:S(2)}) %collective-permute-start.14) | collective-permute-done | bytes 163872 | tf_op jit(solution)/shard_map/ppermute | solution.py:26
  115.3 1.3 collective-permute-done.13.refs_1_
  116.6 4.8 %all-to-all-done.2.refs_1_ = f32[8,24,1088]{2,1,0:T(8,128)S(1)} async-done(((f32[8,24,1088]{2,1,0:T(8,128)}), f32[8,24,1088]{2,1,0:T(8,128)S(1)}, u32[]{:S(2)}, u32[]{:S(2)}) %all-to-all-start.2) | async-done | bytes 835616 | tf_op jit(solution)/shard_map/all_to_all | solution.py:34
  121.6 1.4 copy-done.2
  123.0 6.9 %all-to-all-start.3 = ((f32[8,64,1088]{2,1,0:T(8,128)}), f32[8,64,1088]{2,1,0:T(8,128)S(1)}, u32[]{:S(2)}, u32[]{:S(2)}) async-start(f32[8,64,1088]{2,1,0:T(8,128)} %copy-done.2), calls=%async_computation.3 | async-start | bytes 4718592 | tf_op jit(solution)/shard_map/all_to_all | solution.py:34
  130.3 2.7 %collective-permute-start.16 = (f32[64,640]{1,0:T(8,128)S(1)}, f32[64,640]{1,0:T(8,128)S(1)}, u32[]{:S(2)}, u32[]{:S(2)}) collective-permute-start(f32[64,640]{1,0:T(8,128)S(1)} %collective-permute-done.14.refs_2_), channel_id=1, source_target_pairs={{0,112},{16,0},{32,16},{48,32},{64,48},{80,64},{96,80},{112,96},{1... | collective-permute-start | bytes 491528 | tf_op jit(solution)/shard_map/ppermute | solution.py:26
  132.9 2.7 %collective-permute-done.15.refs_3_ = f32[64,640]{1,0:T(8,128)S(1)} collective-permute-done((f32[64,640]{1,0:T(8,128)S(1)}, f32[64,640]{1,0:T(8,128)S(1)}, u32[]{:S(2)}, u32[]{:S(2)}) %collective-permute-start.15) | collective-permute-done | bytes 163872 | tf_op jit(solution)/shard_map/ppermute | solution.py:26
  135.7 3.0 %collective-permute-start.18 = (f32[64,640]{1,0:T(8,128)S(1)}, f32[64,640]{1,0:T(8,128)S(1)}, u32[]{:S(2)}, u32[]{:S(2)}) collective-permute-start(f32[64,640]{1,0:T(8,128)S(1)} %collective-permute-done.16.refs_4_), channel_id=1, source_target_pairs={{0,112},{16,0},{32,16},{48,32},{64,48},{80,64},{96,80},{112,96},{1... | collective-permute-start | bytes 491528 | tf_op jit(solution)/shard_map/ppermute | solution.py:26
  138.6 2.7 %collective-permute-done.17.refs_5_ = f32[64,640]{1,0:T(8,128)S(1)} collective-permute-done((f32[64,640]{1,0:T(8,128)S(1)}, f32[64,640]{1,0:T(8,128)S(1)}, u32[]{:S(2)}, u32[]{:S(2)}) %collective-permute-start.17) | collective-permute-done | bytes 163872 | tf_op jit(solution)/shard_map/ppermute | solution.py:26
  141.3 5.7 %collective-permute-done.19.refs_7_ = f32[64,640]{1,0:T(8,128)S(1)} collective-permute-done((f32[64,640]{1,0:T(8,128)S(1)}, f32[64,640]{1,0:T(8,128)S(1)}, u32[]{:S(2)}, u32[]{:S(2)}) %collective-permute-start.19) | collective-permute-done | bytes 163872 | tf_op jit(solution)/shard_map/ppermute | solution.py:26
  147.6 4.9 %collective-permute-start.20 = (f32[512,640]{1,0:T(8,128)S(1)}, f32[512,640]{1,0:T(8,128)S(1)}, u32[]{:S(2)}, u32[]{:S(2)}) collective-permute-start(f32[512,640]{1,0:T(8,128)S(1)} %place.1.refs_2_), channel_id=1, source_target_pairs={{0,8},{8,0},{1,9},{9,1},{2,10},{10,2},{3,11},{11,3},{4,12},{12,4},... | collective-permute-start | bytes 3932168 | tf_op jit(solution)/shard_map/ppermute | solution.py:26
  152.6 1.1 copy-done.3
  153.6 1.6 collective-permute-done.20.refs_3_
  155.2 1.1 copy-done.5
  156.3 2.6 %all-to-all-done.3.refs_0_ = f32[8,64,1088]{2,1,0:T(8,128)S(1)} async-done(((f32[8,64,1088]{2,1,0:T(8,128)}), f32[8,64,1088]{2,1,0:T(8,128)S(1)}, u32[]{:S(2)}, u32[]{:S(2)}) %all-to-all-start.3) | async-done | bytes 2228256 | tf_op jit(solution)/shard_map/all_to_all | solution.py:34
  158.9 1.2 collective-permute-start.21
  160.3 4.0 %collective-permute-done.21.refs_1_ = f32[8,64,1088]{2,1,0:T(8,128)S(1)} collective-permute-done((f32[8,64,1088]{2,1,0:T(8,128)S(1)}, f32[8,64,1088]{2,1,0:T(8,128)S(1)}, u32[]{:S(2)}, u32[]{:S(2)}) %collective-permute-start.21) | collective-permute-done | bytes 2228256 | tf_op jit(solution)/shard_map/ppermute | solution.py:26
  164.3 1.3 copy-done.4
  165.6 1.3 copy-done.6
  166.9 8.8 %moments.1 = f32[544,640]{1,0:T(8,128)} custom-call(s32[3]{0:T(128)S(1)} %pad_add_fusion.place, s32[5]{0:T(128)S(1)} %convert_reduce_fusion.bounds, f32[8,64,1088]{2,1,0:T(8,128)S(1)} %all-to-all-done.3.refs_0_, f32[8,64,1088]{2,1,0:T(8,128)S(1)} %collective-permute-done.21.refs_1_, f32[512,640]{1,0:T(8,128)S(1)} %copy-done.4, f32[512,640]{1,0:T(8,128)S(1)} %copy-done.6), custom_call_target="tpu_custom_call" | custom-call | flops 1000 | bytes 1000 | tf_op jit(solution)/shard_map/moments/pallas_call | solution.py:250
  (44 shorter events, 2.6 us)
Async XLA Ops:
  0.0 42.0 %collective-permute-start.5 = (f32[2176,544]{0,1:T(8,128)}, f32[2176,544]{0,1:T(8,128)}, u32[]{:S(2)}, u32[]{:S(2)}) collective-permute-start(f32[2176,544]{0,1:T(8,128)} %param.6), channel_id=1, source_target_pairs={{0,8},{8,0},{1,9},{9,1},{2,10},{10,2},{3,11},{11,3},{4,12},{12,4},... | collective-permute-start | bytes 14204936 | tf_op jit(solution)/shard_map/ppermute | solution.py:26
  3.2 8.5 %collective-permute-start = (f32[32,2176]{1,0:T(8,128)}, f32[32,2176]{1,0:T(8,128)S(1)}, u32[]{:S(2)}, u32[]{:S(2)}) collective-permute-start(f32[32,2176]{1,0:T(8,128)} %param.5), channel_id=1, source_target_pairs={{0,128},{128,0},{1,129},{129,1},{2,130},{130,2},{3,131},{131,3},{4... | collective-permute-start | bytes 835592 | tf_op jit(solution)/shard_map/ppermute | solution.py:26
  3.3 1.1 copy-start.7
  4.4 1.0 copy-start.8
  7.4 8.6 %copy-start.9 = (f32[32,2176]{1,0:T(8,128)S(1)}, f32[32,2176]{1,0:T(8,128)}, u32[]{:S(2)}) copy-start(f32[32,2176]{1,0:T(8,128)} %param.5) | copy-start | bytes 835588
  11.7 3.4 %collective-permute-start.6 = (f32[512,640]{1,0:T(8,128)S(1)}, f32[512,640]{1,0:T(8,128)S(1)}, u32[]{:S(2)}, u32[]{:S(2)}) collective-permute-start(f32[512,640]{1,0:T(8,128)S(1)} %get-tuple-element.44), channel_id=1, source_target_pairs={{0,8},{8,0},{1,9},{9,1},{2,10},{10,2},{3,11},{11,3},{4,12},{12,4},... | collective-permute-start | bytes 3932168 | tf_op jit(solution)/shard_map/ppermute | solution.py:26
  15.9 16.0 %collective-permute-start.7 = (f32[256,640]{1,0:T(8,128)S(1)}, f32[256,640]{1,0:T(8,128)S(1)}, u32[]{:S(2)}, u32[]{:S(2)}) collective-permute-start(f32[256,640]{1,0:T(8,128)S(1)} %get-tuple-element.46), channel_id=1, source_target_pairs={{0,128},{128,0},{1,129},{129,1},{2,130},{130,2},{3,131},{131,3},{4... | collective-permute-start | bytes 1966088 | tf_op jit(solution)/shard_map/ppermute | solution.py:26
  16.1 23.2 %collective-permute-start.2 = (f32[64,2176]{1,0:T(8,128)S(1)}, f32[64,2176]{1,0:T(8,128)S(1)}, u32[]{:S(2)}, u32[]{:S(2)}) collective-permute-start(f32[64,2176]{1,0:T(8,128)S(1)} %constant_dynamic-update-slice_fusion.refs_0_), channel_id=1, source_target_pairs={{0,112},{16,0},{32,16},{48,32},{64,48},{80,64},{96,80},{112,96},{1... | collective-permute-start | bytes 1671176 | tf_op jit(solution)/shard_map/ppermute | solution.py:26
  21.2 20.8 %collective-permute-start.1 = (f32[64,2176]{1,0:T(8,128)S(1)}, f32[64,2176]{1,0:T(8,128)S(1)}, u32[]{:S(2)}, u32[]{:S(2)}) collective-permute-start(f32[64,2176]{1,0:T(8,128)S(1)} %constant_dynamic-update-slice_fusion.refs_0_), channel_id=1, source_target_pairs={{0,16},{16,32},{32,48},{48,64},{64,80},{80,96},{96,112},{112,0},{1... | collective-permute-start | bytes 1671176 | tf_op jit(solution)/shard_map/ppermute | solution.py:26
  32.9 46.4 %all-to-all-start = ((f32[8,32,640]{2,1,0:T(8,128)}), f32[8,32,640]{2,1,0:T(8,128)S(1)}, u32[]{:S(2)}, u32[]{:S(2)}) async-start(f32[8,32,640]{2,1,0:T(8,128)} %bitcast.6), calls=%async_computation | async-start | bytes 1310720 | tf_op jit(solution)/shard_map/all_to_all | solution.py:34
  39.3 27.1 %collective-permute-start.4 = (f32[64,2176]{1,0:T(8,128)S(1)}, f32[64,2176]{1,0:T(8,128)S(1)}, u32[]{:S(2)}, u32[]{:S(2)}) collective-permute-start(f32[64,2176]{1,0:T(8,128)S(1)} %collective-permute-done.2.refs_2_), channel_id=1, source_target_pairs={{0,112},{16,0},{32,16},{48,32},{64,48},{80,64},{96,80},{112,96},{1... | collective-permute-start | bytes 1671176 | tf_op jit(solution)/shard_map/ppermute | solution.py:26
  42.0 26.5 %collective-permute-start.3 = (f32[64,2176]{1,0:T(8,128)S(1)}, f32[64,2176]{1,0:T(8,128)}, u32[]{:S(2)}, u32[]{:S(2)}) collective-permute-start(f32[64,2176]{1,0:T(8,128)S(1)} %collective-permute-done.1.refs_1_), channel_id=1, source_target_pairs={{0,16},{16,32},{32,48},{48,64},{64,80},{80,96},{96,112},{112,0},{1... | collective-permute-start | bytes 1671176 | tf_op jit(solution)/shard_map/ppermute | solution.py:26
  42.0 2.3 %copy-start = (f32[2176,544]{0,1:T(8,128)S(1)}, f32[2176,544]{0,1:T(8,128)}, u32[]{:S(2)}) copy-start(f32[2176,544]{0,1:T(8,128)} %param.6) | copy-start | bytes 14204932
  68.5 17.4 %collective-permute-start.9 = (f32[64,2176]{1,0:T(8,128)}, f32[64,2176]{1,0:T(8,128)}, u32[]{:S(2)}, u32[]{:S(2)}) collective-permute-start(f32[64,2176]{1,0:T(8,128)} %collective-permute-done.3.refs_3_), channel_id=1, source_target_pairs={{0,16},{16,32},{32,48},{48,64},{64,80},{80,96},{96,112},{112,0},{1... | collective-permute-start | bytes 1671176 | tf_op jit(solution)/shard_map/ppermute | solution.py:26
  68.5 18.5 %collective-permute-start.10 = (f32[64,2176]{1,0:T(8,128)S(1)}, f32[64,2176]{1,0:T(8,128)}, u32[]{:S(2)}, u32[]{:S(2)}) collective-permute-start(f32[64,2176]{1,0:T(8,128)S(1)} %collective-permute-done.4.refs_4_), channel_id=1, source_target_pairs={{0,112},{16,0},{32,16},{48,32},{64,48},{80,64},{96,80},{112,96},{1... | collective-permute-start | bytes 1671176 | tf_op jit(solution)/shard_map/ppermute | solution.py:26
  79.2 24.7 %all-to-all-start.1 = ((f32[8,40,1088]{2,1,0:T(8,128)}), f32[8,40,1088]{2,1,0:T(8,128)S(1)}, u32[]{:S(2)}, u32[]{:S(2)}) async-start(f32[8,40,1088]{2,1,0:T(8,128)} %bitcast.7), calls=%async_computation.1 | async-start | bytes 2949120 | tf_op jit(solution)/shard_map/all_to_all | solution.py:34
  86.9 10.4 %collective-permute-start.11 = (f32[32,2176]{1,0:T(8,128)S(1)}, f32[32,2176]{1,0:T(8,128)S(1)}, u32[]{:S(2)}, u32[]{:S(2)}) collective-permute-start(f32[32,2176]{1,0:T(8,128)S(1)} %slice.8), channel_id=1, source_target_pairs={{0,16},{16,32},{32,48},{48,64},{64,80},{80,96},{96,112},{112,0},{1... | collective-permute-start | bytes 835592 | tf_op jit(solution)/shard_map/ppermute | solution.py:26
  87.9 9.3 %collective-permute-start.12 = (f32[32,2176]{1,0:T(8,128)S(1)}, f32[32,2176]{1,0:T(8,128)S(1)}, u32[]{:S(2)}, u32[]{:S(2)}) collective-permute-start(f32[32,2176]{1,0:T(8,128)S(1)} %slice.9), channel_id=1, source_target_pairs={{0,112},{16,0},{32,16},{48,32},{64,48},{80,64},{96,80},{112,96},{1... | collective-permute-start | bytes 835592 | tf_op jit(solution)/shard_map/ppermute | solution.py:26
  90.7 12.6 %collective-permute-start.8 = (f32[1,32,640]{2,1,0:T(8,128)S(1)}, f32[1,32,640]{2,1,0:T(8,128)S(1)}, u32[]{:S(2)}, u32[]{:S(2)}) collective-permute-start(f32[1,32,640]{2,1,0:T(8,128)S(1)} %sum_copies.2.own), channel_id=1, source_target_pairs={{0,128},{128,0},{1,129},{129,1},{2,130},{130,2},{3,131},{131,3},{4... | collective-permute-start | bytes 245768 | tf_op jit(solution)/shard_map/ppermute | solution.py:26
  91.1 2.3 %copy-start.1 = (f32[2176,544]{0,1:T(8,128)S(1)}, f32[2176,544]{0,1:T(8,128)}, u32[]{:S(2)}) copy-start(f32[2176,544]{0,1:T(8,128)} %param.6) | copy-start | bytes 14204932
  103.9 17.5 %all-to-all-start.2 = ((f32[8,24,1088]{2,1,0:T(8,128)}), f32[8,24,1088]{2,1,0:T(8,128)S(1)}, u32[]{:S(2)}, u32[]{:S(2)}) async-start(f32[8,24,1088]{2,1,0:T(8,128)} %bitcast.8), calls=%async_computation.2 | async-start | bytes 1769472 | tf_op jit(solution)/shard_map/all_to_all | solution.py:34
  111.2 4.2 %collective-permute-start.14 = (f32[64,640]{1,0:T(8,128)S(1)}, f32[64,640]{1,0:T(8,128)S(1)}, u32[]{:S(2)}, u32[]{:S(2)}) collective-permute-start(f32[64,640]{1,0:T(8,128)S(1)} %pair.1.refs_0_), channel_id=1, source_target_pairs={{0,112},{16,0},{32,16},{48,32},{64,48},{80,64},{96,80},{112,96},{1... | collective-permute-start | bytes 491528 | tf_op jit(solution)/shard_map/ppermute | solution.py:26
  111.2 5.5 %collective-permute-start.13 = (f32[64,640]{1,0:T(8,128)S(1)}, f32[64,640]{1,0:T(8,128)S(1)}, u32[]{:S(2)}, u32[]{:S(2)}) collective-permute-start(f32[64,640]{1,0:T(8,128)S(1)} %pair.1.refs_0_), channel_id=1, source_target_pairs={{0,16},{16,32},{32,48},{48,64},{64,80},{80,96},{96,112},{112,0},{1... | collective-permute-start | bytes 491528 | tf_op jit(solution)/shard_map/ppermute | solution.py:26
  121.6 1.4 copy-start.2
  123.0 35.9 %all-to-all-start.3 = ((f32[8,64,1088]{2,1,0:T(8,128)}), f32[8,64,1088]{2,1,0:T(8,128)S(1)}, u32[]{:S(2)}, u32[]{:S(2)}) async-start(f32[8,64,1088]{2,1,0:T(8,128)} %copy-done.2), calls=%async_computation.3 | async-start | bytes 4718592 | tf_op jit(solution)/shard_map/all_to_all | solution.py:34
  130.0 30.2 %copy-start.10 = (s32[1024]{0:T(1024)S(1)}, s32[1024]{0:T(1024)}, u32[]{:S(2)}) copy-start(s32[1024]{0:T(1024)} %param.9) | copy-start | bytes 12292
  130.0 5.7 %collective-permute-start.15 = (f32[64,640]{1,0:T(8,128)S(1)}, f32[64,640]{1,0:T(8,128)S(1)}, u32[]{:S(2)}, u32[]{:S(2)}) collective-permute-start(f32[64,640]{1,0:T(8,128)S(1)} %collective-permute-done.13.refs_1_), channel_id=1, source_target_pairs={{0,16},{16,32},{32,48},{48,64},{64,80},{80,96},{96,112},{112,0},{1... | collective-permute-start | bytes 491528 | tf_op jit(solution)/shard_map/ppermute | solution.py:26
  130.3 5.4 %collective-permute-start.16 = (f32[64,640]{1,0:T(8,128)S(1)}, f32[64,640]{1,0:T(8,128)S(1)}, u32[]{:S(2)}, u32[]{:S(2)}) collective-permute-start(f32[64,640]{1,0:T(8,128)S(1)} %collective-permute-done.14.refs_2_), channel_id=1, source_target_pairs={{0,112},{16,0},{32,16},{48,32},{64,48},{80,64},{96,80},{112,96},{1... | collective-permute-start | bytes 491528 | tf_op jit(solution)/shard_map/ppermute | solution.py:26
  135.6 5.7 %collective-permute-start.17 = (f32[64,640]{1,0:T(8,128)S(1)}, f32[64,640]{1,0:T(8,128)S(1)}, u32[]{:S(2)}, u32[]{:S(2)}) collective-permute-start(f32[64,640]{1,0:T(8,128)S(1)} %collective-permute-done.15.refs_3_), channel_id=1, source_target_pairs={{0,16},{16,32},{32,48},{48,64},{64,80},{80,96},{96,112},{112,0},{1... | collective-permute-start | bytes 491528 | tf_op jit(solution)/shard_map/ppermute | solution.py:26
  135.7 5.7 %collective-permute-start.18 = (f32[64,640]{1,0:T(8,128)S(1)}, f32[64,640]{1,0:T(8,128)S(1)}, u32[]{:S(2)}, u32[]{:S(2)}) collective-permute-start(f32[64,640]{1,0:T(8,128)S(1)} %collective-permute-done.16.refs_4_), channel_id=1, source_target_pairs={{0,112},{16,0},{32,16},{48,32},{64,48},{80,64},{96,80},{112,96},{1... | collective-permute-start | bytes 491528 | tf_op jit(solution)/shard_map/ppermute | solution.py:26
  141.3 5.7 %collective-permute-start.19 = (f32[64,640]{1,0:T(8,128)S(1)}, f32[64,640]{1,0:T(8,128)S(1)}, u32[]{:S(2)}, u32[]{:S(2)}) collective-permute-start(f32[64,640]{1,0:T(8,128)S(1)} %collective-permute-done.17.refs_5_), channel_id=1, source_target_pairs={{0,16},{16,32},{32,48},{48,64},{64,80},{80,96},{96,112},{112,0},{1... | collective-permute-start | bytes 491528 | tf_op jit(solution)/shard_map/ppermute | solution.py:26
  147.6 7.6 %collective-permute-start.20 = (f32[512,640]{1,0:T(8,128)S(1)}, f32[512,640]{1,0:T(8,128)S(1)}, u32[]{:S(2)}, u32[]{:S(2)}) collective-permute-start(f32[512,640]{1,0:T(8,128)S(1)} %place.1.refs_2_), channel_id=1, source_target_pairs={{0,8},{8,0},{1,9},{9,1},{2,10},{10,2},{3,11},{11,3},{4,12},{12,4},... | collective-permute-start | bytes 3932168 | tf_op jit(solution)/shard_map/ppermute | solution.py:26
  152.6 1.1 copy-start.3
  155.2 1.1 copy-start.5
  158.9 5.4 %collective-permute-start.21 = (f32[8,64,1088]{2,1,0:T(8,128)S(1)}, f32[8,64,1088]{2,1,0:T(8,128)S(1)}, u32[]{:S(2)}, u32[]{:S(2)}) collective-permute-start(f32[8,64,1088]{2,1,0:T(8,128)S(1)} %all-to-all-done.3.refs_0_), channel_id=1, source_target_pairs={{0,8},{8,0},{1,9},{9,1},{2,10},{10,2},{3,11},{11,3},{4,12},{12,4},... | collective-permute-start | bytes 6684680 | tf_op jit(solution)/shard_map/ppermute | solution.py:26
  164.3 1.3 copy-start.4
  165.6 1.3 copy-start.6

commit v5 on v4

--- a/solution.py
+++ b/solution.py
@@ -183,9 +183,16 @@
     low_ref[rows, :] = (value - high.astype(jnp.float32)).astype(jnp.bfloat16)
 
 
+def split_grads_kernel(place, own, other, high, low):
+    rows = own.shape[0]
+    for ref, core in ((own, place[1]), (other, 1 - place[1])):
+        into = pl.ds(pl.multiple_of(core * rows, rows), rows)
+        high[into, :], low[into, :] = halved(ref[...])
+
+
 def moments_kernel(place, bounds, *refs):
-    acts_refs, grads_refs, out = refs[:2], refs[2:-6], refs[-6]
-    acts_high, acts_low, grads_high, grads_low, moment = refs[-5:]
+    acts_refs, (grads_high, grads_low, out) = refs[:2], refs[2:5]
+    acts_high, acts_low, turned_high, turned_low, moment = refs[5:]
     z, core, lo = place[0], place[1], place[2]
     cols = out.shape[0]
     first_rows = 2 * len(FIRST) * BLOCK // 8
@@ -208,13 +215,14 @@
                 xl = 1 - lo if far else lo
                 row = ((xl * 8 + lax.rem(z + distance + 8, 8)) * 2 + of_core) * BLOCK
                 split_store(value, acts_high, acts_low, row)
-        ref = grads_refs[from_other]
-        rows = pl.ds(pl.multiple_of(of_core * ref.shape[0], ref.shape[0]), ref.shape[0])
-        grads_high[rows, :], grads_low[rows, :] = halved(ref[...])
+    for start in range(0, TOKENS, DEPTH):
+        rows = slice(start, start + DEPTH)
+        for ref, turned in ((acts_high, turned_high), (acts_low, turned_low)):
+            turned[:, rows] = ref[rows, :].T
 
     def product(a, b):
         return lax.dot_general(
-            a, b, (((0,), (0,)), ((), ())), preferred_element_type=jnp.float32
+            a, b, (((1,), (0,)), ((), ())), preferred_element_type=jnp.float32
         )
 
     for seq in range(SEQS):
@@ -227,7 +235,7 @@
             mine = (number >= first) & (number < end)
             grads_h = jnp.where(mine, grads_high[rows, :].astype(jnp.float32), 0.0).astype(jnp.bfloat16)
             grads_l = jnp.where(mine, grads_low[rows, :].astype(jnp.float32), 0.0).astype(jnp.bfloat16)
-            acts_h, acts_l = acts_high[rows, :], acts_low[rows, :]
+            acts_h, acts_l = turned_high[:, rows], turned_low[:, rows]
             moment[...] += product(acts_h, grads_h) + (
                 product(acts_l, grads_h) + product(acts_h, grads_l)
             )
@@ -247,6 +255,12 @@
     labels = jnp.arange(SEQS + 1, dtype=jnp.int32)
     bounds = jnp.sum((seq_ids[None, :] < labels[:, None]).astype(jnp.int32), axis=1)
     cols, out_cols = acts[0].shape[2] // 2, grads[0].shape[1]
+    grads = call(
+        split_grads_kernel,
+        [bf16(TOKENS, out_cols)] * 2,
+        [SMEM, VMEM, VMEM],
+        name="split_grads",
+    )(place, *grads)
     return call(
         moments_kernel,
         f32(cols, out_cols),
@@ -254,8 +268,8 @@
         [
             pltpu.VMEM((TOKENS, cols), jnp.bfloat16),
             pltpu.VMEM((TOKENS, cols), jnp.bfloat16),
-            pltpu.VMEM((TOKENS, out_cols), jnp.bfloat16),
-            pltpu.VMEM((TOKENS, out_cols), jnp.bfloat16),
+            pltpu.VMEM((cols, TOKENS), jnp.bfloat16),
+            pltpu.VMEM((cols, TOKENS), jnp.bfloat16),
             pltpu.VMEM((cols, out_cols), jnp.float32),
         ],
         name="moments",

time: 177 us -> 174 us (0.983)
  waiting for transfers between devices: 66.2 us -> 62.6 us
    ppermute x22, waiting for transfers between devices: 58.8 us -> 55.2 us  [shifted(): return lax.ppermute(value, axis, [(i, (i + by) % n) for i in range(n)])]
  transfers between devices with their start and end apart: 26 -> 26, of which waited for: 14 -> 14; matrix products, arithmetic and copies ran while one was open for 1% -> 1% of each run, Pallas kernels for 15% -> 16%
where the time goes in v5:
time: 174 us; the launch traced here: 173 us
  waiting for transfers between devices  62.6 us (36%)
  starting transfers between devices  58.6 us (34%)
  Pallas kernels  36.4 us (21%)
  local copies, waits for them, and re-layouts  14.9 us (9%)
    ppermute x22, waiting for transfers between devices, shifted(): return lax.ppermute(value, axis, [(i, (i + by) % n) for i in range(n)])  55.2 us
    ppermute x22, starting transfers between devices, shifted(): return lax.ppermute(value, axis, [(i, (i + by) % n) for i in range(n)])  31.4 us
    all_to_all x4, starting transfers between devices, swapped(): return lax.all_to_all(value, axes, 0, 0)  27.3 us
    pallas_call x2, Pallas kernels, products(): call(products_kernel, f32(rows, cols), [VMEM] * (1 + len(blocks)), [pltpu...  14.1 us
    unnamed x23, local copies, waits for them, and re-layouts  13 us
    pallas_call x1, Pallas kernels, eigenvalues(): call(moments_kernel, f32(cols, out_cols), [SMEM, SMEM] + [VMEM] * (len(ac...  8.74 us
    pallas_call x2, Pallas kernels, split_basis(): call(basis_kernel, pltpu.VMEM((2, 2 * rows, depth), jnp.bfloat16), [VMEM,...  7.61 us
    all_to_all x4, waiting for transfers between devices, swapped(): return lax.all_to_all(value, axes, 0, 0)  7.39 us
  transfers between devices with their start and end apart: 26, of which 14 were waited for; matrix products, arithmetic and copies ran while one was open for 1% of the time, Pallas kernels for 16%

profile of v5, /device:TPU:1, one launch (start us, length us, event | category | flops | bytes accessed | tf_op | source)
XLA Modules:
  0.0 173.0 jit_solution(2940150046560445592)
XLA Ops:
  0.0 3.2 %collective-permute-start.5 = (f32[2176,544]{0,1:T(8,128)}, f32[2176,544]{0,1:T(8,128)}, u32[]{:S(2)}, u32[]{:S(2)}) collective-permute-start(f32[2176,544]{0,1:T(8,128)} %param.6), channel_id=1, source_target_pairs={{0,8},{8,0},{1,9},{9,1},{2,10},{10,2},{3,11},{11,3},{4,12},{12,4},... | collective-permute-start | bytes 14204936 | tf_op jit(solution)/shard_map/ppermute | solution.py:26
  3.3 1.1 copy-done.7
  4.4 1.0 copy-done.8
  5.4 2.0 %rotate_grads.1 = (f32[512,640]{1,0:T(8,128)S(1)}, f32[512,640]{1,0:T(8,128)S(1)}) custom-call(s32[3]{0:T(128)S(1)} %pad_add_fusion.place, f32[160,1024]{1,0:T(8,128)S(1)} %bitcast.11, f32[160,640]{1,0:T(8,128)S(1)} %copy-done.8), custom_call_target="tpu_custom_call" | custom-call | flops 1000 | bytes 1000 | tf_op jit(solution)/shard_map/rotate_grads/pallas_call | solution.py:292
  7.4 4.3 %collective-permute-done = f32[32,2176]{1,0:T(8,128)S(1)} collective-permute-done((f32[32,2176]{1,0:T(8,128)}, f32[32,2176]{1,0:T(8,128)S(1)}, u32[]{:S(2)}, u32[]{:S(2)}) %collective-permute-start) | collective-permute-done | bytes 278560 | tf_op jit(solution)/shard_map/ppermute | solution.py:26
  11.7 0.8 collective-permute-start.6
  12.5 2.7 %collective-permute-done.6.arrived = f32[512,640]{1,0:T(8,128)S(1)} collective-permute-done((f32[512,640]{1,0:T(8,128)S(1)}, f32[512,640]{1,0:T(8,128)S(1)}, u32[]{:S(2)}, u32[]{:S(2)}) %collective-permute-start.6) | collective-permute-done | bytes 1310752 | tf_op jit(solution)/shard_map/ppermute | solution.py:26
  15.2 0.7 add_halves.1
  16.1 5.1 %collective-permute-start.2 = (f32[64,2176]{1,0:T(8,128)S(1)}, f32[64,2176]{1,0:T(8,128)S(1)}, u32[]{:S(2)}, u32[]{:S(2)}) collective-permute-start(f32[64,2176]{1,0:T(8,128)S(1)} %constant_dynamic-update-slice_fusion.refs_0_), channel_id=1, source_target_pairs={{0,112},{16,0},{32,16},{48,32},{64,48},{80,64},{96,80},{112,96},{1... | collective-permute-start | bytes 1671176 | tf_op jit(solution)/shard_map/ppermute | solution.py:26
  21.2 10.8 %collective-permute-done.7.b = f32[256,640]{1,0:T(8,128)S(1)} collective-permute-done((f32[256,640]{1,0:T(8,128)S(1)}, f32[256,640]{1,0:T(8,128)S(1)}, u32[]{:S(2)}, u32[]{:S(2)}) %collective-permute-start.7) | collective-permute-done | bytes 655392 | tf_op jit(solution)/shard_map/ppermute | solution.py:26
  32.0 0.9 add.5
  32.9 6.5 %all-to-all-start = ((f32[8,32,640]{2,1,0:T(8,128)}), f32[8,32,640]{2,1,0:T(8,128)S(1)}, u32[]{:S(2)}, u32[]{:S(2)}) async-start(f32[8,32,640]{2,1,0:T(8,128)} %bitcast.6), calls=%async_computation | async-start | bytes 1310720 | tf_op jit(solution)/shard_map/all_to_all | solution.py:34
  39.3 2.7 %collective-permute-start.4 = (f32[64,2176]{1,0:T(8,128)S(1)}, f32[64,2176]{1,0:T(8,128)S(1)}, u32[]{:S(2)}, u32[]{:S(2)}) collective-permute-start(f32[64,2176]{1,0:T(8,128)S(1)} %collective-permute-done.2.refs_2_), channel_id=1, source_target_pairs={{0,112},{16,0},{32,16},{48,32},{64,48},{80,64},{96,80},{112,96},{1... | collective-permute-start | bytes 1671176 | tf_op jit(solution)/shard_map/ppermute | solution.py:26
  42.0 2.3 %copy-done = f32[2176,544]{0,1:T(8,128)S(1)} copy-done((f32[2176,544]{0,1:T(8,128)S(1)}, f32[2176,544]{0,1:T(8,128)}, u32[]{:S(2)}) %copy-start) | copy-done | bytes 4735000
  44.3 3.8 %split_basis.2.refs_5_ = bf16[2,1088,2176]{2,1,0:T(8,128)(2,1)S(1)} custom-call(f32[544,2176]{1,0:T(8,128)S(1)} %bitcast.9, f32[544,2176]{1,0:T(8,128)} %bitcast.5.other), custom_call_target="tpu_custom_call" | custom-call | flops 1000 | bytes 1000 | tf_op jit(solution)/shard_map/split_basis/pallas_call | solution.py:72
  48.2 18.2 %collective-permute-done.4.refs_4_ = f32[64,2176]{1,0:T(8,128)S(1)} collective-permute-done((f32[64,2176]{1,0:T(8,128)S(1)}, f32[64,2176]{1,0:T(8,128)S(1)}, u32[]{:S(2)}, u32[]{:S(2)}) %collective-permute-start.4) | collective-permute-done | bytes 557088 | tf_op jit(solution)/shard_map/ppermute | solution.py:26
  66.4 2.1 %collective-permute-done.3.refs_3_ = f32[64,2176]{1,0:T(8,128)} collective-permute-done((f32[64,2176]{1,0:T(8,128)S(1)}, f32[64,2176]{1,0:T(8,128)}, u32[]{:S(2)}, u32[]{:S(2)}) %collective-permute-start.3) | collective-permute-done | bytes 557088 | tf_op jit(solution)/shard_map/ppermute | solution.py:26
  68.5 2.7 %collective-permute-start.10 = (f32[64,2176]{1,0:T(8,128)S(1)}, f32[64,2176]{1,0:T(8,128)}, u32[]{:S(2)}, u32[]{:S(2)}) collective-permute-start(f32[64,2176]{1,0:T(8,128)S(1)} %collective-permute-done.4.refs_4_), channel_id=1, source_target_pairs={{0,112},{16,0},{32,16},{48,32},{64,48},{80,64},{96,80},{112,96},{1... | collective-permute-start | bytes 1671176 | tf_op jit(solution)/shard_map/ppermute | solution.py:26
  71.1 8.1 %products.2 = f32[320,1088]{1,0:T(8,128)} custom-call(f32[64,2176]{1,0:T(8,128)S(1)} %constant_dynamic-update-slice_fusion.refs_0_, f32[64,2176]{1,0:T(8,128)S(1)} %collective-permute-done.1.refs_1_, f32[64,2176]{1,0:T(8,128)S(1)} %collective-permute-done.2.refs_2_, f32[64,2176]{1,0:T(8,128)} %collective-permute-done.3.refs_3_, ...), custom_call_target="tpu_custom_call" | custom-call | flops 1000 | bytes 1000 | tf_op jit(solution)/shard_map/products/pallas_call | solution.py:101
  79.2 6.7 %all-to-all-start.1 = ((f32[8,40,1088]{2,1,0:T(8,128)}), f32[8,40,1088]{2,1,0:T(8,128)S(1)}, u32[]{:S(2)}, u32[]{:S(2)}) async-start(f32[8,40,1088]{2,1,0:T(8,128)} %bitcast.7), calls=%async_computation.1 | async-start | bytes 2949120 | tf_op jit(solution)/shard_map/all_to_all | solution.py:34
  85.9 1.0 slice.8
  87.0 1.0 slice.9
  87.9 2.7 %collective-permute-start.12 = (f32[32,2176]{1,0:T(8,128)S(1)}, f32[32,2176]{1,0:T(8,128)S(1)}, u32[]{:S(2)}, u32[]{:S(2)}) collective-permute-start(f32[32,2176]{1,0:T(8,128)S(1)} %slice.9), channel_id=1, source_target_pairs={{0,112},{16,0},{32,16},{48,32},{64,48},{80,64},{96,80},{112,96},{1... | collective-permute-start | bytes 835592 | tf_op jit(solution)/shard_map/ppermute | solution.py:26
  91.1 2.3 %copy-done.1 = f32[2176,544]{0,1:T(8,128)S(1)} copy-done((f32[2176,544]{0,1:T(8,128)S(1)}, f32[2176,544]{0,1:T(8,128)}, u32[]{:S(2)}) %copy-start.1) | copy-done | bytes 4735000
  93.4 3.8 %split_basis.3.refs_4_ = bf16[2,1088,2176]{2,1,0:T(8,128)(2,1)S(1)} custom-call(f32[544,2176]{1,0:T(8,128)S(1)} %bitcast.10, f32[544,2176]{1,0:T(8,128)} %bitcast.5.other), custom_call_target="tpu_custom_call" | custom-call | flops 1000 | bytes 1000 | tf_op jit(solution)/shard_map/split_basis/pallas_call | solution.py:72
  97.3 6.1 %products.3 = f32[192,1088]{1,0:T(8,128)} custom-call(f32[64,2176]{1,0:T(8,128)} %collective-permute-done.9.refs_0_, f32[64,2176]{1,0:T(8,128)} %collective-permute-done.10.refs_1_, f32[32,2176]{1,0:T(8,128)S(1)} %collective-permute-done.11.refs_2_, f32[32,2176]{1,0:T(8,128)S(1)} %collective-permute-done.12.refs_3_, ...), custom_call_target="tpu_custom_call" | custom-call | flops 5000000000 | bytes 1000 | tf_op jit(solution)/shard_map/products/pallas_call | solution.py:101
  103.9 7.3 %all-to-all-start.2 = ((f32[8,24,1088]{2,1,0:T(8,128)}), f32[8,24,1088]{2,1,0:T(8,128)S(1)}, u32[]{:S(2)}, u32[]{:S(2)}) async-start(f32[8,24,1088]{2,1,0:T(8,128)} %bitcast.8), calls=%async_computation.2 | async-start | bytes 1769472 | tf_op jit(solution)/shard_map/all_to_all | solution.py:34
  111.2 1.4 collective-permute-start.13
  112.6 2.7 %collective-permute-done.14.refs_2_ = f32[64,640]{1,0:T(8,128)S(1)} collective-permute-done((f32[64,640]{1,0:T(8,128)S(1)}, f32[64,640]{1,0:T(8,128)S(1)}, u32[]{:S(2)}, u32[]{:S(2)}) %collective-permute-start.14) | collective-permute-done | bytes 163872 | tf_op jit(solution)/shard_map/ppermute | solution.py:26
  115.3 1.3 collective-permute-done.13.refs_1_
  116.6 4.8 %all-to-all-done.2.refs_1_ = f32[8,24,1088]{2,1,0:T(8,128)S(1)} async-done(((f32[8,24,1088]{2,1,0:T(8,128)}), f32[8,24,1088]{2,1,0:T(8,128)S(1)}, u32[]{:S(2)}, u32[]{:S(2)}) %all-to-all-start.2) | async-done | bytes 835616 | tf_op jit(solution)/shard_map/all_to_all | solution.py:34
  121.6 1.4 copy-done.2
  123.0 6.9 %all-to-all-start.3 = ((f32[8,64,1088]{2,1,0:T(8,128)}), f32[8,64,1088]{2,1,0:T(8,128)S(1)}, u32[]{:S(2)}, u32[]{:S(2)}) async-start(f32[8,64,1088]{2,1,0:T(8,128)} %copy-done.2), calls=%async_computation.3 | async-start | bytes 4718592 | tf_op jit(solution)/shard_map/all_to_all | solution.py:34
  130.3 2.7 %collective-permute-start.16 = (f32[64,640]{1,0:T(8,128)S(1)}, f32[64,640]{1,0:T(8,128)S(1)}, u32[]{:S(2)}, u32[]{:S(2)}) collective-permute-start(f32[64,640]{1,0:T(8,128)S(1)} %collective-permute-done.14.refs_2_), channel_id=1, source_target_pairs={{0,112},{16,0},{32,16},{48,32},{64,48},{80,64},{96,80},{112,96},{1... | collective-permute-start | bytes 491528 | tf_op jit(solution)/shard_map/ppermute | solution.py:26
  132.9 2.7 %collective-permute-done.15.refs_3_ = f32[64,640]{1,0:T(8,128)S(1)} collective-permute-done((f32[64,640]{1,0:T(8,128)S(1)}, f32[64,640]{1,0:T(8,128)S(1)}, u32[]{:S(2)}, u32[]{:S(2)}) %collective-permute-start.15) | collective-permute-done | bytes 163872 | tf_op jit(solution)/shard_map/ppermute | solution.py:26
  135.6 3.0 %collective-permute-start.18 = (f32[64,640]{1,0:T(8,128)S(1)}, f32[64,640]{1,0:T(8,128)S(1)}, u32[]{:S(2)}, u32[]{:S(2)}) collective-permute-start(f32[64,640]{1,0:T(8,128)S(1)} %collective-permute-done.16.refs_4_), channel_id=1, source_target_pairs={{0,112},{16,0},{32,16},{48,32},{64,48},{80,64},{96,80},{112,96},{1... | collective-permute-start | bytes 491528 | tf_op jit(solution)/shard_map/ppermute | solution.py:26
  138.6 2.7 %collective-permute-done.17.refs_5_ = f32[64,640]{1,0:T(8,128)S(1)} collective-permute-done((f32[64,640]{1,0:T(8,128)S(1)}, f32[64,640]{1,0:T(8,128)S(1)}, u32[]{:S(2)}, u32[]{:S(2)}) %collective-permute-start.17) | collective-permute-done | bytes 163872 | tf_op jit(solution)/shard_map/ppermute | solution.py:26
  141.3 5.7 %collective-permute-done.19.refs_7_ = f32[64,640]{1,0:T(8,128)S(1)} collective-permute-done((f32[64,640]{1,0:T(8,128)S(1)}, f32[64,640]{1,0:T(8,128)S(1)}, u32[]{:S(2)}, u32[]{:S(2)}) %collective-permute-start.19) | collective-permute-done | bytes 163872 | tf_op jit(solution)/shard_map/ppermute | solution.py:26
  147.6 5.0 %collective-permute-start.20 = (f32[512,640]{1,0:T(8,128)S(1)}, f32[512,640]{1,0:T(8,128)S(1)}, u32[]{:S(2)}, u32[]{:S(2)}) collective-permute-start(f32[512,640]{1,0:T(8,128)S(1)} %place.1.own), channel_id=1, source_target_pairs={{0,8},{8,0},{1,9},{9,1},{2,10},{10,2},{3,11},{11,3},{4,12},{12,4},... | collective-permute-start | bytes 3932168 | tf_op jit(solution)/shard_map/ppermute | solution.py:26
  152.6 1.1 copy-done.3
  153.6 1.6 collective-permute-done.20.other
  155.2 1.1 copy-done.5
  156.3 2.6 %all-to-all-done.3.refs_0_ = f32[8,64,1088]{2,1,0:T(8,128)S(1)} async-done(((f32[8,64,1088]{2,1,0:T(8,128)}), f32[8,64,1088]{2,1,0:T(8,128)S(1)}, u32[]{:S(2)}, u32[]{:S(2)}) %all-to-all-start.3) | async-done | bytes 2228256 | tf_op jit(solution)/shard_map/all_to_all | solution.py:34
  158.9 1.2 collective-permute-start.21
  160.2 1.3 copy-done.4
  161.6 1.3 copy-done.6
  162.9 0.9 split_grads.1
  164.3 8.7 %moments.1 = f32[544,640]{1,0:T(8,128)} custom-call(s32[3]{0:T(128)S(1)} %pad_add_fusion.place, s32[5]{0:T(128)S(1)} %convert_reduce_fusion.bounds, f32[8,64,1088]{2,1,0:T(8,128)S(1)} %all-to-all-done.3.refs_0_, f32[8,64,1088]{2,1,0:T(8,128)S(1)} %collective-permute-done.21.refs_1_, bf16[1024,640]{1,0:T(8,128)(2,1)S(1)} %get-tuple-element.67.refs_2_, ...), custom_call_target="tpu_custom_call" | custom-call | flops 1000 | bytes 1000 | tf_op jit(solution)/shard_map/moments/pallas_call | solution.py:264
  (45 shorter events, 3.1 us)
Async XLA Ops:
  0.0 42.0 %collective-permute-start.5 = (f32[2176,544]{0,1:T(8,128)}, f32[2176,544]{0,1:T(8,128)}, u32[]{:S(2)}, u32[]{:S(2)}) collective-permute-start(f32[2176,544]{0,1:T(8,128)} %param.6), channel_id=1, source_target_pairs={{0,8},{8,0},{1,9},{9,1},{2,10},{10,2},{3,11},{11,3},{4,12},{12,4},... | collective-permute-start | bytes 14204936 | tf_op jit(solution)/shard_map/ppermute | solution.py:26
  3.2 8.5 %collective-permute-start = (f32[32,2176]{1,0:T(8,128)}, f32[32,2176]{1,0:T(8,128)S(1)}, u32[]{:S(2)}, u32[]{:S(2)}) collective-permute-start(f32[32,2176]{1,0:T(8,128)} %param.5), channel_id=1, source_target_pairs={{0,128},{128,0},{1,129},{129,1},{2,130},{130,2},{3,131},{131,3},{4... | collective-permute-start | bytes 835592 | tf_op jit(solution)/shard_map/ppermute | solution.py:26
  3.3 1.1 copy-start.7
  4.4 1.0 copy-start.8
  7.4 8.6 %copy-start.9 = (f32[32,2176]{1,0:T(8,128)S(1)}, f32[32,2176]{1,0:T(8,128)}, u32[]{:S(2)}) copy-start(f32[32,2176]{1,0:T(8,128)} %param.5) | copy-start | bytes 835588
  11.7 3.4 %collective-permute-start.6 = (f32[512,640]{1,0:T(8,128)S(1)}, f32[512,640]{1,0:T(8,128)S(1)}, u32[]{:S(2)}, u32[]{:S(2)}) collective-permute-start(f32[512,640]{1,0:T(8,128)S(1)} %get-tuple-element.46), channel_id=1, source_target_pairs={{0,8},{8,0},{1,9},{9,1},{2,10},{10,2},{3,11},{11,3},{4,12},{12,4},... | collective-permute-start | bytes 3932168 | tf_op jit(solution)/shard_map/ppermute | solution.py:26
  15.9 16.0 %collective-permute-start.7 = (f32[256,640]{1,0:T(8,128)S(1)}, f32[256,640]{1,0:T(8,128)S(1)}, u32[]{:S(2)}, u32[]{:S(2)}) collective-permute-start(f32[256,640]{1,0:T(8,128)S(1)} %get-tuple-element.48), channel_id=1, source_target_pairs={{0,128},{128,0},{1,129},{129,1},{2,130},{130,2},{3,131},{131,3},{4... | collective-permute-start | bytes 1966088 | tf_op jit(solution)/shard_map/ppermute | solution.py:26
  16.1 23.2 %collective-permute-start.2 = (f32[64,2176]{1,0:T(8,128)S(1)}, f32[64,2176]{1,0:T(8,128)S(1)}, u32[]{:S(2)}, u32[]{:S(2)}) collective-permute-start(f32[64,2176]{1,0:T(8,128)S(1)} %constant_dynamic-update-slice_fusion.refs_0_), channel_id=1, source_target_pairs={{0,112},{16,0},{32,16},{48,32},{64,48},{80,64},{96,80},{112,96},{1... | collective-permute-start | bytes 1671176 | tf_op jit(solution)/shard_map/ppermute | solution.py:26
  21.2 20.8 %collective-permute-start.1 = (f32[64,2176]{1,0:T(8,128)S(1)}, f32[64,2176]{1,0:T(8,128)S(1)}, u32[]{:S(2)}, u32[]{:S(2)}) collective-permute-start(f32[64,2176]{1,0:T(8,128)S(1)} %constant_dynamic-update-slice_fusion.refs_0_), channel_id=1, source_target_pairs={{0,16},{16,32},{32,48},{48,64},{64,80},{80,96},{96,112},{112,0},{1... | collective-permute-start | bytes 1671176 | tf_op jit(solution)/shard_map/ppermute | solution.py:26
  32.9 46.4 %all-to-all-start = ((f32[8,32,640]{2,1,0:T(8,128)}), f32[8,32,640]{2,1,0:T(8,128)S(1)}, u32[]{:S(2)}, u32[]{:S(2)}) async-start(f32[8,32,640]{2,1,0:T(8,128)} %bitcast.6), calls=%async_computation | async-start | bytes 1310720 | tf_op jit(solution)/shard_map/all_to_all | solution.py:34
  39.3 27.1 %collective-permute-start.4 = (f32[64,2176]{1,0:T(8,128)S(1)}, f32[64,2176]{1,0:T(8,128)S(1)}, u32[]{:S(2)}, u32[]{:S(2)}) collective-permute-start(f32[64,2176]{1,0:T(8,128)S(1)} %collective-permute-done.2.refs_2_), channel_id=1, source_target_pairs={{0,112},{16,0},{32,16},{48,32},{64,48},{80,64},{96,80},{112,96},{1... | collective-permute-start | bytes 1671176 | tf_op jit(solution)/shard_map/ppermute | solution.py:26
  42.0 26.5 %collective-permute-start.3 = (f32[64,2176]{1,0:T(8,128)S(1)}, f32[64,2176]{1,0:T(8,128)}, u32[]{:S(2)}, u32[]{:S(2)}) collective-permute-start(f32[64,2176]{1,0:T(8,128)S(1)} %collective-permute-done.1.refs_1_), channel_id=1, source_target_pairs={{0,16},{16,32},{32,48},{48,64},{64,80},{80,96},{96,112},{112,0},{1... | collective-permute-start | bytes 1671176 | tf_op jit(solution)/shard_map/ppermute | solution.py:26
  42.0 2.3 %copy-start = (f32[2176,544]{0,1:T(8,128)S(1)}, f32[2176,544]{0,1:T(8,128)}, u32[]{:S(2)}) copy-start(f32[2176,544]{0,1:T(8,128)} %param.6) | copy-start | bytes 14204932
  68.5 17.4 %collective-permute-start.9 = (f32[64,2176]{1,0:T(8,128)}, f32[64,2176]{1,0:T(8,128)}, u32[]{:S(2)}, u32[]{:S(2)}) collective-permute-start(f32[64,2176]{1,0:T(8,128)} %collective-permute-done.3.refs_3_), channel_id=1, source_target_pairs={{0,16},{16,32},{32,48},{48,64},{64,80},{80,96},{96,112},{112,0},{1... | collective-permute-start | bytes 1671176 | tf_op jit(solution)/shard_map/ppermute | solution.py:26
  68.5 18.5 %collective-permute-start.10 = (f32[64,2176]{1,0:T(8,128)S(1)}, f32[64,2176]{1,0:T(8,128)}, u32[]{:S(2)}, u32[]{:S(2)}) collective-permute-start(f32[64,2176]{1,0:T(8,128)S(1)} %collective-permute-done.4.refs_4_), channel_id=1, source_target_pairs={{0,112},{16,0},{32,16},{48,32},{64,48},{80,64},{96,80},{112,96},{1... | collective-permute-start | bytes 1671176 | tf_op jit(solution)/shard_map/ppermute | solution.py:26
  79.2 24.7 %all-to-all-start.1 = ((f32[8,40,1088]{2,1,0:T(8,128)}), f32[8,40,1088]{2,1,0:T(8,128)S(1)}, u32[]{:S(2)}, u32[]{:S(2)}) async-start(f32[8,40,1088]{2,1,0:T(8,128)} %bitcast.7), calls=%async_computation.1 | async-start | bytes 2949120 | tf_op jit(solution)/shard_map/all_to_all | solution.py:34
  86.9 10.4 %collective-permute-start.11 = (f32[32,2176]{1,0:T(8,128)S(1)}, f32[32,2176]{1,0:T(8,128)S(1)}, u32[]{:S(2)}, u32[]{:S(2)}) collective-permute-start(f32[32,2176]{1,0:T(8,128)S(1)} %slice.8), channel_id=1, source_target_pairs={{0,16},{16,32},{32,48},{48,64},{64,80},{80,96},{96,112},{112,0},{1... | collective-permute-start | bytes 835592 | tf_op jit(solution)/shard_map/ppermute | solution.py:26
  87.9 9.3 %collective-permute-start.12 = (f32[32,2176]{1,0:T(8,128)S(1)}, f32[32,2176]{1,0:T(8,128)S(1)}, u32[]{:S(2)}, u32[]{:S(2)}) collective-permute-start(f32[32,2176]{1,0:T(8,128)S(1)} %slice.9), channel_id=1, source_target_pairs={{0,112},{16,0},{32,16},{48,32},{64,48},{80,64},{96,80},{112,96},{1... | collective-permute-start | bytes 835592 | tf_op jit(solution)/shard_map/ppermute | solution.py:26
  90.7 12.6 %collective-permute-start.8 = (f32[1,32,640]{2,1,0:T(8,128)S(1)}, f32[1,32,640]{2,1,0:T(8,128)S(1)}, u32[]{:S(2)}, u32[]{:S(2)}) collective-permute-start(f32[1,32,640]{2,1,0:T(8,128)S(1)} %sum_copies.2.own), channel_id=1, source_target_pairs={{0,128},{128,0},{1,129},{129,1},{2,130},{130,2},{3,131},{131,3},{4... | collective-permute-start | bytes 245768 | tf_op jit(solution)/shard_map/ppermute | solution.py:26
  91.1 2.3 %copy-start.1 = (f32[2176,544]{0,1:T(8,128)S(1)}, f32[2176,544]{0,1:T(8,128)}, u32[]{:S(2)}) copy-start(f32[2176,544]{0,1:T(8,128)} %param.6) | copy-start | bytes 14204932
  103.9 17.5 %all-to-all-start.2 = ((f32[8,24,1088]{2,1,0:T(8,128)}), f32[8,24,1088]{2,1,0:T(8,128)S(1)}, u32[]{:S(2)}, u32[]{:S(2)}) async-start(f32[8,24,1088]{2,1,0:T(8,128)} %bitcast.8), calls=%async_computation.2 | async-start | bytes 1769472 | tf_op jit(solution)/shard_map/all_to_all | solution.py:34
  111.2 4.2 %collective-permute-start.14 = (f32[64,640]{1,0:T(8,128)S(1)}, f32[64,640]{1,0:T(8,128)S(1)}, u32[]{:S(2)}, u32[]{:S(2)}) collective-permute-start(f32[64,640]{1,0:T(8,128)S(1)} %pair.1.refs_0_), channel_id=1, source_target_pairs={{0,112},{16,0},{32,16},{48,32},{64,48},{80,64},{96,80},{112,96},{1... | collective-permute-start | bytes 491528 | tf_op jit(solution)/shard_map/ppermute | solution.py:26
  111.2 5.4 %collective-permute-start.13 = (f32[64,640]{1,0:T(8,128)S(1)}, f32[64,640]{1,0:T(8,128)S(1)}, u32[]{:S(2)}, u32[]{:S(2)}) collective-permute-start(f32[64,640]{1,0:T(8,128)S(1)} %pair.1.refs_0_), channel_id=1, source_target_pairs={{0,16},{16,32},{32,48},{48,64},{64,80},{80,96},{96,112},{112,0},{1... | collective-permute-start | bytes 491528 | tf_op jit(solution)/shard_map/ppermute | solution.py:26
  121.6 1.4 copy-start.2
  123.0 35.8 %all-to-all-start.3 = ((f32[8,64,1088]{2,1,0:T(8,128)}), f32[8,64,1088]{2,1,0:T(8,128)S(1)}, u32[]{:S(2)}, u32[]{:S(2)}) async-start(f32[8,64,1088]{2,1,0:T(8,128)} %copy-done.2), calls=%async_computation.3 | async-start | bytes 4718592 | tf_op jit(solution)/shard_map/all_to_all | solution.py:34
  129.9 30.2 %copy-start.10 = (s32[1024]{0:T(1024)S(1)}, s32[1024]{0:T(1024)}, u32[]{:S(2)}) copy-start(s32[1024]{0:T(1024)} %param.9) | copy-start | bytes 12292
  129.9 5.7 %collective-permute-start.15 = (f32[64,640]{1,0:T(8,128)S(1)}, f32[64,640]{1,0:T(8,128)S(1)}, u32[]{:S(2)}, u32[]{:S(2)}) collective-permute-start(f32[64,640]{1,0:T(8,128)S(1)} %collective-permute-done.13.refs_1_), channel_id=1, source_target_pairs={{0,16},{16,32},{32,48},{48,64},{64,80},{80,96},{96,112},{112,0},{1... | collective-permute-start | bytes 491528 | tf_op jit(solution)/shard_map/ppermute | solution.py:26
  130.3 5.4 %collective-permute-start.16 = (f32[64,640]{1,0:T(8,128)S(1)}, f32[64,640]{1,0:T(8,128)S(1)}, u32[]{:S(2)}, u32[]{:S(2)}) collective-permute-start(f32[64,640]{1,0:T(8,128)S(1)} %collective-permute-done.14.refs_2_), channel_id=1, source_target_pairs={{0,112},{16,0},{32,16},{48,32},{64,48},{80,64},{96,80},{112,96},{1... | collective-permute-start | bytes 491528 | tf_op jit(solution)/shard_map/ppermute | solution.py:26
  135.6 5.7 %collective-permute-start.17 = (f32[64,640]{1,0:T(8,128)S(1)}, f32[64,640]{1,0:T(8,128)S(1)}, u32[]{:S(2)}, u32[]{:S(2)}) collective-permute-start(f32[64,640]{1,0:T(8,128)S(1)} %collective-permute-done.15.refs_3_), channel_id=1, source_target_pairs={{0,16},{16,32},{32,48},{48,64},{64,80},{80,96},{96,112},{112,0},{1... | collective-permute-start | bytes 491528 | tf_op jit(solution)/shard_map/ppermute | solution.py:26
  135.6 5.7 %collective-permute-start.18 = (f32[64,640]{1,0:T(8,128)S(1)}, f32[64,640]{1,0:T(8,128)S(1)}, u32[]{:S(2)}, u32[]{:S(2)}) collective-permute-start(f32[64,640]{1,0:T(8,128)S(1)} %collective-permute-done.16.refs_4_), channel_id=1, source_target_pairs={{0,112},{16,0},{32,16},{48,32},{64,48},{80,64},{96,80},{112,96},{1... | collective-permute-start | bytes 491528 | tf_op jit(solution)/shard_map/ppermute | solution.py:26
  141.3 5.7 %collective-permute-start.19 = (f32[64,640]{1,0:T(8,128)S(1)}, f32[64,640]{1,0:T(8,128)S(1)}, u32[]{:S(2)}, u32[]{:S(2)}) collective-permute-start(f32[64,640]{1,0:T(8,128)S(1)} %collective-permute-done.17.refs_5_), channel_id=1, source_target_pairs={{0,16},{16,32},{32,48},{48,64},{64,80},{80,96},{96,112},{112,0},{1... | collective-permute-start | bytes 491528 | tf_op jit(solution)/shard_map/ppermute | solution.py:26
  147.6 7.6 %collective-permute-start.20 = (f32[512,640]{1,0:T(8,128)S(1)}, f32[512,640]{1,0:T(8,128)S(1)}, u32[]{:S(2)}, u32[]{:S(2)}) collective-permute-start(f32[512,640]{1,0:T(8,128)S(1)} %place.1.own), channel_id=1, source_target_pairs={{0,8},{8,0},{1,9},{9,1},{2,10},{10,2},{3,11},{11,3},{4,12},{12,4},... | collective-permute-start | bytes 3932168 | tf_op jit(solution)/shard_map/ppermute | solution.py:26
  152.6 1.1 copy-start.3
  155.2 1.1 copy-start.5
  158.9 5.4 %collective-permute-start.21 = (f32[8,64,1088]{2,1,0:T(8,128)S(1)}, f32[8,64,1088]{2,1,0:T(8,128)S(1)}, u32[]{:S(2)}, u32[]{:S(2)}) collective-permute-start(f32[8,64,1088]{2,1,0:T(8,128)S(1)} %all-to-all-done.3.refs_0_), channel_id=1, source_target_pairs={{0,8},{8,0},{1,9},{9,1},{2,10},{10,2},{3,11},{11,3},{4,12},{12,4},... | collective-permute-start | bytes 6684680 | tf_op jit(solution)/shard_map/ppermute | solution.py:26
  160.2 1.3 copy-start.4
  161.6 1.3 copy-start.6

commit v6 on v5

--- a/solution.py
+++ b/solution.py
@@ -188,11 +188,13 @@
     for ref, core in ((own, place[1]), (other, 1 - place[1])):
         into = pl.ds(pl.multiple_of(core * rows, rows), rows)
         high[into, :], low[into, :] = halved(ref[...])
+    for ref in (high, low):
+        ref[2 * rows :, :] = jnp.zeros((DEPTH, own.shape[1]), jnp.bfloat16)
 
 
 def moments_kernel(place, bounds, *refs):
     acts_refs, (grads_high, grads_low, out) = refs[:2], refs[2:5]
-    acts_high, acts_low, turned_high, turned_low, moment = refs[5:]
+    acts_high, acts_low, moment = refs[5:]
     z, core, lo = place[0], place[1], place[2]
     cols = out.shape[0]
     first_rows = 2 * len(FIRST) * BLOCK // 8
@@ -215,40 +217,45 @@
                 xl = 1 - lo if far else lo
                 row = ((xl * 8 + lax.rem(z + distance + 8, 8)) * 2 + of_core) * BLOCK
                 split_store(value, acts_high, acts_low, row)
-    for start in range(0, TOKENS, DEPTH):
-        rows = slice(start, start + DEPTH)
-        for ref, turned in ((acts_high, turned_high), (acts_low, turned_low)):
-            turned[:, rows] = ref[rows, :].T
+    for ref in (acts_high, acts_low):
+        ref[TOKENS:, :] = jnp.zeros((DEPTH, cols), jnp.bfloat16)
 
     def product(a, b):
         return lax.dot_general(
-            a, b, (((1,), (0,)), ((), ())), preferred_element_type=jnp.float32
+            a, b, (((0,), (0,)), ((), ())), preferred_element_type=jnp.float32
         )
 
-    for seq in range(SEQS):
+    out[...] = jnp.zeros_like(out)
+
+    def add_sequence(seq, carry):
         first, end = bounds[seq], bounds[seq + 1]
-        moment[...] = jnp.zeros_like(moment)
-
-        def block(step, carry):
-            rows = pl.ds(pl.multiple_of(step * DEPTH, DEPTH), DEPTH)
-            number = step * DEPTH + lax.broadcasted_iota(jnp.int32, (DEPTH, 1), 0)
+        base = (first // 16) * 16
+
+        def block(step):
+            start = pl.multiple_of(base + step * DEPTH, 16)
+            rows = pl.ds(start, DEPTH)
+            number = start + lax.broadcasted_iota(jnp.int32, (DEPTH, 1), 0)
             mine = (number >= first) & (number < end)
-            grads_h = jnp.where(mine, grads_high[rows, :].astype(jnp.float32), 0.0).astype(jnp.bfloat16)
-            grads_l = jnp.where(mine, grads_low[rows, :].astype(jnp.float32), 0.0).astype(jnp.bfloat16)
-            acts_h, acts_l = turned_high[:, rows], turned_low[:, rows]
-            moment[...] += product(acts_h, grads_h) + (
+            grads_h, grads_l = [
+                jnp.where(mine, ref[rows, :].astype(jnp.float32), 0.0).astype(jnp.bfloat16)
+                for ref in (grads_high, grads_low)
+            ]
+            acts_h, acts_l = acts_high[rows, :], acts_low[rows, :]
+            return product(acts_h, grads_h) + (
                 product(acts_l, grads_h) + product(acts_h, grads_l)
             )
+
+        moment[...] = block(0)
+
+        def add_block(step, carry):
+            moment[...] += block(step)
             return carry
 
-        lax.fori_loop(first // DEPTH, (end + DEPTH - 1) // DEPTH, block, 0)
-        squared = moment[...] * moment[...]
-        if seq == 0:
-            out[...] = squared
-        elif seq < SEQS - 1:
-            out[...] += squared
-        else:
-            out[...] = (out[...] + squared) * (1.0 / SEQS)
+        lax.fori_loop(1, (end - base + DEPTH - 1) // DEPTH, add_block, 0)
+        out[...] += moment[...] * moment[...] * (1.0 / SEQS)
+        return carry
+
+    lax.fori_loop(0, SEQS, add_sequence, 0)
 
 
 def eigenvalues(place, acts, grads, seq_ids):
@@ -257,7 +264,7 @@
     cols, out_cols = acts[0].shape[2] // 2, grads[0].shape[1]
     grads = call(
         split_grads_kernel,
-        [bf16(TOKENS, out_cols)] * 2,
+        [bf16(TOKENS + DEPTH, out_cols)] * 2,
         [SMEM, VMEM, VMEM],
         name="split_grads",
     )(place, *grads)
@@ -266,10 +273,8 @@
         f32(cols, out_cols),
         [SMEM, SMEM] + [VMEM] * (len(acts) + len(grads)),
         [
-            pltpu.VMEM((TOKENS, cols), jnp.bfloat16),
-            pltpu.VMEM((TOKENS, cols), jnp.bfloat16),
-            pltpu.VMEM((cols, TOKENS), jnp.bfloat16),
-            pltpu.VMEM((cols, TOKENS), jnp.bfloat16),
+            pltpu.VMEM((TOKENS + DEPTH, cols), jnp.bfloat16),
+            pltpu.VMEM((TOKENS + DEPTH, cols), jnp.bfloat16),
             pltpu.VMEM((cols, out_cols), jnp.float32),
         ],
         name="moments",

time: 174 us -> 172 us (0.989)
  no operation moved by 1% of the time
where the time goes in v6:
time: 172 us; the launch traced here: 171 us
  waiting for transfers between devices  62.6 us (36%)
  starting transfers between devices  58.6 us (34%)
  Pallas kernels  34.9 us (20%)
  local copies, waits for them, and re-layouts  14.9 us (9%)
    ppermute x22, waiting for transfers between devices, shifted(): return lax.ppermute(value, axis, [(i, (i + by) % n) for i in range(n)])  55.2 us
    ppermute x22, starting transfers between devices, shifted(): return lax.ppermute(value, axis, [(i, (i + by) % n) for i in range(n)])  31.4 us
    all_to_all x4, starting transfers between devices, swapped(): return lax.all_to_all(value, axes, 0, 0)  27.3 us
    pallas_call x2, Pallas kernels, products(): call(products_kernel, f32(rows, cols), [VMEM] * (1 + len(blocks)), [pltpu...  14.1 us
    unnamed x23, local copies, waits for them, and re-layouts  13 us
    pallas_call x2, Pallas kernels, split_basis(): call(basis_kernel, pltpu.VMEM((2, 2 * rows, depth), jnp.bfloat16), [VMEM,...  7.61 us
    all_to_all x4, waiting for transfers between devices, swapped(): return lax.all_to_all(value, axes, 0, 0)  7.39 us
    pallas_call x1, Pallas kernels, eigenvalues(): call(moments_kernel, f32(cols, out_cols), [SMEM, SMEM] + [VMEM] * (len(ac...  7.22 us
  transfers between devices with their start and end apart: 26, of which 14 were waited for; matrix products, arithmetic and copies ran while one was open for 1% of the time, Pallas kernels for 16%

profile of v6, /device:TPU:1, one launch (start us, length us, event | category | flops | bytes accessed | tf_op | source)
XLA Modules:
  0.0 171.5 jit_solution(16736141833978836662)
XLA Ops:
  0.0 3.2 %collective-permute-start.5 = (f32[2176,544]{0,1:T(8,128)}, f32[2176,544]{0,1:T(8,128)}, u32[]{:S(2)}, u32[]{:S(2)}) collective-permute-start(f32[2176,544]{0,1:T(8,128)} %param.6), channel_id=1, source_target_pairs={{0,8},{8,0},{1,9},{9,1},{2,10},{10,2},{3,11},{11,3},{4,12},{12,4},... | collective-permute-start | bytes 14204936 | tf_op jit(solution)/shard_map/ppermute | solution.py:26
  3.3 1.1 copy-done.7
  4.4 1.0 copy-done.8
  5.4 2.0 %rotate_grads.1 = (f32[512,640]{1,0:T(8,128)S(1)}, f32[512,640]{1,0:T(8,128)S(1)}) custom-call(s32[3]{0:T(128)S(1)} %pad_add_fusion.place, f32[160,1024]{1,0:T(8,128)S(1)} %bitcast.11, f32[160,640]{1,0:T(8,128)S(1)} %copy-done.8), custom_call_target="tpu_custom_call" | custom-call | flops 1000 | bytes 1000 | tf_op jit(solution)/shard_map/rotate_grads/pallas_call | solution.py:297
  7.4 4.3 %collective-permute-done = f32[32,2176]{1,0:T(8,128)S(1)} collective-permute-done((f32[32,2176]{1,0:T(8,128)}, f32[32,2176]{1,0:T(8,128)S(1)}, u32[]{:S(2)}, u32[]{:S(2)}) %collective-permute-start) | collective-permute-done | bytes 278560 | tf_op jit(solution)/shard_map/ppermute | solution.py:26
  11.7 0.8 collective-permute-start.6
  12.5 2.7 %collective-permute-done.6.arrived = f32[512,640]{1,0:T(8,128)S(1)} collective-permute-done((f32[512,640]{1,0:T(8,128)S(1)}, f32[512,640]{1,0:T(8,128)S(1)}, u32[]{:S(2)}, u32[]{:S(2)}) %collective-permute-start.6) | collective-permute-done | bytes 1310752 | tf_op jit(solution)/shard_map/ppermute | solution.py:26
  15.2 0.7 add_halves.1
  16.1 5.1 %collective-permute-start.2 = (f32[64,2176]{1,0:T(8,128)S(1)}, f32[64,2176]{1,0:T(8,128)S(1)}, u32[]{:S(2)}, u32[]{:S(2)}) collective-permute-start(f32[64,2176]{1,0:T(8,128)S(1)} %constant_dynamic-update-slice_fusion.refs_0_), channel_id=1, source_target_pairs={{0,112},{16,0},{32,16},{48,32},{64,48},{80,64},{96,80},{112,96},{1... | collective-permute-start | bytes 1671176 | tf_op jit(solution)/shard_map/ppermute | solution.py:26
  21.2 10.8 %collective-permute-done.7.b = f32[256,640]{1,0:T(8,128)S(1)} collective-permute-done((f32[256,640]{1,0:T(8,128)S(1)}, f32[256,640]{1,0:T(8,128)S(1)}, u32[]{:S(2)}, u32[]{:S(2)}) %collective-permute-start.7) | collective-permute-done | bytes 655392 | tf_op jit(solution)/shard_map/ppermute | solution.py:26
  32.0 0.9 add.5
  32.9 6.5 %all-to-all-start = ((f32[8,32,640]{2,1,0:T(8,128)}), f32[8,32,640]{2,1,0:T(8,128)S(1)}, u32[]{:S(2)}, u32[]{:S(2)}) async-start(f32[8,32,640]{2,1,0:T(8,128)} %bitcast.6), calls=%async_computation | async-start | bytes 1310720 | tf_op jit(solution)/shard_map/all_to_all | solution.py:34
  39.3 2.7 %collective-permute-start.4 = (f32[64,2176]{1,0:T(8,128)S(1)}, f32[64,2176]{1,0:T(8,128)S(1)}, u32[]{:S(2)}, u32[]{:S(2)}) collective-permute-start(f32[64,2176]{1,0:T(8,128)S(1)} %collective-permute-done.2.refs_2_), channel_id=1, source_target_pairs={{0,112},{16,0},{32,16},{48,32},{64,48},{80,64},{96,80},{112,96},{1... | collective-permute-start | bytes 1671176 | tf_op jit(solution)/shard_map/ppermute | solution.py:26
  42.0 2.3 %copy-done = f32[2176,544]{0,1:T(8,128)S(1)} copy-done((f32[2176,544]{0,1:T(8,128)S(1)}, f32[2176,544]{0,1:T(8,128)}, u32[]{:S(2)}) %copy-start) | copy-done | bytes 4735000
  44.3 3.8 %split_basis.2.refs_5_ = bf16[2,1088,2176]{2,1,0:T(8,128)(2,1)S(1)} custom-call(f32[544,2176]{1,0:T(8,128)S(1)} %bitcast.9, f32[544,2176]{1,0:T(8,128)} %bitcast.5.other), custom_call_target="tpu_custom_call" | custom-call | flops 1000 | bytes 1000 | tf_op jit(solution)/shard_map/split_basis/pallas_call | solution.py:72
  48.2 18.2 %collective-permute-done.4.refs_4_ = f32[64,2176]{1,0:T(8,128)S(1)} collective-permute-done((f32[64,2176]{1,0:T(8,128)S(1)}, f32[64,2176]{1,0:T(8,128)S(1)}, u32[]{:S(2)}, u32[]{:S(2)}) %collective-permute-start.4) | collective-permute-done | bytes 557088 | tf_op jit(solution)/shard_map/ppermute | solution.py:26
  66.4 2.1 %collective-permute-done.3.refs_3_ = f32[64,2176]{1,0:T(8,128)} collective-permute-done((f32[64,2176]{1,0:T(8,128)S(1)}, f32[64,2176]{1,0:T(8,128)}, u32[]{:S(2)}, u32[]{:S(2)}) %collective-permute-start.3) | collective-permute-done | bytes 557088 | tf_op jit(solution)/shard_map/ppermute | solution.py:26
  68.5 2.7 %collective-permute-start.10 = (f32[64,2176]{1,0:T(8,128)S(1)}, f32[64,2176]{1,0:T(8,128)}, u32[]{:S(2)}, u32[]{:S(2)}) collective-permute-start(f32[64,2176]{1,0:T(8,128)S(1)} %collective-permute-done.4.refs_4_), channel_id=1, source_target_pairs={{0,112},{16,0},{32,16},{48,32},{64,48},{80,64},{96,80},{112,96},{1... | collective-permute-start | bytes 1671176 | tf_op jit(solution)/shard_map/ppermute | solution.py:26
  71.1 8.1 %products.2 = f32[320,1088]{1,0:T(8,128)} custom-call(f32[64,2176]{1,0:T(8,128)S(1)} %constant_dynamic-update-slice_fusion.refs_0_, f32[64,2176]{1,0:T(8,128)S(1)} %collective-permute-done.1.refs_1_, f32[64,2176]{1,0:T(8,128)S(1)} %collective-permute-done.2.refs_2_, f32[64,2176]{1,0:T(8,128)} %collective-permute-done.3.refs_3_, ...), custom_call_target="tpu_custom_call" | custom-call | flops 1000 | bytes 1000 | tf_op jit(solution)/shard_map/products/pallas_call | solution.py:101
  79.2 6.7 %all-to-all-start.1 = ((f32[8,40,1088]{2,1,0:T(8,128)}), f32[8,40,1088]{2,1,0:T(8,128)S(1)}, u32[]{:S(2)}, u32[]{:S(2)}) async-start(f32[8,40,1088]{2,1,0:T(8,128)} %bitcast.7), calls=%async_computation.1 | async-start | bytes 2949120 | tf_op jit(solution)/shard_map/all_to_all | solution.py:34
  85.9 1.0 slice.8
  87.0 1.0 slice.9
  87.9 2.7 %collective-permute-start.12 = (f32[32,2176]{1,0:T(8,128)S(1)}, f32[32,2176]{1,0:T(8,128)S(1)}, u32[]{:S(2)}, u32[]{:S(2)}) collective-permute-start(f32[32,2176]{1,0:T(8,128)S(1)} %slice.9), channel_id=1, source_target_pairs={{0,112},{16,0},{32,16},{48,32},{64,48},{80,64},{96,80},{112,96},{1... | collective-permute-start | bytes 835592 | tf_op jit(solution)/shard_map/ppermute | solution.py:26
  91.1 2.3 %copy-done.1 = f32[2176,544]{0,1:T(8,128)S(1)} copy-done((f32[2176,544]{0,1:T(8,128)S(1)}, f32[2176,544]{0,1:T(8,128)}, u32[]{:S(2)}) %copy-start.1) | copy-done | bytes 4735000
  93.4 3.8 %split_basis.3.refs_4_ = bf16[2,1088,2176]{2,1,0:T(8,128)(2,1)S(1)} custom-call(f32[544,2176]{1,0:T(8,128)S(1)} %bitcast.10, f32[544,2176]{1,0:T(8,128)} %bitcast.5.other), custom_call_target="tpu_custom_call" | custom-call | flops 1000 | bytes 1000 | tf_op jit(solution)/shard_map/split_basis/pallas_call | solution.py:72
  97.3 6.1 %products.3 = f32[192,1088]{1,0:T(8,128)} custom-call(f32[64,2176]{1,0:T(8,128)} %collective-permute-done.9.refs_0_, f32[64,2176]{1,0:T(8,128)} %collective-permute-done.10.refs_1_, f32[32,2176]{1,0:T(8,128)S(1)} %collective-permute-done.11.refs_2_, f32[32,2176]{1,0:T(8,128)S(1)} %collective-permute-done.12.refs_3_, ...), custom_call_target="tpu_custom_call" | custom-call | flops 5000000000 | bytes 1000 | tf_op jit(solution)/shard_map/products/pallas_call | solution.py:101
  103.9 7.3 %all-to-all-start.2 = ((f32[8,24,1088]{2,1,0:T(8,128)}), f32[8,24,1088]{2,1,0:T(8,128)S(1)}, u32[]{:S(2)}, u32[]{:S(2)}) async-start(f32[8,24,1088]{2,1,0:T(8,128)} %bitcast.8), calls=%async_computation.2 | async-start | bytes 1769472 | tf_op jit(solution)/shard_map/all_to_all | solution.py:34
  111.2 1.4 collective-permute-start.13
  112.6 2.7 %collective-permute-done.14.refs_2_ = f32[64,640]{1,0:T(8,128)S(1)} collective-permute-done((f32[64,640]{1,0:T(8,128)S(1)}, f32[64,640]{1,0:T(8,128)S(1)}, u32[]{:S(2)}, u32[]{:S(2)}) %collective-permute-start.14) | collective-permute-done | bytes 163872 | tf_op jit(solution)/shard_map/ppermute | solution.py:26
  115.3 1.3 collective-permute-done.13.refs_1_
  116.6 4.8 %all-to-all-done.2.refs_1_ = f32[8,24,1088]{2,1,0:T(8,128)S(1)} async-done(((f32[8,24,1088]{2,1,0:T(8,128)}), f32[8,24,1088]{2,1,0:T(8,128)S(1)}, u32[]{:S(2)}, u32[]{:S(2)}) %all-to-all-start.2) | async-done | bytes 835616 | tf_op jit(solution)/shard_map/all_to_all | solution.py:34
  121.6 1.4 copy-done.2
  123.0 6.9 %all-to-all-start.3 = ((f32[8,64,1088]{2,1,0:T(8,128)}), f32[8,64,1088]{2,1,0:T(8,128)S(1)}, u32[]{:S(2)}, u32[]{:S(2)}) async-start(f32[8,64,1088]{2,1,0:T(8,128)} %copy-done.2), calls=%async_computation.3 | async-start | bytes 4718592 | tf_op jit(solution)/shard_map/all_to_all | solution.py:34
  130.3 2.7 %collective-permute-start.16 = (f32[64,640]{1,0:T(8,128)S(1)}, f32[64,640]{1,0:T(8,128)S(1)}, u32[]{:S(2)}, u32[]{:S(2)}) collective-permute-start(f32[64,640]{1,0:T(8,128)S(1)} %collective-permute-done.14.refs_2_), channel_id=1, source_target_pairs={{0,112},{16,0},{32,16},{48,32},{64,48},{80,64},{96,80},{112,96},{1... | collective-permute-start | bytes 491528 | tf_op jit(solution)/shard_map/ppermute | solution.py:26
  132.9 2.7 %collective-permute-done.15.refs_3_ = f32[64,640]{1,0:T(8,128)S(1)} collective-permute-done((f32[64,640]{1,0:T(8,128)S(1)}, f32[64,640]{1,0:T(8,128)S(1)}, u32[]{:S(2)}, u32[]{:S(2)}) %collective-permute-start.15) | collective-permute-done | bytes 163872 | tf_op jit(solution)/shard_map/ppermute | solution.py:26
  135.6 3.0 %collective-permute-start.18 = (f32[64,640]{1,0:T(8,128)S(1)}, f32[64,640]{1,0:T(8,128)S(1)}, u32[]{:S(2)}, u32[]{:S(2)}) collective-permute-start(f32[64,640]{1,0:T(8,128)S(1)} %collective-permute-done.16.refs_4_), channel_id=1, source_target_pairs={{0,112},{16,0},{32,16},{48,32},{64,48},{80,64},{96,80},{112,96},{1... | collective-permute-start | bytes 491528 | tf_op jit(solution)/shard_map/ppermute | solution.py:26
  138.6 2.7 %collective-permute-done.17.refs_5_ = f32[64,640]{1,0:T(8,128)S(1)} collective-permute-done((f32[64,640]{1,0:T(8,128)S(1)}, f32[64,640]{1,0:T(8,128)S(1)}, u32[]{:S(2)}, u32[]{:S(2)}) %collective-permute-start.17) | collective-permute-done | bytes 163872 | tf_op jit(solution)/shard_map/ppermute | solution.py:26
  141.3 5.7 %collective-permute-done.19.refs_7_ = f32[64,640]{1,0:T(8,128)S(1)} collective-permute-done((f32[64,640]{1,0:T(8,128)S(1)}, f32[64,640]{1,0:T(8,128)S(1)}, u32[]{:S(2)}, u32[]{:S(2)}) %collective-permute-start.19) | collective-permute-done | bytes 163872 | tf_op jit(solution)/shard_map/ppermute | solution.py:26
  147.6 5.0 %collective-permute-start.20 = (f32[512,640]{1,0:T(8,128)S(1)}, f32[512,640]{1,0:T(8,128)S(1)}, u32[]{:S(2)}, u32[]{:S(2)}) collective-permute-start(f32[512,640]{1,0:T(8,128)S(1)} %place.1.own), channel_id=1, source_target_pairs={{0,8},{8,0},{1,9},{9,1},{2,10},{10,2},{3,11},{11,3},{4,12},{12,4},... | collective-permute-start | bytes 3932168 | tf_op jit(solution)/shard_map/ppermute | solution.py:26
  152.6 1.1 copy-done.3
  153.6 1.6 collective-permute-done.20.other
  155.2 1.1 copy-done.5
  156.3 2.6 %all-to-all-done.3.refs_0_ = f32[8,64,1088]{2,1,0:T(8,128)S(1)} async-done(((f32[8,64,1088]{2,1,0:T(8,128)}), f32[8,64,1088]{2,1,0:T(8,128)S(1)}, u32[]{:S(2)}, u32[]{:S(2)}) %all-to-all-start.3) | async-done | bytes 2228256 | tf_op jit(solution)/shard_map/all_to_all | solution.py:34
  158.9 1.2 collective-permute-start.21
  160.2 1.3 copy-done.4
  161.6 1.3 copy-done.6
  162.9 1.0 split_grads.1
  164.3 7.2 %moments.1 = f32[544,640]{1,0:T(8,128)} custom-call(s32[3]{0:T(128)S(1)} %pad_add_fusion.place, s32[5]{0:T(128)S(1)} %convert_reduce_fusion.bounds, f32[8,64,1088]{2,1,0:T(8,128)S(1)} %all-to-all-done.3.refs_0_, f32[8,64,1088]{2,1,0:T(8,128)S(1)} %collective-permute-done.21.refs_1_, bf16[1280,640]{1,0:T(8,128)(2,1)S(1)} %get-tuple-element.67.refs_2_, ...), custom_call_target="tpu_custom_call" | custom-call | flops 1000 | bytes 1000 | tf_op jit(solution)/shard_map/moments/pallas_call | solution.py:271
  (45 shorter events, 3.0 us)
Async XLA Ops:
  0.0 42.0 %collective-permute-start.5 = (f32[2176,544]{0,1:T(8,128)}, f32[2176,544]{0,1:T(8,128)}, u32[]{:S(2)}, u32[]{:S(2)}) collective-permute-start(f32[2176,544]{0,1:T(8,128)} %param.6), channel_id=1, source_target_pairs={{0,8},{8,0},{1,9},{9,1},{2,10},{10,2},{3,11},{11,3},{4,12},{12,4},... | collective-permute-start | bytes 14204936 | tf_op jit(solution)/shard_map/ppermute | solution.py:26
  3.2 8.5 %collective-permute-start = (f32[32,2176]{1,0:T(8,128)}, f32[32,2176]{1,0:T(8,128)S(1)}, u32[]{:S(2)}, u32[]{:S(2)}) collective-permute-start(f32[32,2176]{1,0:T(8,128)} %param.5), channel_id=1, source_target_pairs={{0,128},{128,0},{1,129},{129,1},{2,130},{130,2},{3,131},{131,3},{4... | collective-permute-start | bytes 835592 | tf_op jit(solution)/shard_map/ppermute | solution.py:26
  3.3 1.1 copy-start.7
  4.4 1.0 copy-start.8
  5.4 10.6 %copy-start.9 = (f32[32,2176]{1,0:T(8,128)S(1)}, f32[32,2176]{1,0:T(8,128)}, u32[]{:S(2)}) copy-start(f32[32,2176]{1,0:T(8,128)} %param.5) | copy-start | bytes 835588
  11.7 3.4 %collective-permute-start.6 = (f32[512,640]{1,0:T(8,128)S(1)}, f32[512,640]{1,0:T(8,128)S(1)}, u32[]{:S(2)}, u32[]{:S(2)}) collective-permute-start(f32[512,640]{1,0:T(8,128)S(1)} %get-tuple-element.46), channel_id=1, source_target_pairs={{0,8},{8,0},{1,9},{9,1},{2,10},{10,2},{3,11},{11,3},{4,12},{12,4},... | collective-permute-start | bytes 3932168 | tf_op jit(solution)/shard_map/ppermute | solution.py:26
  15.9 16.0 %collective-permute-start.7 = (f32[256,640]{1,0:T(8,128)S(1)}, f32[256,640]{1,0:T(8,128)S(1)}, u32[]{:S(2)}, u32[]{:S(2)}) collective-permute-start(f32[256,640]{1,0:T(8,128)S(1)} %get-tuple-element.48), channel_id=1, source_target_pairs={{0,128},{128,0},{1,129},{129,1},{2,130},{130,2},{3,131},{131,3},{4... | collective-permute-start | bytes 1966088 | tf_op jit(solution)/shard_map/ppermute | solution.py:26
  16.1 23.2 %collective-permute-start.2 = (f32[64,2176]{1,0:T(8,128)S(1)}, f32[64,2176]{1,0:T(8,128)S(1)}, u32[]{:S(2)}, u32[]{:S(2)}) collective-permute-start(f32[64,2176]{1,0:T(8,128)S(1)} %constant_dynamic-update-slice_fusion.refs_0_), channel_id=1, source_target_pairs={{0,112},{16,0},{32,16},{48,32},{64,48},{80,64},{96,80},{112,96},{1... | collective-permute-start | bytes 1671176 | tf_op jit(solution)/shard_map/ppermute | solution.py:26
  21.2 20.8 %collective-permute-start.1 = (f32[64,2176]{1,0:T(8,128)S(1)}, f32[64,2176]{1,0:T(8,128)S(1)}, u32[]{:S(2)}, u32[]{:S(2)}) collective-permute-start(f32[64,2176]{1,0:T(8,128)S(1)} %constant_dynamic-update-slice_fusion.refs_0_), channel_id=1, source_target_pairs={{0,16},{16,32},{32,48},{48,64},{64,80},{80,96},{96,112},{112,0},{1... | collective-permute-start | bytes 1671176 | tf_op jit(solution)/shard_map/ppermute | solution.py:26
  32.9 46.4 %all-to-all-start = ((f32[8,32,640]{2,1,0:T(8,128)}), f32[8,32,640]{2,1,0:T(8,128)S(1)}, u32[]{:S(2)}, u32[]{:S(2)}) async-start(f32[8,32,640]{2,1,0:T(8,128)} %bitcast.6), calls=%async_computation | async-start | bytes 1310720 | tf_op jit(solution)/shard_map/all_to_all | solution.py:34
  39.3 27.1 %collective-permute-start.4 = (f32[64,2176]{1,0:T(8,128)S(1)}, f32[64,2176]{1,0:T(8,128)S(1)}, u32[]{:S(2)}, u32[]{:S(2)}) collective-permute-start(f32[64,2176]{1,0:T(8,128)S(1)} %collective-permute-done.2.refs_2_), channel_id=1, source_target_pairs={{0,112},{16,0},{32,16},{48,32},{64,48},{80,64},{96,80},{112,96},{1... | collective-permute-start | bytes 1671176 | tf_op jit(solution)/shard_map/ppermute | solution.py:26
  42.0 26.5 %collective-permute-start.3 = (f32[64,2176]{1,0:T(8,128)S(1)}, f32[64,2176]{1,0:T(8,128)}, u32[]{:S(2)}, u32[]{:S(2)}) collective-permute-start(f32[64,2176]{1,0:T(8,128)S(1)} %collective-permute-done.1.refs_1_), channel_id=1, source_target_pairs={{0,16},{16,32},{32,48},{48,64},{64,80},{80,96},{96,112},{112,0},{1... | collective-permute-start | bytes 1671176 | tf_op jit(solution)/shard_map/ppermute | solution.py:26
  42.0 2.3 %copy-start = (f32[2176,544]{0,1:T(8,128)S(1)}, f32[2176,544]{0,1:T(8,128)}, u32[]{:S(2)}) copy-start(f32[2176,544]{0,1:T(8,128)} %param.6) | copy-start | bytes 14204932
  68.5 17.4 %collective-permute-start.9 = (f32[64,2176]{1,0:T(8,128)}, f32[64,2176]{1,0:T(8,128)}, u32[]{:S(2)}, u32[]{:S(2)}) collective-permute-start(f32[64,2176]{1,0:T(8,128)} %collective-permute-done.3.refs_3_), channel_id=1, source_target_pairs={{0,16},{16,32},{32,48},{48,64},{64,80},{80,96},{96,112},{112,0},{1... | collective-permute-start | bytes 1671176 | tf_op jit(solution)/shard_map/ppermute | solution.py:26
  68.5 18.5 %collective-permute-start.10 = (f32[64,2176]{1,0:T(8,128)S(1)}, f32[64,2176]{1,0:T(8,128)}, u32[]{:S(2)}, u32[]{:S(2)}) collective-permute-start(f32[64,2176]{1,0:T(8,128)S(1)} %collective-permute-done.4.refs_4_), channel_id=1, source_target_pairs={{0,112},{16,0},{32,16},{48,32},{64,48},{80,64},{96,80},{112,96},{1... | collective-permute-start | bytes 1671176 | tf_op jit(solution)/shard_map/ppermute | solution.py:26
  79.2 24.7 %all-to-all-start.1 = ((f32[8,40,1088]{2,1,0:T(8,128)}), f32[8,40,1088]{2,1,0:T(8,128)S(1)}, u32[]{:S(2)}, u32[]{:S(2)}) async-start(f32[8,40,1088]{2,1,0:T(8,128)} %bitcast.7), calls=%async_computation.1 | async-start | bytes 2949120 | tf_op jit(solution)/shard_map/all_to_all | solution.py:34
  86.9 10.4 %collective-permute-start.11 = (f32[32,2176]{1,0:T(8,128)S(1)}, f32[32,2176]{1,0:T(8,128)S(1)}, u32[]{:S(2)}, u32[]{:S(2)}) collective-permute-start(f32[32,2176]{1,0:T(8,128)S(1)} %slice.8), channel_id=1, source_target_pairs={{0,16},{16,32},{32,48},{48,64},{64,80},{80,96},{96,112},{112,0},{1... | collective-permute-start | bytes 835592 | tf_op jit(solution)/shard_map/ppermute | solution.py:26
  87.9 9.3 %collective-permute-start.12 = (f32[32,2176]{1,0:T(8,128)S(1)}, f32[32,2176]{1,0:T(8,128)S(1)}, u32[]{:S(2)}, u32[]{:S(2)}) collective-permute-start(f32[32,2176]{1,0:T(8,128)S(1)} %slice.9), channel_id=1, source_target_pairs={{0,112},{16,0},{32,16},{48,32},{64,48},{80,64},{96,80},{112,96},{1... | collective-permute-start | bytes 835592 | tf_op jit(solution)/shard_map/ppermute | solution.py:26
  90.7 12.6 %collective-permute-start.8 = (f32[1,32,640]{2,1,0:T(8,128)S(1)}, f32[1,32,640]{2,1,0:T(8,128)S(1)}, u32[]{:S(2)}, u32[]{:S(2)}) collective-permute-start(f32[1,32,640]{2,1,0:T(8,128)S(1)} %sum_copies.2.own), channel_id=1, source_target_pairs={{0,128},{128,0},{1,129},{129,1},{2,130},{130,2},{3,131},{131,3},{4... | collective-permute-start | bytes 245768 | tf_op jit(solution)/shard_map/ppermute | solution.py:26
  91.1 2.3 %copy-start.1 = (f32[2176,544]{0,1:T(8,128)S(1)}, f32[2176,544]{0,1:T(8,128)}, u32[]{:S(2)}) copy-start(f32[2176,544]{0,1:T(8,128)} %param.6) | copy-start | bytes 14204932
  103.9 17.5 %all-to-all-start.2 = ((f32[8,24,1088]{2,1,0:T(8,128)}), f32[8,24,1088]{2,1,0:T(8,128)S(1)}, u32[]{:S(2)}, u32[]{:S(2)}) async-start(f32[8,24,1088]{2,1,0:T(8,128)} %bitcast.8), calls=%async_computation.2 | async-start | bytes 1769472 | tf_op jit(solution)/shard_map/all_to_all | solution.py:34
  111.2 4.2 %collective-permute-start.14 = (f32[64,640]{1,0:T(8,128)S(1)}, f32[64,640]{1,0:T(8,128)S(1)}, u32[]{:S(2)}, u32[]{:S(2)}) collective-permute-start(f32[64,640]{1,0:T(8,128)S(1)} %pair.1.refs_0_), channel_id=1, source_target_pairs={{0,112},{16,0},{32,16},{48,32},{64,48},{80,64},{96,80},{112,96},{1... | collective-permute-start | bytes 491528 | tf_op jit(solution)/shard_map/ppermute | solution.py:26
  111.2 5.4 %collective-permute-start.13 = (f32[64,640]{1,0:T(8,128)S(1)}, f32[64,640]{1,0:T(8,128)S(1)}, u32[]{:S(2)}, u32[]{:S(2)}) collective-permute-start(f32[64,640]{1,0:T(8,128)S(1)} %pair.1.refs_0_), channel_id=1, source_target_pairs={{0,16},{16,32},{32,48},{48,64},{64,80},{80,96},{96,112},{112,0},{1... | collective-permute-start | bytes 491528 | tf_op jit(solution)/shard_map/ppermute | solution.py:26
  121.6 1.4 copy-start.2
  123.0 35.8 %all-to-all-start.3 = ((f32[8,64,1088]{2,1,0:T(8,128)}), f32[8,64,1088]{2,1,0:T(8,128)S(1)}, u32[]{:S(2)}, u32[]{:S(2)}) async-start(f32[8,64,1088]{2,1,0:T(8,128)} %copy-done.2), calls=%async_computation.3 | async-start | bytes 4718592 | tf_op jit(solution)/shard_map/all_to_all | solution.py:34
  129.9 30.2 %copy-start.10 = (s32[1024]{0:T(1024)S(1)}, s32[1024]{0:T(1024)}, u32[]{:S(2)}) copy-start(s32[1024]{0:T(1024)} %param.9) | copy-start | bytes 12292
  129.9 5.7 %collective-permute-start.15 = (f32[64,640]{1,0:T(8,128)S(1)}, f32[64,640]{1,0:T(8,128)S(1)}, u32[]{:S(2)}, u32[]{:S(2)}) collective-permute-start(f32[64,640]{1,0:T(8,128)S(1)} %collective-permute-done.13.refs_1_), channel_id=1, source_target_pairs={{0,16},{16,32},{32,48},{48,64},{64,80},{80,96},{96,112},{112,0},{1... | collective-permute-start | bytes 491528 | tf_op jit(solution)/shard_map/ppermute | solution.py:26
  130.3 5.4 %collective-permute-start.16 = (f32[64,640]{1,0:T(8,128)S(1)}, f32[64,640]{1,0:T(8,128)S(1)}, u32[]{:S(2)}, u32[]{:S(2)}) collective-permute-start(f32[64,640]{1,0:T(8,128)S(1)} %collective-permute-done.14.refs_2_), channel_id=1, source_target_pairs={{0,112},{16,0},{32,16},{48,32},{64,48},{80,64},{96,80},{112,96},{1... | collective-permute-start | bytes 491528 | tf_op jit(solution)/shard_map/ppermute | solution.py:26
  135.6 5.7 %collective-permute-start.17 = (f32[64,640]{1,0:T(8,128)S(1)}, f32[64,640]{1,0:T(8,128)S(1)}, u32[]{:S(2)}, u32[]{:S(2)}) collective-permute-start(f32[64,640]{1,0:T(8,128)S(1)} %collective-permute-done.15.refs_3_), channel_id=1, source_target_pairs={{0,16},{16,32},{32,48},{48,64},{64,80},{80,96},{96,112},{112,0},{1... | collective-permute-start | bytes 491528 | tf_op jit(solution)/shard_map/ppermute | solution.py:26
  135.6 5.7 %collective-permute-start.18 = (f32[64,640]{1,0:T(8,128)S(1)}, f32[64,640]{1,0:T(8,128)S(1)}, u32[]{:S(2)}, u32[]{:S(2)}) collective-permute-start(f32[64,640]{1,0:T(8,128)S(1)} %collective-permute-done.16.refs_4_), channel_id=1, source_target_pairs={{0,112},{16,0},{32,16},{48,32},{64,48},{80,64},{96,80},{112,96},{1... | collective-permute-start | bytes 491528 | tf_op jit(solution)/shard_map/ppermute | solution.py:26
  141.3 5.7 %collective-permute-start.19 = (f32[64,640]{1,0:T(8,128)S(1)}, f32[64,640]{1,0:T(8,128)S(1)}, u32[]{:S(2)}, u32[]{:S(2)}) collective-permute-start(f32[64,640]{1,0:T(8,128)S(1)} %collective-permute-done.17.refs_5_), channel_id=1, source_target_pairs={{0,16},{16,32},{32,48},{48,64},{64,80},{80,96},{96,112},{112,0},{1... | collective-permute-start | bytes 491528 | tf_op jit(solution)/shard_map/ppermute | solution.py:26
  147.6 7.6 %collective-permute-start.20 = (f32[512,640]{1,0:T(8,128)S(1)}, f32[512,640]{1,0:T(8,128)S(1)}, u32[]{:S(2)}, u32[]{:S(2)}) collective-permute-start(f32[512,640]{1,0:T(8,128)S(1)} %place.1.own), channel_id=1, source_target_pairs={{0,8},{8,0},{1,9},{9,1},{2,10},{10,2},{3,11},{11,3},{4,12},{12,4},... | collective-permute-start | bytes 3932168 | tf_op jit(solution)/shard_map/ppermute | solution.py:26
  152.6 1.1 copy-start.3
  155.2 1.1 copy-start.5
  158.9 5.4 %collective-permute-start.21 = (f32[8,64,1088]{2,1,0:T(8,128)S(1)}, f32[8,64,1088]{2,1,0:T(8,128)S(1)}, u32[]{:S(2)}, u32[]{:S(2)}) collective-permute-start(f32[8,64,1088]{2,1,0:T(8,128)S(1)} %all-to-all-done.3.refs_0_), channel_id=1, source_target_pairs={{0,8},{8,0},{1,9},{9,1},{2,10},{10,2},{3,11},{11,3},{4,12},{12,4},... | collective-permute-start | bytes 6684680 | tf_op jit(solution)/shard_map/ppermute | solution.py:26
  160.2 1.3 copy-start.4
  161.6 1.3 copy-start.6

commit v7 on v6

--- a/solution.py
+++ b/solution.py
@@ -62,17 +62,24 @@
 
 def basis_kernel(own, other, out):
     rows = own.shape[0]
-    for at, ref in enumerate((own, other)):
-        into = slice(at * rows, (at + 1) * rows)
+    half = out.shape[1] // 2
+    for base, ref in ((0, own), (half, other)):
+        start = pl.multiple_of(base + pl.program_id(0) * rows, 16)
+        into = pl.ds(start, rows)
         out[0, into, :], out[1, into, :] = halved(ref[...])
 
 
 def split_basis(own, other):
     rows, depth = own.shape
-    return call(
+    block = pl.BlockSpec((rows // 2, depth), lambda step: (step, 0))
+    return pl.pallas_call(
         basis_kernel,
-        pltpu.VMEM((2, 2 * rows, depth), jnp.bfloat16),
-        [VMEM, VMEM],
+        grid=(2,),
+        out_shape=pltpu.VMEM((2, 2 * rows, depth), jnp.bfloat16),
+        in_specs=[block, block],
+        out_specs=VMEM,
+        compiler_params=pltpu.CompilerParams(vmem_limit_bytes=50 << 20),
+        cost_estimate=pl.CostEstimate(flops=1000, bytes_accessed=1000, transcendentals=0),
         name="split_basis",
     )(own, other)
 

time: 172 us -> 174 us (1.012)
  local copies, waits for them, and re-layouts: 14.9 us -> 10.3 us
  waiting for transfers between devices: 62.6 us -> 65.9 us
  Pallas kernels: 34.9 us -> 38 us
    unnamed x23 -> x19, local copies, waits for them, and re-layouts: 13 us -> 8.28 us
    ppermute x22, waiting for transfers between devices: 55.2 us -> 57.8 us  [shifted(): return lax.ppermute(value, axis, [(i, (i + by) % n) for i in range(n)])]
  transfers between devices with their start and end apart: 26 -> 26, of which waited for: 14 -> 16; matrix products, arithmetic and copies ran while one was open for 1% -> 1% of each run, Pallas kernels for 16% -> 17%
where the time goes in v7:
time: 174 us; the launch traced here: 173 us
  waiting for transfers between devices  65.9 us (38%)
  starting transfers between devices  58.9 us (34%)
  Pallas kernels  38 us (22%)
  local copies, waits for them, and re-layouts  10.3 us (6%)
    ppermute x22, waiting for transfers between devices, shifted(): return lax.ppermute(value, axis, [(i, (i + by) % n) for i in range(n)])  57.8 us
    ppermute x22, starting transfers between devices, shifted(): return lax.ppermute(value, axis, [(i, (i + by) % n) for i in range(n)])  30.7 us
    all_to_all x4, starting transfers between devices, swapped(): return lax.all_to_all(value, axes, 0, 0)  28.2 us
    pallas_call x2, Pallas kernels, products(): call(products_kernel, f32(rows, cols), [VMEM] * (1 + len(blocks)), [pltpu...  14.1 us
    pallas_call x2, Pallas kernels, split_basis(): pl.pallas_call(basis_kernel, grid=(2,), out_shape=pltpu.VMEM((2, 2 * rows...  8.98 us
    pallas_call x1, Pallas kernels, eigenvalues(): call(moments_kernel, f32(cols, out_cols), [SMEM, SMEM] + [VMEM] * (len(ac...  8.94 us
    unnamed x19, local copies, waits for them, and re-layouts  8.28 us
    all_to_all x4, waiting for transfers between devices, swapped(): return lax.all_to_all(value, axes, 0, 0)  8.09 us
  transfers between devices with their start and end apart: 26, of which 16 were waited for; matrix products, arithmetic and copies ran while one was open for 1% of the time, Pallas kernels for 17%

profile of v7, /device:TPU:1, one launch (start us, length us, event | category | flops | bytes accessed | tf_op | source)
XLA Modules:
  0.0 173.5 jit_solution(7899036301769374285)
XLA Ops:
  0.0 3.2 %collective-permute-start.5 = (f32[2176,544]{0,1:T(8,128)}, f32[2176,544]{0,1:T(8,128)}, u32[]{:S(2)}, u32[]{:S(2)}) collective-permute-start(f32[2176,544]{0,1:T(8,128)} %param.6), channel_id=1, source_target_pairs={{0,8},{8,0},{1,9},{9,1},{2,10},{10,2},{3,11},{11,3},{4,12},{12,4},... | collective-permute-start | bytes 14204936 | tf_op jit(solution)/shard_map/ppermute | solution.py:26
  3.3 1.1 copy-done.5
  4.4 1.0 copy-done.6
  5.4 2.0 %rotate_grads.1 = (f32[512,640]{1,0:T(8,128)S(1)}, f32[512,640]{1,0:T(8,128)S(1)}) custom-call(s32[3]{0:T(128)S(1)} %pad_add_fusion.place, f32[160,1024]{1,0:T(8,128)S(1)} %bitcast.9, f32[160,640]{1,0:T(8,128)S(1)} %copy-done.6), custom_call_target="tpu_custom_call" | custom-call | flops 1000 | bytes 1000 | tf_op jit(solution)/shard_map/rotate_grads/pallas_call | solution.py:304
  7.4 4.3 %collective-permute-done = f32[32,2176]{1,0:T(8,128)S(1)} collective-permute-done((f32[32,2176]{1,0:T(8,128)}, f32[32,2176]{1,0:T(8,128)S(1)}, u32[]{:S(2)}, u32[]{:S(2)}) %collective-permute-start) | collective-permute-done | bytes 278560 | tf_op jit(solution)/shard_map/ppermute | solution.py:26
  11.7 0.8 collective-permute-start.6
  12.5 2.7 %collective-permute-done.6.arrived = f32[512,640]{1,0:T(8,128)S(1)} collective-permute-done((f32[512,640]{1,0:T(8,128)S(1)}, f32[512,640]{1,0:T(8,128)S(1)}, u32[]{:S(2)}, u32[]{:S(2)}) %collective-permute-start.6) | collective-permute-done | bytes 1310752 | tf_op jit(solution)/shard_map/ppermute | solution.py:26
  15.2 0.7 add_halves.1
  16.1 5.1 %collective-permute-start.2 = (f32[64,2176]{1,0:T(8,128)S(1)}, f32[64,2176]{1,0:T(8,128)S(1)}, u32[]{:S(2)}, u32[]{:S(2)}) collective-permute-start(f32[64,2176]{1,0:T(8,128)S(1)} %constant_dynamic-update-slice_fusion.refs_0_), channel_id=1, source_target_pairs={{0,112},{16,0},{32,16},{48,32},{64,48},{80,64},{96,80},{112,96},{1... | collective-permute-start | bytes 1671176 | tf_op jit(solution)/shard_map/ppermute | solution.py:26
  21.2 10.8 %collective-permute-done.7.b = f32[256,640]{1,0:T(8,128)S(1)} collective-permute-done((f32[256,640]{1,0:T(8,128)S(1)}, f32[256,640]{1,0:T(8,128)S(1)}, u32[]{:S(2)}, u32[]{:S(2)}) %collective-permute-start.7) | collective-permute-done | bytes 655392 | tf_op jit(solution)/shard_map/ppermute | solution.py:26
  32.0 0.9 add.5
  32.9 6.5 %all-to-all-start = ((f32[8,32,640]{2,1,0:T(8,128)}), f32[8,32,640]{2,1,0:T(8,128)S(1)}, u32[]{:S(2)}, u32[]{:S(2)}) async-start(f32[8,32,640]{2,1,0:T(8,128)} %bitcast.6), calls=%async_computation | async-start | bytes 1310720 | tf_op jit(solution)/shard_map/all_to_all | solution.py:34
  39.3 2.7 %collective-permute-start.4 = (f32[64,2176]{1,0:T(8,128)S(1)}, f32[64,2176]{1,0:T(8,128)S(1)}, u32[]{:S(2)}, u32[]{:S(2)}) collective-permute-start(f32[64,2176]{1,0:T(8,128)S(1)} %collective-permute-done.2.refs_2_), channel_id=1, source_target_pairs={{0,112},{16,0},{32,16},{48,32},{64,48},{80,64},{96,80},{112,96},{1... | collective-permute-start | bytes 1671176 | tf_op jit(solution)/shard_map/ppermute | solution.py:26
  42.0 4.5 %split_basis.2.refs_5_ = bf16[2,1088,2176]{2,1,0:T(8,128)(2,1)S(1)} custom-call(f32[544,2176]{1,0:T(8,128)} %bitcast.10, f32[544,2176]{1,0:T(8,128)} %bitcast.5.other), custom_call_target="tpu_custom_call" | custom-call | flops 1000 | bytes 1000 | tf_op jit(solution)/shard_map/split_basis/pallas_call | solution.py:75
  46.5 19.9 %collective-permute-done.4.refs_4_ = f32[64,2176]{1,0:T(8,128)S(1)} collective-permute-done((f32[64,2176]{1,0:T(8,128)S(1)}, f32[64,2176]{1,0:T(8,128)S(1)}, u32[]{:S(2)}, u32[]{:S(2)}) %collective-permute-start.4) | collective-permute-done | bytes 557088 | tf_op jit(solution)/shard_map/ppermute | solution.py:26
  66.4 2.1 %collective-permute-done.3.refs_3_ = f32[64,2176]{1,0:T(8,128)} collective-permute-done((f32[64,2176]{1,0:T(8,128)S(1)}, f32[64,2176]{1,0:T(8,128)}, u32[]{:S(2)}, u32[]{:S(2)}) %collective-permute-start.3) | collective-permute-done | bytes 557088 | tf_op jit(solution)/shard_map/ppermute | solution.py:26
  68.5 2.7 %collective-permute-start.10 = (f32[64,2176]{1,0:T(8,128)S(1)}, f32[64,2176]{1,0:T(8,128)}, u32[]{:S(2)}, u32[]{:S(2)}) collective-permute-start(f32[64,2176]{1,0:T(8,128)S(1)} %collective-permute-done.4.refs_4_), channel_id=1, source_target_pairs={{0,112},{16,0},{32,16},{48,32},{64,48},{80,64},{96,80},{112,96},{1... | collective-permute-start | bytes 1671176 | tf_op jit(solution)/shard_map/ppermute | solution.py:26
  71.1 8.1 %products.2 = f32[320,1088]{1,0:T(8,128)} custom-call(f32[64,2176]{1,0:T(8,128)S(1)} %constant_dynamic-update-slice_fusion.refs_0_, f32[64,2176]{1,0:T(8,128)S(1)} %collective-permute-done.1.refs_1_, f32[64,2176]{1,0:T(8,128)S(1)} %collective-permute-done.2.refs_2_, f32[64,2176]{1,0:T(8,128)} %collective-permute-done.3.refs_3_, ...), custom_call_target="tpu_custom_call" | custom-call | flops 1000 | bytes 1000 | tf_op jit(solution)/shard_map/products/pallas_call | solution.py:108
  79.2 6.7 %all-to-all-start.1 = ((f32[8,40,1088]{2,1,0:T(8,128)}), f32[8,40,1088]{2,1,0:T(8,128)S(1)}, u32[]{:S(2)}, u32[]{:S(2)}) async-start(f32[8,40,1088]{2,1,0:T(8,128)} %bitcast.7), calls=%async_computation.1 | async-start | bytes 2949120 | tf_op jit(solution)/shard_map/all_to_all | solution.py:34
  85.9 1.0 slice.8
  87.0 1.0 slice.9
  87.9 2.7 %collective-permute-start.12 = (f32[32,2176]{1,0:T(8,128)S(1)}, f32[32,2176]{1,0:T(8,128)S(1)}, u32[]{:S(2)}, u32[]{:S(2)}) collective-permute-start(f32[32,2176]{1,0:T(8,128)S(1)} %slice.9), channel_id=1, source_target_pairs={{0,112},{16,0},{32,16},{48,32},{64,48},{80,64},{96,80},{112,96},{1... | collective-permute-start | bytes 835592 | tf_op jit(solution)/shard_map/ppermute | solution.py:26
  91.1 4.5 %split_basis.3.refs_4_ = bf16[2,1088,2176]{2,1,0:T(8,128)(2,1)S(1)} custom-call(f32[544,2176]{1,0:T(8,128)} %bitcast.11, f32[544,2176]{1,0:T(8,128)} %bitcast.5.other), custom_call_target="tpu_custom_call" | custom-call | flops 1000 | bytes 1000 | tf_op jit(solution)/shard_map/split_basis/pallas_call | solution.py:75
  95.6 6.1 %products.3 = f32[192,1088]{1,0:T(8,128)} custom-call(f32[64,2176]{1,0:T(8,128)} %collective-permute-done.9.refs_0_, f32[64,2176]{1,0:T(8,128)} %collective-permute-done.10.refs_1_, f32[32,2176]{1,0:T(8,128)S(1)} %collective-permute-done.11.refs_2_, f32[32,2176]{1,0:T(8,128)S(1)} %collective-permute-done.12.refs_3_, ...), custom_call_target="tpu_custom_call" | custom-call | flops 5000000000 | bytes 1000 | tf_op jit(solution)/shard_map/products/pallas_call | solution.py:108
  101.7 1.0 collective-permute-done.8.other
  103.3 7.8 %all-to-all-start.2 = ((f32[8,24,1088]{2,1,0:T(8,128)}), f32[8,24,1088]{2,1,0:T(8,128)S(1)}, u32[]{:S(2)}, u32[]{:S(2)}) async-start(f32[8,24,1088]{2,1,0:T(8,128)} %bitcast.8), calls=%async_computation.2 | async-start | bytes 1769472 | tf_op jit(solution)/shard_map/all_to_all | solution.py:34
  111.1 1.4 collective-permute-start.13
  112.5 2.7 %collective-permute-done.14.refs_2_ = f32[64,640]{1,0:T(8,128)S(1)} collective-permute-done((f32[64,640]{1,0:T(8,128)S(1)}, f32[64,640]{1,0:T(8,128)S(1)}, u32[]{:S(2)}, u32[]{:S(2)}) %collective-permute-start.14) | collective-permute-done | bytes 163872 | tf_op jit(solution)/shard_map/ppermute | solution.py:26
  115.2 1.3 collective-permute-done.13.refs_1_
  116.5 4.8 %all-to-all-done.2.refs_1_ = f32[8,24,1088]{2,1,0:T(8,128)S(1)} async-done(((f32[8,24,1088]{2,1,0:T(8,128)}), f32[8,24,1088]{2,1,0:T(8,128)S(1)}, u32[]{:S(2)}, u32[]{:S(2)}) %all-to-all-start.2) | async-done | bytes 835616 | tf_op jit(solution)/shard_map/all_to_all | solution.py:34
  121.5 1.4 copy-done
  122.9 7.3 %all-to-all-start.3 = ((f32[8,64,1088]{2,1,0:T(8,128)}), f32[8,64,1088]{2,1,0:T(8,128)S(1)}, u32[]{:S(2)}, u32[]{:S(2)}) async-start(f32[8,64,1088]{2,1,0:T(8,128)} %copy-done), calls=%async_computation.3 | async-start | bytes 4718592 | tf_op jit(solution)/shard_map/all_to_all | solution.py:34
  130.3 2.7 %collective-permute-start.16 = (f32[64,640]{1,0:T(8,128)S(1)}, f32[64,640]{1,0:T(8,128)S(1)}, u32[]{:S(2)}, u32[]{:S(2)}) collective-permute-start(f32[64,640]{1,0:T(8,128)S(1)} %collective-permute-done.14.refs_2_), channel_id=1, source_target_pairs={{0,112},{16,0},{32,16},{48,32},{64,48},{80,64},{96,80},{112,96},{1... | collective-permute-start | bytes 491528 | tf_op jit(solution)/shard_map/ppermute | solution.py:26
  133.0 2.7 %collective-permute-done.15.refs_3_ = f32[64,640]{1,0:T(8,128)S(1)} collective-permute-done((f32[64,640]{1,0:T(8,128)S(1)}, f32[64,640]{1,0:T(8,128)S(1)}, u32[]{:S(2)}, u32[]{:S(2)}) %collective-permute-start.15) | collective-permute-done | bytes 163872 | tf_op jit(solution)/shard_map/ppermute | solution.py:26
  135.7 3.0 %collective-permute-start.18 = (f32[64,640]{1,0:T(8,128)S(1)}, f32[64,640]{1,0:T(8,128)S(1)}, u32[]{:S(2)}, u32[]{:S(2)}) collective-permute-start(f32[64,640]{1,0:T(8,128)S(1)} %collective-permute-done.16.refs_4_), channel_id=1, source_target_pairs={{0,112},{16,0},{32,16},{48,32},{64,48},{80,64},{96,80},{112,96},{1... | collective-permute-start | bytes 491528 | tf_op jit(solution)/shard_map/ppermute | solution.py:26
  138.6 2.7 %collective-permute-done.17.refs_5_ = f32[64,640]{1,0:T(8,128)S(1)} collective-permute-done((f32[64,640]{1,0:T(8,128)S(1)}, f32[64,640]{1,0:T(8,128)S(1)}, u32[]{:S(2)}, u32[]{:S(2)}) %collective-permute-start.17) | collective-permute-done | bytes 163872 | tf_op jit(solution)/shard_map/ppermute | solution.py:26
  141.4 5.7 %collective-permute-done.19.refs_7_ = f32[64,640]{1,0:T(8,128)S(1)} collective-permute-done((f32[64,640]{1,0:T(8,128)S(1)}, f32[64,640]{1,0:T(8,128)S(1)}, u32[]{:S(2)}, u32[]{:S(2)}) %collective-permute-start.19) | collective-permute-done | bytes 163872 | tf_op jit(solution)/shard_map/ppermute | solution.py:26
  147.0 0.6 place.1.own
  147.7 4.5 %collective-permute-start.20 = (f32[512,640]{1,0:T(8,128)S(1)}, f32[512,640]{1,0:T(8,128)S(1)}, u32[]{:S(2)}, u32[]{:S(2)}) collective-permute-start(f32[512,640]{1,0:T(8,128)S(1)} %place.1.own), channel_id=1, source_target_pairs={{0,8},{8,0},{1,9},{9,1},{2,10},{10,2},{3,11},{11,3},{4,12},{12,4},... | collective-permute-start | bytes 3932168 | tf_op jit(solution)/shard_map/ppermute | solution.py:26
  152.2 1.1 copy-done.1
  153.3 1.6 collective-permute-done.20.other
  154.9 1.1 copy-done.3
  155.9 3.2 %all-to-all-done.3.refs_0_ = f32[8,64,1088]{2,1,0:T(8,128)S(1)} async-done(((f32[8,64,1088]{2,1,0:T(8,128)}), f32[8,64,1088]{2,1,0:T(8,128)S(1)}, u32[]{:S(2)}, u32[]{:S(2)}) %all-to-all-start.3) | async-done | bytes 2228256 | tf_op jit(solution)/shard_map/all_to_all | solution.py:34
  159.2 1.2 collective-permute-start.21
  160.5 1.3 copy-done.2
  161.8 1.3 copy-done.4
  163.1 1.0 split_grads.1
  164.6 8.9 %moments.1 = f32[544,640]{1,0:T(8,128)} custom-call(s32[3]{0:T(128)S(1)} %pad_add_fusion.place, s32[5]{0:T(128)S(1)} %convert_reduce_fusion.bounds, f32[8,64,1088]{2,1,0:T(8,128)S(1)} %all-to-all-done.3.refs_0_, f32[8,64,1088]{2,1,0:T(8,128)S(1)} %collective-permute-done.21.refs_1_, bf16[1280,640]{1,0:T(8,128)(2,1)S(1)} %get-tuple-element.67.refs_2_, ...), custom_call_target="tpu_custom_call" | custom-call | flops 1000 | bytes 1000 | tf_op jit(solution)/shard_map/moments/pallas_call | solution.py:278
  (41 shorter events, 2.2 us)
Async XLA Ops:
  0.0 42.0 %collective-permute-start.5 = (f32[2176,544]{0,1:T(8,128)}, f32[2176,544]{0,1:T(8,128)}, u32[]{:S(2)}, u32[]{:S(2)}) collective-permute-start(f32[2176,544]{0,1:T(8,128)} %param.6), channel_id=1, source_target_pairs={{0,8},{8,0},{1,9},{9,1},{2,10},{10,2},{3,11},{11,3},{4,12},{12,4},... | collective-permute-start | bytes 14204936 | tf_op jit(solution)/shard_map/ppermute | solution.py:26
  3.2 8.5 %collective-permute-start = (f32[32,2176]{1,0:T(8,128)}, f32[32,2176]{1,0:T(8,128)S(1)}, u32[]{:S(2)}, u32[]{:S(2)}) collective-permute-start(f32[32,2176]{1,0:T(8,128)} %param.5), channel_id=1, source_target_pairs={{0,128},{128,0},{1,129},{129,1},{2,130},{130,2},{3,131},{131,3},{4... | collective-permute-start | bytes 835592 | tf_op jit(solution)/shard_map/ppermute | solution.py:26
  3.3 1.1 copy-start.5
  4.4 1.0 copy-start.6
  5.4 10.6 %copy-start.7 = (f32[32,2176]{1,0:T(8,128)S(1)}, f32[32,2176]{1,0:T(8,128)}, u32[]{:S(2)}) copy-start(f32[32,2176]{1,0:T(8,128)} %param.5) | copy-start | bytes 835588
  11.7 3.4 %collective-permute-start.6 = (f32[512,640]{1,0:T(8,128)S(1)}, f32[512,640]{1,0:T(8,128)S(1)}, u32[]{:S(2)}, u32[]{:S(2)}) collective-permute-start(f32[512,640]{1,0:T(8,128)S(1)} %get-tuple-element.46), channel_id=1, source_target_pairs={{0,8},{8,0},{1,9},{9,1},{2,10},{10,2},{3,11},{11,3},{4,12},{12,4},... | collective-permute-start | bytes 3932168 | tf_op jit(solution)/shard_map/ppermute | solution.py:26
  15.9 16.0 %collective-permute-start.7 = (f32[256,640]{1,0:T(8,128)S(1)}, f32[256,640]{1,0:T(8,128)S(1)}, u32[]{:S(2)}, u32[]{:S(2)}) collective-permute-start(f32[256,640]{1,0:T(8,128)S(1)} %get-tuple-element.48), channel_id=1, source_target_pairs={{0,128},{128,0},{1,129},{129,1},{2,130},{130,2},{3,131},{131,3},{4... | collective-permute-start | bytes 1966088 | tf_op jit(solution)/shard_map/ppermute | solution.py:26
  16.1 23.2 %collective-permute-start.2 = (f32[64,2176]{1,0:T(8,128)S(1)}, f32[64,2176]{1,0:T(8,128)S(1)}, u32[]{:S(2)}, u32[]{:S(2)}) collective-permute-start(f32[64,2176]{1,0:T(8,128)S(1)} %constant_dynamic-update-slice_fusion.refs_0_), channel_id=1, source_target_pairs={{0,112},{16,0},{32,16},{48,32},{64,48},{80,64},{96,80},{112,96},{1... | collective-permute-start | bytes 1671176 | tf_op jit(solution)/shard_map/ppermute | solution.py:26
  21.2 20.8 %collective-permute-start.1 = (f32[64,2176]{1,0:T(8,128)S(1)}, f32[64,2176]{1,0:T(8,128)S(1)}, u32[]{:S(2)}, u32[]{:S(2)}) collective-permute-start(f32[64,2176]{1,0:T(8,128)S(1)} %constant_dynamic-update-slice_fusion.refs_0_), channel_id=1, source_target_pairs={{0,16},{16,32},{32,48},{48,64},{64,80},{80,96},{96,112},{112,0},{1... | collective-permute-start | bytes 1671176 | tf_op jit(solution)/shard_map/ppermute | solution.py:26
  32.9 46.4 %all-to-all-start = ((f32[8,32,640]{2,1,0:T(8,128)}), f32[8,32,640]{2,1,0:T(8,128)S(1)}, u32[]{:S(2)}, u32[]{:S(2)}) async-start(f32[8,32,640]{2,1,0:T(8,128)} %bitcast.6), calls=%async_computation | async-start | bytes 1310720 | tf_op jit(solution)/shard_map/all_to_all | solution.py:34
  39.3 27.1 %collective-permute-start.4 = (f32[64,2176]{1,0:T(8,128)S(1)}, f32[64,2176]{1,0:T(8,128)S(1)}, u32[]{:S(2)}, u32[]{:S(2)}) collective-permute-start(f32[64,2176]{1,0:T(8,128)S(1)} %collective-permute-done.2.refs_2_), channel_id=1, source_target_pairs={{0,112},{16,0},{32,16},{48,32},{64,48},{80,64},{96,80},{112,96},{1... | collective-permute-start | bytes 1671176 | tf_op jit(solution)/shard_map/ppermute | solution.py:26
  42.0 26.5 %collective-permute-start.3 = (f32[64,2176]{1,0:T(8,128)S(1)}, f32[64,2176]{1,0:T(8,128)}, u32[]{:S(2)}, u32[]{:S(2)}) collective-permute-start(f32[64,2176]{1,0:T(8,128)S(1)} %collective-permute-done.1.refs_1_), channel_id=1, source_target_pairs={{0,16},{16,32},{32,48},{48,64},{64,80},{80,96},{96,112},{112,0},{1... | collective-permute-start | bytes 1671176 | tf_op jit(solution)/shard_map/ppermute | solution.py:26
  68.5 17.4 %collective-permute-start.9 = (f32[64,2176]{1,0:T(8,128)}, f32[64,2176]{1,0:T(8,128)}, u32[]{:S(2)}, u32[]{:S(2)}) collective-permute-start(f32[64,2176]{1,0:T(8,128)} %collective-permute-done.3.refs_3_), channel_id=1, source_target_pairs={{0,16},{16,32},{32,48},{48,64},{64,80},{80,96},{96,112},{112,0},{1... | collective-permute-start | bytes 1671176 | tf_op jit(solution)/shard_map/ppermute | solution.py:26
  68.5 18.5 %collective-permute-start.10 = (f32[64,2176]{1,0:T(8,128)S(1)}, f32[64,2176]{1,0:T(8,128)}, u32[]{:S(2)}, u32[]{:S(2)}) collective-permute-start(f32[64,2176]{1,0:T(8,128)S(1)} %collective-permute-done.4.refs_4_), channel_id=1, source_target_pairs={{0,112},{16,0},{32,16},{48,32},{64,48},{80,64},{96,80},{112,96},{1... | collective-permute-start | bytes 1671176 | tf_op jit(solution)/shard_map/ppermute | solution.py:26
  79.2 24.0 %all-to-all-start.1 = ((f32[8,40,1088]{2,1,0:T(8,128)}), f32[8,40,1088]{2,1,0:T(8,128)S(1)}, u32[]{:S(2)}, u32[]{:S(2)}) async-start(f32[8,40,1088]{2,1,0:T(8,128)} %bitcast.7), calls=%async_computation.1 | async-start | bytes 2949120 | tf_op jit(solution)/shard_map/all_to_all | solution.py:34
  86.9 8.7 %collective-permute-start.11 = (f32[32,2176]{1,0:T(8,128)S(1)}, f32[32,2176]{1,0:T(8,128)S(1)}, u32[]{:S(2)}, u32[]{:S(2)}) collective-permute-start(f32[32,2176]{1,0:T(8,128)S(1)} %slice.8), channel_id=1, source_target_pairs={{0,16},{16,32},{32,48},{48,64},{64,80},{80,96},{96,112},{112,0},{1... | collective-permute-start | bytes 835592 | tf_op jit(solution)/shard_map/ppermute | solution.py:26
  87.9 7.7 %collective-permute-start.12 = (f32[32,2176]{1,0:T(8,128)S(1)}, f32[32,2176]{1,0:T(8,128)S(1)}, u32[]{:S(2)}, u32[]{:S(2)}) collective-permute-start(f32[32,2176]{1,0:T(8,128)S(1)} %slice.9), channel_id=1, source_target_pairs={{0,112},{16,0},{32,16},{48,32},{64,48},{80,64},{96,80},{112,96},{1... | collective-permute-start | bytes 835592 | tf_op jit(solution)/shard_map/ppermute | solution.py:26
  90.7 11.9 %collective-permute-start.8 = (f32[1,32,640]{2,1,0:T(8,128)S(1)}, f32[1,32,640]{2,1,0:T(8,128)S(1)}, u32[]{:S(2)}, u32[]{:S(2)}) collective-permute-start(f32[1,32,640]{2,1,0:T(8,128)S(1)} %sum_copies.2.own), channel_id=1, source_target_pairs={{0,128},{128,0},{1,129},{129,1},{2,130},{130,2},{3,131},{131,3},{4... | collective-permute-start | bytes 245768 | tf_op jit(solution)/shard_map/ppermute | solution.py:26
  103.3 18.1 %all-to-all-start.2 = ((f32[8,24,1088]{2,1,0:T(8,128)}), f32[8,24,1088]{2,1,0:T(8,128)S(1)}, u32[]{:S(2)}, u32[]{:S(2)}) async-start(f32[8,24,1088]{2,1,0:T(8,128)} %bitcast.8), calls=%async_computation.2 | async-start | bytes 1769472 | tf_op jit(solution)/shard_map/all_to_all | solution.py:34
  111.0 4.2 %collective-permute-start.14 = (f32[64,640]{1,0:T(8,128)S(1)}, f32[64,640]{1,0:T(8,128)S(1)}, u32[]{:S(2)}, u32[]{:S(2)}) collective-permute-start(f32[64,640]{1,0:T(8,128)S(1)} %pair.1.refs_0_), channel_id=1, source_target_pairs={{0,112},{16,0},{32,16},{48,32},{64,48},{80,64},{96,80},{112,96},{1... | collective-permute-start | bytes 491528 | tf_op jit(solution)/shard_map/ppermute | solution.py:26
  111.1 5.4 %collective-permute-start.13 = (f32[64,640]{1,0:T(8,128)S(1)}, f32[64,640]{1,0:T(8,128)S(1)}, u32[]{:S(2)}, u32[]{:S(2)}) collective-permute-start(f32[64,640]{1,0:T(8,128)S(1)} %pair.1.refs_0_), channel_id=1, source_target_pairs={{0,16},{16,32},{32,48},{48,64},{64,80},{80,96},{96,112},{112,0},{1... | collective-permute-start | bytes 491528 | tf_op jit(solution)/shard_map/ppermute | solution.py:26
  121.5 1.4 copy-start
  122.9 36.2 %all-to-all-start.3 = ((f32[8,64,1088]{2,1,0:T(8,128)}), f32[8,64,1088]{2,1,0:T(8,128)S(1)}, u32[]{:S(2)}, u32[]{:S(2)}) async-start(f32[8,64,1088]{2,1,0:T(8,128)} %copy-done), calls=%async_computation.3 | async-start | bytes 4718592 | tf_op jit(solution)/shard_map/all_to_all | solution.py:34
  130.2 30.2 %copy-start.8 = (s32[1024]{0:T(1024)S(1)}, s32[1024]{0:T(1024)}, u32[]{:S(2)}) copy-start(s32[1024]{0:T(1024)} %param.9) | copy-start | bytes 12292
  130.2 5.5 %collective-permute-start.15 = (f32[64,640]{1,0:T(8,128)S(1)}, f32[64,640]{1,0:T(8,128)S(1)}, u32[]{:S(2)}, u32[]{:S(2)}) collective-permute-start(f32[64,640]{1,0:T(8,128)S(1)} %collective-permute-done.13.refs_1_), channel_id=1, source_target_pairs={{0,16},{16,32},{32,48},{48,64},{64,80},{80,96},{96,112},{112,0},{1... | collective-permute-start | bytes 491528 | tf_op jit(solution)/shard_map/ppermute | solution.py:26
  130.3 5.4 %collective-permute-start.16 = (f32[64,640]{1,0:T(8,128)S(1)}, f32[64,640]{1,0:T(8,128)S(1)}, u32[]{:S(2)}, u32[]{:S(2)}) collective-permute-start(f32[64,640]{1,0:T(8,128)S(1)} %collective-permute-done.14.refs_2_), channel_id=1, source_target_pairs={{0,112},{16,0},{32,16},{48,32},{64,48},{80,64},{96,80},{112,96},{1... | collective-permute-start | bytes 491528 | tf_op jit(solution)/shard_map/ppermute | solution.py:26
  135.7 5.7 %collective-permute-start.17 = (f32[64,640]{1,0:T(8,128)S(1)}, f32[64,640]{1,0:T(8,128)S(1)}, u32[]{:S(2)}, u32[]{:S(2)}) collective-permute-start(f32[64,640]{1,0:T(8,128)S(1)} %collective-permute-done.15.refs_3_), channel_id=1, source_target_pairs={{0,16},{16,32},{32,48},{48,64},{64,80},{80,96},{96,112},{112,0},{1... | collective-permute-start | bytes 491528 | tf_op jit(solution)/shard_map/ppermute | solution.py:26
  135.7 5.7 %collective-permute-start.18 = (f32[64,640]{1,0:T(8,128)S(1)}, f32[64,640]{1,0:T(8,128)S(1)}, u32[]{:S(2)}, u32[]{:S(2)}) collective-permute-start(f32[64,640]{1,0:T(8,128)S(1)} %collective-permute-done.16.refs_4_), channel_id=1, source_target_pairs={{0,112},{16,0},{32,16},{48,32},{64,48},{80,64},{96,80},{112,96},{1... | collective-permute-start | bytes 491528 | tf_op jit(solution)/shard_map/ppermute | solution.py:26
  141.3 5.7 %collective-permute-start.19 = (f32[64,640]{1,0:T(8,128)S(1)}, f32[64,640]{1,0:T(8,128)S(1)}, u32[]{:S(2)}, u32[]{:S(2)}) collective-permute-start(f32[64,640]{1,0:T(8,128)S(1)} %collective-permute-done.17.refs_5_), channel_id=1, source_target_pairs={{0,16},{16,32},{32,48},{48,64},{64,80},{80,96},{96,112},{112,0},{1... | collective-permute-start | bytes 491528 | tf_op jit(solution)/shard_map/ppermute | solution.py:26
  147.7 7.2 %collective-permute-start.20 = (f32[512,640]{1,0:T(8,128)S(1)}, f32[512,640]{1,0:T(8,128)S(1)}, u32[]{:S(2)}, u32[]{:S(2)}) collective-permute-start(f32[512,640]{1,0:T(8,128)S(1)} %place.1.own), channel_id=1, source_target_pairs={{0,8},{8,0},{1,9},{9,1},{2,10},{10,2},{3,11},{11,3},{4,12},{12,4},... | collective-permute-start | bytes 3932168 | tf_op jit(solution)/shard_map/ppermute | solution.py:26
  152.2 1.1 copy-start.1
  154.9 1.1 copy-start.3
  159.2 5.4 %collective-permute-start.21 = (f32[8,64,1088]{2,1,0:T(8,128)S(1)}, f32[8,64,1088]{2,1,0:T(8,128)S(1)}, u32[]{:S(2)}, u32[]{:S(2)}) collective-permute-start(f32[8,64,1088]{2,1,0:T(8,128)S(1)} %all-to-all-done.3.refs_0_), channel_id=1, source_target_pairs={{0,8},{8,0},{1,9},{9,1},{2,10},{10,2},{3,11},{11,3},{4,12},{12,4},... | collective-permute-start | bytes 6684680 | tf_op jit(solution)/shard_map/ppermute | solution.py:26
  160.5 1.3 copy-start.2
  161.8 1.3 copy-start.4

commit v8 on v7

--- a/solution.py
+++ b/solution.py
@@ -84,11 +84,15 @@
     )(own, other)
 
 
-def products_kernel(*refs):
-    *blocks, basis, out, both = refs
-    total = out.shape[0]
+def products_kernel(known, *refs):
+    *inputs, basis, out, both = refs
+    base = 0
+    for ref in inputs[:known]:
+        out[base : base + ref.shape[0], :] = ref[...]
+        base += ref.shape[0]
+    total = out.shape[0] - base
     at = 0
-    for ref in blocks:
+    for ref in inputs[known:]:
         rows = ref.shape[0]
         both[at : at + rows, :], both[total + at : total + at + rows, :] = halved(ref[...])
         at += rows
@@ -99,21 +103,21 @@
         )
 
     main = product(both[...], basis[0])
-    out[...] = main[:total] + (main[total:] + product(both[:total, :], basis[1]))
-
-
-def products(blocks, basis, flops):
+    out[base:, :] = main[:total] + (main[total:] + product(both[:total, :], basis[1]))
+
+
+def products(blocks, basis, flops, earlier=()):
     rows = sum(block.shape[0] for block in blocks)
     _, cols, depth = basis.shape
     return call(
-        products_kernel,
-        f32(rows, cols),
-        [VMEM] * (1 + len(blocks)),
+        functools.partial(products_kernel, len(earlier)),
+        f32(rows + sum(value.shape[0] for value in earlier), cols),
+        [VMEM] * (1 + len(blocks) + len(earlier)),
         [pltpu.VMEM((2 * rows, depth), jnp.bfloat16)],
         name="products",
         mib=16,
         flops=flops,
-    )(*blocks, basis)
+    )(*earlier, *blocks, basis)
 
 
 def sum_kernel(*refs):
@@ -321,9 +325,10 @@
     part_arrived = swapped(in_pieces(part, 8), "z")
     second = [shifted(near[0], "z", 1), shifted(near[1], "z", -1)]
     basis = split_basis(*tied([act_basis.T, other_basis], near[0]))
-    *second, basis = tied([*second, basis])
+    near_products = products([block, *near], basis, 1000)
+    *second, basis, near_products = tied([*second, basis, near_products])
     third = [shifted(second[0], "z", 1), shifted(second[1], "z", -1)]
-    first_products = products([block, *near, *second], basis, 1000)
+    first_products = products(second, basis, 1000, [near_products])
     first_products, part_arrived = tied([first_products, part_arrived])
     first_arrived = swapped(in_pieces(first_products, 8), NARROW)
 

time: 174 us -> 171 us (0.983)
  waiting for transfers between devices: 65.9 us -> 62.8 us
    ppermute x22, waiting for transfers between devices: 57.8 us -> 54.7 us  [shifted(): return lax.ppermute(value, axis, [(i, (i + by) % n) for i in range(n)])]
    pallas_call x2 -> x3, Pallas kernels: 14.1 us -> 15.2 us  [products(): call(functools.partial(products_kernel, len(earlier)), f32(rows + sum((va...]
  transfers between devices with their start and end apart: 26 -> 26, of which waited for: 16 -> 16; matrix products, arithmetic and copies ran while one was open for 1% -> 1% of each run, Pallas kernels for 17% -> 18%
where the time goes in v8:
time: 171 us
  waiting for transfers between devices  62.8 us (37%)
  starting transfers between devices  59.2 us (35%)
  Pallas kernels  39.1 us (23%)
  local copies, waits for them, and re-layouts  9.3 us (5%)
    ppermute x22, waiting for transfers between devices, shifted(): return lax.ppermute(value, axis, [(i, (i + by) % n) for i in range(n)])  54.7 us
    ppermute x22, starting transfers between devices, shifted(): return lax.ppermute(value, axis, [(i, (i + by) % n) for i in range(n)])  31 us
    all_to_all x4, starting transfers between devices, swapped(): return lax.all_to_all(value, axes, 0, 0)  28.2 us
    pallas_call x3, Pallas kernels, products(): call(functools.partial(products_kernel, len(earlier)), f32(rows + sum((va...  15.2 us
    pallas_call x2, Pallas kernels, split_basis(): pl.pallas_call(basis_kernel, grid=(2,), out_shape=pltpu.VMEM((2, 2 * rows...  8.98 us
    pallas_call x1, Pallas kernels, eigenvalues(): call(moments_kernel, f32(cols, out_cols), [SMEM, SMEM] + [VMEM] * (len(ac...  8.95 us
    unnamed x19, local copies, waits for them, and re-layouts  8.28 us
    all_to_all x4, waiting for transfers between devices, swapped(): return lax.all_to_all(value, axes, 0, 0)  8.09 us
  transfers between devices with their start and end apart: 26, of which 16 were waited for; matrix products, arithmetic and copies ran while one was open for 1% of the time, Pallas kernels for 18%

profile of v8, /device:TPU:1, one launch (start us, length us, event | category | flops | bytes accessed | tf_op | source)
XLA Modules:
  0.0 170.8 jit_solution(1189755275694683153)
XLA Ops:
  0.0 3.2 %collective-permute-start.5 = (f32[2176,544]{0,1:T(8,128)}, f32[2176,544]{0,1:T(8,128)}, u32[]{:S(2)}, u32[]{:S(2)}) collective-permute-start(f32[2176,544]{0,1:T(8,128)} %param.6), channel_id=1, source_target_pairs={{0,8},{8,0},{1,9},{9,1},{2,10},{10,2},{3,11},{11,3},{4,12},{12,4},... | collective-permute-start | bytes 14204936 | tf_op jit(solution)/shard_map/ppermute | solution.py:26
  3.3 1.1 copy-done.5
  4.4 1.0 copy-done.6
  5.4 2.0 %rotate_grads.1 = (f32[512,640]{1,0:T(8,128)S(1)}, f32[512,640]{1,0:T(8,128)S(1)}) custom-call(s32[3]{0:T(128)S(1)} %pad_add_fusion.place, f32[160,1024]{1,0:T(8,128)S(1)} %bitcast.9, f32[160,640]{1,0:T(8,128)S(1)} %copy-done.6), custom_call_target="tpu_custom_call" | custom-call | flops 1000 | bytes 1000 | tf_op jit(solution)/shard_map/rotate_grads/pallas_call | solution.py:308
  7.4 4.3 %collective-permute-done = f32[32,2176]{1,0:T(8,128)S(1)} collective-permute-done((f32[32,2176]{1,0:T(8,128)}, f32[32,2176]{1,0:T(8,128)S(1)}, u32[]{:S(2)}, u32[]{:S(2)}) %collective-permute-start) | collective-permute-done | bytes 278560 | tf_op jit(solution)/shard_map/ppermute | solution.py:26
  11.7 0.8 collective-permute-start.6
  12.5 2.7 %collective-permute-done.6.arrived = f32[512,640]{1,0:T(8,128)S(1)} collective-permute-done((f32[512,640]{1,0:T(8,128)S(1)}, f32[512,640]{1,0:T(8,128)S(1)}, u32[]{:S(2)}, u32[]{:S(2)}) %collective-permute-start.6) | collective-permute-done | bytes 1310752 | tf_op jit(solution)/shard_map/ppermute | solution.py:26
  15.2 0.7 add_halves.1
  16.1 5.1 %collective-permute-start.3 = (f32[64,2176]{1,0:T(8,128)S(1)}, f32[64,2176]{1,0:T(8,128)S(1)}, u32[]{:S(2)}, u32[]{:S(2)}) collective-permute-start(f32[64,2176]{1,0:T(8,128)S(1)} %constant_dynamic-update-slice_fusion.refs_0_), channel_id=1, source_target_pairs={{0,112},{16,0},{32,16},{48,32},{64,48},{80,64},{96,80},{112,96},{1... | collective-permute-start | bytes 1671176 | tf_op jit(solution)/shard_map/ppermute | solution.py:26
  21.2 10.8 %collective-permute-done.7.b = f32[256,640]{1,0:T(8,128)S(1)} collective-permute-done((f32[256,640]{1,0:T(8,128)S(1)}, f32[256,640]{1,0:T(8,128)S(1)}, u32[]{:S(2)}, u32[]{:S(2)}) %collective-permute-start.7) | collective-permute-done | bytes 655392 | tf_op jit(solution)/shard_map/ppermute | solution.py:26
  32.0 0.9 add.5
  32.9 6.5 %all-to-all-start = ((f32[8,32,640]{2,1,0:T(8,128)}), f32[8,32,640]{2,1,0:T(8,128)S(1)}, u32[]{:S(2)}, u32[]{:S(2)}) async-start(f32[8,32,640]{2,1,0:T(8,128)} %bitcast.6), calls=%async_computation | async-start | bytes 1310720 | tf_op jit(solution)/shard_map/all_to_all | solution.py:34
  39.3 2.7 %collective-permute-start.4 = (f32[64,2176]{1,0:T(8,128)S(1)}, f32[64,2176]{1,0:T(8,128)S(1)}, u32[]{:S(2)}, u32[]{:S(2)}) collective-permute-start(f32[64,2176]{1,0:T(8,128)S(1)} %collective-permute-done.3.refs_2_), channel_id=1, source_target_pairs={{0,112},{16,0},{32,16},{48,32},{64,48},{80,64},{96,80},{112,96},{1... | collective-permute-start | bytes 1671176 | tf_op jit(solution)/shard_map/ppermute | solution.py:26
  42.0 4.5 %split_basis.2.refs_3_ = bf16[2,1088,2176]{2,1,0:T(8,128)(2,1)S(1)} custom-call(f32[544,2176]{1,0:T(8,128)} %bitcast.10, f32[544,2176]{1,0:T(8,128)} %bitcast.5.other), custom_call_target="tpu_custom_call" | custom-call | flops 1000 | bytes 1000 | tf_op jit(solution)/shard_map/split_basis/pallas_call | solution.py:75
  46.5 3.9 %products.3.refs_0_ = f32[192,1088]{1,0:T(8,128)S(1)} custom-call(f32[64,2176]{1,0:T(8,128)S(1)} %constant_dynamic-update-slice_fusion.refs_0_, f32[64,2176]{1,0:T(8,128)S(1)} %collective-permute-done.1.refs_1_, f32[64,2176]{1,0:T(8,128)S(1)} %collective-permute-done.3.refs_2_, bf16[2,1088,2176]{2,1,0:T(8,128)(2,1)S(1)} %split_basis.2.refs_3_), custom_call_target="tpu_custom_call" | custom-call | flops 1000 | bytes 1000 | tf_op jit(solution)/shard_map/products/pallas_call | solution.py:112
  50.4 15.9 %collective-permute-done.4.refs_2_ = f32[64,2176]{1,0:T(8,128)S(1)} collective-permute-done((f32[64,2176]{1,0:T(8,128)S(1)}, f32[64,2176]{1,0:T(8,128)S(1)}, u32[]{:S(2)}, u32[]{:S(2)}) %collective-permute-start.4) | collective-permute-done | bytes 557088 | tf_op jit(solution)/shard_map/ppermute | solution.py:26
  66.4 2.1 %collective-permute-done.2.refs_1_ = f32[64,2176]{1,0:T(8,128)} collective-permute-done((f32[64,2176]{1,0:T(8,128)S(1)}, f32[64,2176]{1,0:T(8,128)}, u32[]{:S(2)}, u32[]{:S(2)}) %collective-permute-start.2) | collective-permute-done | bytes 557088 | tf_op jit(solution)/shard_map/ppermute | solution.py:26
  68.5 2.7 %collective-permute-start.10 = (f32[64,2176]{1,0:T(8,128)S(1)}, f32[64,2176]{1,0:T(8,128)}, u32[]{:S(2)}, u32[]{:S(2)}) collective-permute-start(f32[64,2176]{1,0:T(8,128)S(1)} %collective-permute-done.4.refs_2_), channel_id=1, source_target_pairs={{0,112},{16,0},{32,16},{48,32},{64,48},{80,64},{96,80},{112,96},{1... | collective-permute-start | bytes 1671176 | tf_op jit(solution)/shard_map/ppermute | solution.py:26
  71.1 5.3 %products.4 = f32[320,1088]{1,0:T(8,128)} custom-call(f32[192,1088]{1,0:T(8,128)S(1)} %products.3.refs_0_, f32[64,2176]{1,0:T(8,128)} %collective-permute-done.2.refs_1_, f32[64,2176]{1,0:T(8,128)S(1)} %collective-permute-done.4.refs_2_, bf16[2,1088,2176]{2,1,0:T(8,128)(2,1)S(1)} %split_basis.2.refs_3_), custom_call_target="tpu_custom_call" | custom-call | flops 1000 | bytes 1000 | tf_op jit(solution)/shard_map/products/pallas_call | solution.py:112
  76.5 6.6 %all-to-all-start.1 = ((f32[8,40,1088]{2,1,0:T(8,128)}), f32[8,40,1088]{2,1,0:T(8,128)S(1)}, u32[]{:S(2)}, u32[]{:S(2)}) async-start(f32[8,40,1088]{2,1,0:T(8,128)} %bitcast.7), calls=%async_computation.1 | async-start | bytes 2949120 | tf_op jit(solution)/shard_map/all_to_all | solution.py:34
  83.3 1.0 slice.9
  84.2 2.7 %collective-permute-start.12 = (f32[32,2176]{1,0:T(8,128)S(1)}, f32[32,2176]{1,0:T(8,128)S(1)}, u32[]{:S(2)}, u32[]{:S(2)}) collective-permute-start(f32[32,2176]{1,0:T(8,128)S(1)} %slice.9), channel_id=1, source_target_pairs={{0,112},{16,0},{32,16},{48,32},{64,48},{80,64},{96,80},{112,96},{1... | collective-permute-start | bytes 835592 | tf_op jit(solution)/shard_map/ppermute | solution.py:26
  87.0 0.7 collective-permute-start.8
  87.7 4.5 %split_basis.3.refs_4_ = bf16[2,1088,2176]{2,1,0:T(8,128)(2,1)S(1)} custom-call(f32[544,2176]{1,0:T(8,128)} %bitcast.11, f32[544,2176]{1,0:T(8,128)} %bitcast.5.other), custom_call_target="tpu_custom_call" | custom-call | flops 1000 | bytes 1000 | tf_op jit(solution)/shard_map/split_basis/pallas_call | solution.py:75
  92.2 5.9 %products.5 = f32[192,1088]{1,0:T(8,128)} custom-call(f32[64,2176]{1,0:T(8,128)S(1)} %collective-permute-done.9.refs_0_, f32[64,2176]{1,0:T(8,128)} %collective-permute-done.10.refs_1_, f32[32,2176]{1,0:T(8,128)S(1)} %collective-permute-done.11.refs_2_, f32[32,2176]{1,0:T(8,128)S(1)} %collective-permute-done.12.refs_3_, ...), custom_call_target="tpu_custom_call" | custom-call | flops 5000000000 | bytes 1000 | tf_op jit(solution)/shard_map/products/pallas_call | solution.py:112
  98.1 1.8 %collective-permute-done.8.other = f32[1,32,640]{2,1,0:T(8,128)S(1)} collective-permute-done((f32[1,32,640]{2,1,0:T(8,128)S(1)}, f32[1,32,640]{2,1,0:T(8,128)S(1)}, u32[]{:S(2)}, u32[]{:S(2)}) %collective-permute-start.8) | collective-permute-done | bytes 81952 | tf_op jit(solution)/shard_map/ppermute | solution.py:26
  100.5 7.8 %all-to-all-start.2 = ((f32[8,24,1088]{2,1,0:T(8,128)}), f32[8,24,1088]{2,1,0:T(8,128)S(1)}, u32[]{:S(2)}, u32[]{:S(2)}) async-start(f32[8,24,1088]{2,1,0:T(8,128)} %bitcast.8), calls=%async_computation.2 | async-start | bytes 1769472 | tf_op jit(solution)/shard_map/all_to_all | solution.py:34
  108.3 1.4 collective-permute-start.13
  109.8 2.7 %collective-permute-done.14.refs_2_ = f32[64,640]{1,0:T(8,128)S(1)} collective-permute-done((f32[64,640]{1,0:T(8,128)S(1)}, f32[64,640]{1,0:T(8,128)S(1)}, u32[]{:S(2)}, u32[]{:S(2)}) %collective-permute-start.14) | collective-permute-done | bytes 163872 | tf_op jit(solution)/shard_map/ppermute | solution.py:26
  112.5 1.3 collective-permute-done.13.refs_1_
  113.8 4.8 %all-to-all-done.2.refs_1_ = f32[8,24,1088]{2,1,0:T(8,128)S(1)} async-done(((f32[8,24,1088]{2,1,0:T(8,128)}), f32[8,24,1088]{2,1,0:T(8,128)S(1)}, u32[]{:S(2)}, u32[]{:S(2)}) %all-to-all-start.2) | async-done | bytes 835616 | tf_op jit(solution)/shard_map/all_to_all | solution.py:34
  118.8 1.4 copy-done
  120.2 7.3 %all-to-all-start.3 = ((f32[8,64,1088]{2,1,0:T(8,128)}), f32[8,64,1088]{2,1,0:T(8,128)S(1)}, u32[]{:S(2)}, u32[]{:S(2)}) async-start(f32[8,64,1088]{2,1,0:T(8,128)} %copy-done), calls=%async_computation.3 | async-start | bytes 4718592 | tf_op jit(solution)/shard_map/all_to_all | solution.py:34
  127.6 2.7 %collective-permute-start.16 = (f32[64,640]{1,0:T(8,128)S(1)}, f32[64,640]{1,0:T(8,128)S(1)}, u32[]{:S(2)}, u32[]{:S(2)}) collective-permute-start(f32[64,640]{1,0:T(8,128)S(1)} %collective-permute-done.14.refs_2_), channel_id=1, source_target_pairs={{0,112},{16,0},{32,16},{48,32},{64,48},{80,64},{96,80},{112,96},{1... | collective-permute-start | bytes 491528 | tf_op jit(solution)/shard_map/ppermute | solution.py:26
  130.2 2.7 %collective-permute-done.15.refs_3_ = f32[64,640]{1,0:T(8,128)S(1)} collective-permute-done((f32[64,640]{1,0:T(8,128)S(1)}, f32[64,640]{1,0:T(8,128)S(1)}, u32[]{:S(2)}, u32[]{:S(2)}) %collective-permute-start.15) | collective-permute-done | bytes 163872 | tf_op jit(solution)/shard_map/ppermute | solution.py:26
  132.9 3.0 %collective-permute-start.18 = (f32[64,640]{1,0:T(8,128)S(1)}, f32[64,640]{1,0:T(8,128)S(1)}, u32[]{:S(2)}, u32[]{:S(2)}) collective-permute-start(f32[64,640]{1,0:T(8,128)S(1)} %collective-permute-done.16.refs_4_), channel_id=1, source_target_pairs={{0,112},{16,0},{32,16},{48,32},{64,48},{80,64},{96,80},{112,96},{1... | collective-permute-start | bytes 491528 | tf_op jit(solution)/shard_map/ppermute | solution.py:26
  135.9 2.7 %collective-permute-done.17.refs_5_ = f32[64,640]{1,0:T(8,128)S(1)} collective-permute-done((f32[64,640]{1,0:T(8,128)S(1)}, f32[64,640]{1,0:T(8,128)S(1)}, u32[]{:S(2)}, u32[]{:S(2)}) %collective-permute-start.17) | collective-permute-done | bytes 163872 | tf_op jit(solution)/shard_map/ppermute | solution.py:26
  138.6 5.7 %collective-permute-done.19.refs_7_ = f32[64,640]{1,0:T(8,128)S(1)} collective-permute-done((f32[64,640]{1,0:T(8,128)S(1)}, f32[64,640]{1,0:T(8,128)S(1)}, u32[]{:S(2)}, u32[]{:S(2)}) %collective-permute-start.19) | collective-permute-done | bytes 163872 | tf_op jit(solution)/shard_map/ppermute | solution.py:26
  144.9 4.5 %collective-permute-start.20 = (f32[512,640]{1,0:T(8,128)S(1)}, f32[512,640]{1,0:T(8,128)S(1)}, u32[]{:S(2)}, u32[]{:S(2)}) collective-permute-start(f32[512,640]{1,0:T(8,128)S(1)} %place.1.own), channel_id=1, source_target_pairs={{0,8},{8,0},{1,9},{9,1},{2,10},{10,2},{3,11},{11,3},{4,12},{12,4},... | collective-permute-start | bytes 3932168 | tf_op jit(solution)/shard_map/ppermute | solution.py:26
  149.5 1.1 copy-done.1
  150.5 1.6 collective-permute-done.20.other
  152.1 1.1 copy-done.3
  153.2 3.2 %all-to-all-done.3.refs_0_ = f32[8,64,1088]{2,1,0:T(8,128)S(1)} async-done(((f32[8,64,1088]{2,1,0:T(8,128)}), f32[8,64,1088]{2,1,0:T(8,128)S(1)}, u32[]{:S(2)}, u32[]{:S(2)}) %all-to-all-start.3) | async-done | bytes 2228256 | tf_op jit(solution)/shard_map/all_to_all | solution.py:34
  156.4 1.2 collective-permute-start.21
  157.8 1.3 copy-done.2
  159.1 1.3 copy-done.4
  160.4 1.0 split_grads.1
  161.8 8.9 %moments.1 = f32[544,640]{1,0:T(8,128)} custom-call(s32[3]{0:T(128)S(1)} %pad_add_fusion.place, s32[5]{0:T(128)S(1)} %convert_reduce_fusion.bounds, f32[8,64,1088]{2,1,0:T(8,128)S(1)} %all-to-all-done.3.refs_0_, f32[8,64,1088]{2,1,0:T(8,128)S(1)} %collective-permute-done.21.refs_1_, bf16[1280,640]{1,0:T(8,128)(2,1)S(1)} %get-tuple-element.69.refs_2_, ...), custom_call_target="tpu_custom_call" | custom-call | flops 1000 | bytes 1000 | tf_op jit(solution)/shard_map/moments/pallas_call | solution.py:282
  (42 shorter events, 2.5 us)
Async XLA Ops:
  0.0 42.0 %collective-permute-start.5 = (f32[2176,544]{0,1:T(8,128)}, f32[2176,544]{0,1:T(8,128)}, u32[]{:S(2)}, u32[]{:S(2)}) collective-permute-start(f32[2176,544]{0,1:T(8,128)} %param.6), channel_id=1, source_target_pairs={{0,8},{8,0},{1,9},{9,1},{2,10},{10,2},{3,11},{11,3},{4,12},{12,4},... | collective-permute-start | bytes 14204936 | tf_op jit(solution)/shard_map/ppermute | solution.py:26
  3.2 8.5 %collective-permute-start = (f32[32,2176]{1,0:T(8,128)}, f32[32,2176]{1,0:T(8,128)S(1)}, u32[]{:S(2)}, u32[]{:S(2)}) collective-permute-start(f32[32,2176]{1,0:T(8,128)} %param.5), channel_id=1, source_target_pairs={{0,128},{128,0},{1,129},{129,1},{2,130},{130,2},{3,131},{131,3},{4... | collective-permute-start | bytes 835592 | tf_op jit(solution)/shard_map/ppermute | solution.py:26
  3.3 1.1 copy-start.5
  4.4 1.0 copy-start.6
  5.4 10.6 %copy-start.7 = (f32[32,2176]{1,0:T(8,128)S(1)}, f32[32,2176]{1,0:T(8,128)}, u32[]{:S(2)}) copy-start(f32[32,2176]{1,0:T(8,128)} %param.5) | copy-start | bytes 835588
  11.7 3.4 %collective-permute-start.6 = (f32[512,640]{1,0:T(8,128)S(1)}, f32[512,640]{1,0:T(8,128)S(1)}, u32[]{:S(2)}, u32[]{:S(2)}) collective-permute-start(f32[512,640]{1,0:T(8,128)S(1)} %get-tuple-element.48), channel_id=1, source_target_pairs={{0,8},{8,0},{1,9},{9,1},{2,10},{10,2},{3,11},{11,3},{4,12},{12,4},... | collective-permute-start | bytes 3932168 | tf_op jit(solution)/shard_map/ppermute | solution.py:26
  15.9 16.0 %collective-permute-start.7 = (f32[256,640]{1,0:T(8,128)S(1)}, f32[256,640]{1,0:T(8,128)S(1)}, u32[]{:S(2)}, u32[]{:S(2)}) collective-permute-start(f32[256,640]{1,0:T(8,128)S(1)} %get-tuple-element.50), channel_id=1, source_target_pairs={{0,128},{128,0},{1,129},{129,1},{2,130},{130,2},{3,131},{131,3},{4... | collective-permute-start | bytes 1966088 | tf_op jit(solution)/shard_map/ppermute | solution.py:26
  16.1 23.2 %collective-permute-start.3 = (f32[64,2176]{1,0:T(8,128)S(1)}, f32[64,2176]{1,0:T(8,128)S(1)}, u32[]{:S(2)}, u32[]{:S(2)}) collective-permute-start(f32[64,2176]{1,0:T(8,128)S(1)} %constant_dynamic-update-slice_fusion.refs_0_), channel_id=1, source_target_pairs={{0,112},{16,0},{32,16},{48,32},{64,48},{80,64},{96,80},{112,96},{1... | collective-permute-start | bytes 1671176 | tf_op jit(solution)/shard_map/ppermute | solution.py:26
  21.2 20.8 %collective-permute-start.1 = (f32[64,2176]{1,0:T(8,128)S(1)}, f32[64,2176]{1,0:T(8,128)S(1)}, u32[]{:S(2)}, u32[]{:S(2)}) collective-permute-start(f32[64,2176]{1,0:T(8,128)S(1)} %constant_dynamic-update-slice_fusion.refs_0_), channel_id=1, source_target_pairs={{0,16},{16,32},{32,48},{48,64},{64,80},{80,96},{96,112},{112,0},{1... | collective-permute-start | bytes 1671176 | tf_op jit(solution)/shard_map/ppermute | solution.py:26
  32.9 43.6 %all-to-all-start = ((f32[8,32,640]{2,1,0:T(8,128)}), f32[8,32,640]{2,1,0:T(8,128)S(1)}, u32[]{:S(2)}, u32[]{:S(2)}) async-start(f32[8,32,640]{2,1,0:T(8,128)} %bitcast.6), calls=%async_computation | async-start | bytes 1310720 | tf_op jit(solution)/shard_map/all_to_all | solution.py:34
  39.3 27.1 %collective-permute-start.4 = (f32[64,2176]{1,0:T(8,128)S(1)}, f32[64,2176]{1,0:T(8,128)S(1)}, u32[]{:S(2)}, u32[]{:S(2)}) collective-permute-start(f32[64,2176]{1,0:T(8,128)S(1)} %collective-permute-done.3.refs_2_), channel_id=1, source_target_pairs={{0,112},{16,0},{32,16},{48,32},{64,48},{80,64},{96,80},{112,96},{1... | collective-permute-start | bytes 1671176 | tf_op jit(solution)/shard_map/ppermute | solution.py:26
  42.0 26.5 %collective-permute-start.2 = (f32[64,2176]{1,0:T(8,128)S(1)}, f32[64,2176]{1,0:T(8,128)}, u32[]{:S(2)}, u32[]{:S(2)}) collective-permute-start(f32[64,2176]{1,0:T(8,128)S(1)} %collective-permute-done.1.refs_1_), channel_id=1, source_target_pairs={{0,16},{16,32},{32,48},{48,64},{64,80},{80,96},{96,112},{112,0},{1... | collective-permute-start | bytes 1671176 | tf_op jit(solution)/shard_map/ppermute | solution.py:26
  68.5 14.7 %collective-permute-start.9 = (f32[64,2176]{1,0:T(8,128)}, f32[64,2176]{1,0:T(8,128)S(1)}, u32[]{:S(2)}, u32[]{:S(2)}) collective-permute-start(f32[64,2176]{1,0:T(8,128)} %collective-permute-done.2.refs_1_), channel_id=1, source_target_pairs={{0,16},{16,32},{32,48},{48,64},{64,80},{80,96},{96,112},{112,0},{1... | collective-permute-start | bytes 1671176 | tf_op jit(solution)/shard_map/ppermute | solution.py:26
  68.5 14.8 %collective-permute-start.10 = (f32[64,2176]{1,0:T(8,128)S(1)}, f32[64,2176]{1,0:T(8,128)}, u32[]{:S(2)}, u32[]{:S(2)}) collective-permute-start(f32[64,2176]{1,0:T(8,128)S(1)} %collective-permute-done.4.refs_2_), channel_id=1, source_target_pairs={{0,112},{16,0},{32,16},{48,32},{64,48},{80,64},{96,80},{112,96},{1... | collective-permute-start | bytes 1671176 | tf_op jit(solution)/shard_map/ppermute | solution.py:26
  76.5 24.0 %all-to-all-start.1 = ((f32[8,40,1088]{2,1,0:T(8,128)}), f32[8,40,1088]{2,1,0:T(8,128)S(1)}, u32[]{:S(2)}, u32[]{:S(2)}) async-start(f32[8,40,1088]{2,1,0:T(8,128)} %bitcast.7), calls=%async_computation.1 | async-start | bytes 2949120 | tf_op jit(solution)/shard_map/all_to_all | solution.py:34
  83.2 9.0 %collective-permute-start.11 = (f32[32,2176]{1,0:T(8,128)S(1)}, f32[32,2176]{1,0:T(8,128)S(1)}, u32[]{:S(2)}, u32[]{:S(2)}) collective-permute-start(f32[32,2176]{1,0:T(8,128)S(1)} %slice.8), channel_id=1, source_target_pairs={{0,16},{16,32},{32,48},{48,64},{64,80},{80,96},{96,112},{112,0},{1... | collective-permute-start | bytes 835592 | tf_op jit(solution)/shard_map/ppermute | solution.py:26
  84.2 8.0 %collective-permute-start.12 = (f32[32,2176]{1,0:T(8,128)S(1)}, f32[32,2176]{1,0:T(8,128)S(1)}, u32[]{:S(2)}, u32[]{:S(2)}) collective-permute-start(f32[32,2176]{1,0:T(8,128)S(1)} %slice.9), channel_id=1, source_target_pairs={{0,112},{16,0},{32,16},{48,32},{64,48},{80,64},{96,80},{112,96},{1... | collective-permute-start | bytes 835592 | tf_op jit(solution)/shard_map/ppermute | solution.py:26
  87.0 12.9 %collective-permute-start.8 = (f32[1,32,640]{2,1,0:T(8,128)S(1)}, f32[1,32,640]{2,1,0:T(8,128)S(1)}, u32[]{:S(2)}, u32[]{:S(2)}) collective-permute-start(f32[1,32,640]{2,1,0:T(8,128)S(1)} %sum_copies.2.own), channel_id=1, source_target_pairs={{0,128},{128,0},{1,129},{129,1},{2,130},{130,2},{3,131},{131,3},{4... | collective-permute-start | bytes 245768 | tf_op jit(solution)/shard_map/ppermute | solution.py:26
  100.5 18.1 %all-to-all-start.2 = ((f32[8,24,1088]{2,1,0:T(8,128)}), f32[8,24,1088]{2,1,0:T(8,128)S(1)}, u32[]{:S(2)}, u32[]{:S(2)}) async-start(f32[8,24,1088]{2,1,0:T(8,128)} %bitcast.8), calls=%async_computation.2 | async-start | bytes 1769472 | tf_op jit(solution)/shard_map/all_to_all | solution.py:34
  108.3 4.2 %collective-permute-start.14 = (f32[64,640]{1,0:T(8,128)S(1)}, f32[64,640]{1,0:T(8,128)S(1)}, u32[]{:S(2)}, u32[]{:S(2)}) collective-permute-start(f32[64,640]{1,0:T(8,128)S(1)} %pair.1.refs_0_), channel_id=1, source_target_pairs={{0,112},{16,0},{32,16},{48,32},{64,48},{80,64},{96,80},{112,96},{1... | collective-permute-start | bytes 491528 | tf_op jit(solution)/shard_map/ppermute | solution.py:26
  108.3 5.4 %collective-permute-start.13 = (f32[64,640]{1,0:T(8,128)S(1)}, f32[64,640]{1,0:T(8,128)S(1)}, u32[]{:S(2)}, u32[]{:S(2)}) collective-permute-start(f32[64,640]{1,0:T(8,128)S(1)} %pair.1.refs_0_), channel_id=1, source_target_pairs={{0,16},{16,32},{32,48},{48,64},{64,80},{80,96},{96,112},{112,0},{1... | collective-permute-start | bytes 491528 | tf_op jit(solution)/shard_map/ppermute | solution.py:26
  118.7 1.4 copy-start
  120.2 36.2 %all-to-all-start.3 = ((f32[8,64,1088]{2,1,0:T(8,128)}), f32[8,64,1088]{2,1,0:T(8,128)S(1)}, u32[]{:S(2)}, u32[]{:S(2)}) async-start(f32[8,64,1088]{2,1,0:T(8,128)} %copy-done), calls=%async_computation.3 | async-start | bytes 4718592 | tf_op jit(solution)/shard_map/all_to_all | solution.py:34
  127.5 30.2 %copy-start.8 = (s32[1024]{0:T(1024)S(1)}, s32[1024]{0:T(1024)}, u32[]{:S(2)}) copy-start(s32[1024]{0:T(1024)} %param.9) | copy-start | bytes 12292
  127.5 5.5 %collective-permute-start.15 = (f32[64,640]{1,0:T(8,128)S(1)}, f32[64,640]{1,0:T(8,128)S(1)}, u32[]{:S(2)}, u32[]{:S(2)}) collective-permute-start(f32[64,640]{1,0:T(8,128)S(1)} %collective-permute-done.13.refs_1_), channel_id=1, source_target_pairs={{0,16},{16,32},{32,48},{48,64},{64,80},{80,96},{96,112},{112,0},{1... | collective-permute-start | bytes 491528 | tf_op jit(solution)/shard_map/ppermute | solution.py:26
  127.6 5.4 %collective-permute-start.16 = (f32[64,640]{1,0:T(8,128)S(1)}, f32[64,640]{1,0:T(8,128)S(1)}, u32[]{:S(2)}, u32[]{:S(2)}) collective-permute-start(f32[64,640]{1,0:T(8,128)S(1)} %collective-permute-done.14.refs_2_), channel_id=1, source_target_pairs={{0,112},{16,0},{32,16},{48,32},{64,48},{80,64},{96,80},{112,96},{1... | collective-permute-start | bytes 491528 | tf_op jit(solution)/shard_map/ppermute | solution.py:26
  132.9 5.7 %collective-permute-start.17 = (f32[64,640]{1,0:T(8,128)S(1)}, f32[64,640]{1,0:T(8,128)S(1)}, u32[]{:S(2)}, u32[]{:S(2)}) collective-permute-start(f32[64,640]{1,0:T(8,128)S(1)} %collective-permute-done.15.refs_3_), channel_id=1, source_target_pairs={{0,16},{16,32},{32,48},{48,64},{64,80},{80,96},{96,112},{112,0},{1... | collective-permute-start | bytes 491528 | tf_op jit(solution)/shard_map/ppermute | solution.py:26
  132.9 5.7 %collective-permute-start.18 = (f32[64,640]{1,0:T(8,128)S(1)}, f32[64,640]{1,0:T(8,128)S(1)}, u32[]{:S(2)}, u32[]{:S(2)}) collective-permute-start(f32[64,640]{1,0:T(8,128)S(1)} %collective-permute-done.16.refs_4_), channel_id=1, source_target_pairs={{0,112},{16,0},{32,16},{48,32},{64,48},{80,64},{96,80},{112,96},{1... | collective-permute-start | bytes 491528 | tf_op jit(solution)/shard_map/ppermute | solution.py:26
  138.6 5.7 %collective-permute-start.19 = (f32[64,640]{1,0:T(8,128)S(1)}, f32[64,640]{1,0:T(8,128)S(1)}, u32[]{:S(2)}, u32[]{:S(2)}) collective-permute-start(f32[64,640]{1,0:T(8,128)S(1)} %collective-permute-done.17.refs_5_), channel_id=1, source_target_pairs={{0,16},{16,32},{32,48},{48,64},{64,80},{80,96},{96,112},{112,0},{1... | collective-permute-start | bytes 491528 | tf_op jit(solution)/shard_map/ppermute | solution.py:26
  144.9 7.2 %collective-permute-start.20 = (f32[512,640]{1,0:T(8,128)S(1)}, f32[512,640]{1,0:T(8,128)S(1)}, u32[]{:S(2)}, u32[]{:S(2)}) collective-permute-start(f32[512,640]{1,0:T(8,128)S(1)} %place.1.own), channel_id=1, source_target_pairs={{0,8},{8,0},{1,9},{9,1},{2,10},{10,2},{3,11},{11,3},{4,12},{12,4},... | collective-permute-start | bytes 3932168 | tf_op jit(solution)/shard_map/ppermute | solution.py:26
  149.5 1.1 copy-start.1
  152.1 1.1 copy-start.3
  156.4 5.4 %collective-permute-start.21 = (f32[8,64,1088]{2,1,0:T(8,128)S(1)}, f32[8,64,1088]{2,1,0:T(8,128)S(1)}, u32[]{:S(2)}, u32[]{:S(2)}) collective-permute-start(f32[8,64,1088]{2,1,0:T(8,128)S(1)} %all-to-all-done.3.refs_0_), channel_id=1, source_target_pairs={{0,8},{8,0},{1,9},{9,1},{2,10},{10,2},{3,11},{11,3},{4,12},{12,4},... | collective-permute-start | bytes 6684680 | tf_op jit(solution)/shard_map/ppermute | solution.py:26
  157.8 1.3 copy-start.2
  159.1 1.3 copy-start.4
